TPU v7x, 32 devices: a whole 2x2x4 slice. The times are simulated.
32 devices in a mesh: narrow: 4 (over y, x), wide: 8 (over z, core).
Axes of the slice: x: 2, y: 2, z: 4, core: 2. Of those that a mesh axis runs over, the one named last changes fastest.
Arguments:
- tokens: bfloat16 [8, 2, 1024, 768], P('wide', None, 'narrow'), may hold values from -6 to 6
- lengths: int32 [8], P('wide'), may hold values from 128 to 1024, as said below
- w_qkv: bfloat16 [2, 768, 2304], P(None, 'narrow'), may hold values from -0.21875 to 0.21875
- w_out: bfloat16 [2, 768, 768], P(None, 'narrow'), may hold values from -1.5 to 1.5
- w_up: bfloat16 [2, 768, 3072], P(None, 'narrow'), may hold values from -0.21875 to 0.21875
- w_down: bfloat16 [2, 3072, 768], P(None, 'narrow'), may hold values from -0.109375 to 0.109375
- norm_gains: bfloat16 [2, 2, 768], P(None, None, 'narrow'), may hold values from 0.099609375 to 1.8984375
- norm_biases: bfloat16 [2, 2, 768], P(None, None, 'narrow'), may hold values from -2 to 2
- cotangent: bfloat16 [8, 2, 1024, 768], P('wide', None, 'narrow'), may hold values from -6 to 6
Outputs:
- result: bfloat16 [8, 2, 1024, 768], P('wide', None, 'narrow')
- grad_tokens: bfloat16 [8, 2, 1024, 768], P('wide', None, 'narrow')
- grad_qkv: float32 [2, 768, 2304], P(None, 'narrow')
- grad_out: float32 [2, 768, 768], P(None, 'narrow')
- grad_up: float32 [2, 768, 3072], P(None, 'narrow')
- grad_down: float32 [2, 3072, 768], P(None, 'narrow')
- grad_gains: float32 [2, 2, 768], P(None, None, 'narrow')
- biases_first: float32 [2, 768], P(None, 'narrow')
- biases_second: float32 [2, 768], P(None, 'narrow')
Inputs may be any that keep to these rules, and one draw needn't show every extreme that they name: `lengths`: each length is a multiple of 16; some row has exactly 1024 and some exactly 128.
All inputs are finite; a program needn't handle non-finite values.
Results may differ from a plain program's by a relative error of at most 0.019.
Values may be sent and summed in bfloat16 or wider, within the bound.
A program may use at most 256 MiB of HBM per device.

v0:
```python
from functools import partial

import jax
import jax.numpy as jnp
from jax import lax
from jax.sharding import PartitionSpec as P

H = 12
BLOCK = 16


def norm_rows(hidden, gain, bias):
    mean = jnp.mean(hidden, axis=-1, keepdims=True)
    centred = hidden - mean
    inverse = lax.rsqrt(jnp.mean(centred * centred, axis=-1, keepdims=True) + 1e-05)
    return (centred * inverse * gain + bias, centred * inverse, inverse)


def norm_back(grad, normed, inverse, gain):
    scaled = grad * gain
    inner = (
        scaled
        - jnp.mean(scaled, axis=-1, keepdims=True)
        - normed * jnp.mean(scaled * normed, axis=-1, keepdims=True)
    )
    return (inverse * inner, jnp.sum(grad * normed, axis=0), jnp.sum(grad, axis=0))


def tables(positions, width):
    half = width // 2
    freq = jnp.exp(-jnp.log(10000.0) * jnp.arange(half, dtype=jnp.float32) * 2.0 / width)
    angle = positions.astype(jnp.float32)[:, None] * freq[None, :]
    return (jnp.cos(angle)[:, None, :], jnp.sin(angle)[:, None, :])


def rotate(values, cosine, sine):
    half = values.shape[-1] // 2
    first = values[..., :half]
    second = values[..., half:]
    return jnp.concatenate(
        [first * cosine - second * sine, second * cosine + first * sine], axis=-1
    )


def rotate_back(values, cosine, sine):
    half = values.shape[-1] // 2
    first = values[..., :half]
    second = values[..., half:]
    return jnp.concatenate(
        [first * cosine + second * sine, second * cosine - first * sine], axis=-1
    )


def outer_sum(left, right):
    return lax.dot_general(
        left, right, (((0,), (0,)), ((), ())), preferred_element_type=jnp.float32
    )


def times_back(left, weight):
    return lax.dot_general(
        left, weight, (((1,), (1,)), ((), ())), preferred_element_type=jnp.float32
    )


def safe_top(values):
    return jnp.where(jnp.isfinite(values), values, 0.0)


def on_device(tokens, lengths, w_qkv, w_out, w_up, w_down, norm_gains, norm_biases, cotangent):
    rows, _, share, width = tokens.shape
    parts = lax.axis_size("narrow")
    here = lax.axis_index("narrow")
    seq = share * parts
    layers = w_qkv.shape[0]
    heads = H
    head_dim = width // heads
    count = rows * 2 * share
    scale = head_dim ** (-0.5)
    tile = min(128, share)
    tiles = share // tile
    local = here * share + jnp.arange(share, dtype=jnp.int32)
    cosine, sine = tables(local, head_dim)
    query_block = (jnp.concatenate([local, local]) // BLOCK)[:, None]
    query_clean = jnp.concatenate([jnp.zeros((share,), bool), jnp.ones((share,), bool)])[:, None]
    key_offsets = jnp.arange(share, dtype=jnp.int32)
    tile_block = jnp.arange(tile, dtype=jnp.int32) // BLOCK
    same_block = tile_block[:, None] == tile_block[None, :]
    stop = here + 1

    def group_scores(query, keys_all, group):
        keys = lax.dynamic_slice_in_dim(keys_all, group * share, share, 1)
        score = (
            jnp.einsum("rqhd,rkhd->rhqk", query, keys, preferred_element_type=jnp.float32) * scale
        )
        key_block = ((group * share + key_offsets) // BLOCK)[None, :]
        allow = jnp.where(query_clean, key_block <= query_block, key_block < query_block)
        return jnp.where(allow[None, None], score, -jnp.inf)

    def as_tiles(values):
        return values.reshape(rows, tiles, tile, heads, head_dim)

    def to_rows(values):
        return values.transpose(0, 2, 1, 3).reshape(rows, heads, share)

    def to_tiles(values):
        return values.reshape(rows, heads, tiles, tile).transpose(0, 2, 1, 3)[..., None]

    def noisy_scores(query_noisy, key_noisy):
        score = (
            jnp.einsum(
                "rtqhd,rtkhd->rthqk",
                as_tiles(query_noisy),
                as_tiles(key_noisy),
                preferred_element_type=jnp.float32,
            )
            * scale
        )
        return jnp.where(same_block[None, None, None], score, -jnp.inf)

    def attend_forward(query, clean_k, clean_v, noisy_k, noisy_v):
        local_score = noisy_scores(query[:, :share], noisy_k)
        local_top = jnp.max(local_score, axis=-1)
        local_total = jnp.sum(jnp.exp(local_score - local_top[..., None]), axis=-1)
        top_start = jnp.concatenate(
            [to_rows(local_top), jnp.full((rows, heads, share), -jnp.inf, jnp.float32)], axis=2
        )
        total_start = jnp.concatenate(
            [to_rows(local_total), jnp.zeros((rows, heads, share), jnp.float32)], axis=2
        )

        def stat_step(group, carry):
            top, total = carry
            score = group_scores(query, clean_k, group)
            group_top = safe_top(jnp.max(score, axis=-1))
            group_total = jnp.sum(jnp.exp(score - group_top[..., None]), axis=-1)
            joined = safe_top(jnp.maximum(top, group_top))
            total = total * jnp.exp(top - joined) + group_total * jnp.exp(group_top - joined)
            return (joined, total)

        top, total = lax.fori_loop(0, stop, stat_step, (top_start, total_start))
        logsum = top + jnp.log(total)
        local_probs = jnp.exp(local_score - to_tiles(logsum[:, :, :share])).astype(jnp.bfloat16)
        local_out = jnp.einsum(
            "rthqk,rtkhd->rtqhd", local_probs, as_tiles(noisy_v), preferred_element_type=jnp.float32
        ).reshape(rows, share, heads, head_dim)
        out_start = jnp.concatenate(
            [local_out, jnp.zeros((rows, share, heads, head_dim), jnp.float32)], axis=1
        )

        def out_step(group, attended):
            probs = jnp.exp(group_scores(query, clean_k, group) - logsum[..., None]).astype(
                jnp.bfloat16
            )
            values = lax.dynamic_slice_in_dim(clean_v, group * share, share, 1)
            return attended + jnp.einsum(
                "rhqk,rkhd->rqhd", probs, values, preferred_element_type=jnp.float32
            )

        attended = lax.fori_loop(0, stop, out_step, out_start)
        return (attended, logsum)

    def attend_backward(query, clean_k, clean_v, noisy_k, noisy_v, grad_ctx, logsum):
        local_score = noisy_scores(query[:, :share], noisy_k)
        local_probs = jnp.exp(local_score - to_tiles(logsum[:, :, :share]))
        grad_tiles = as_tiles(grad_ctx[:, :share])
        local_dp = jnp.einsum(
            "rtqhd,rtkhd->rthqk", grad_tiles, as_tiles(noisy_v), preferred_element_type=jnp.float32
        )
        delta_start = jnp.concatenate(
            [
                to_rows(jnp.sum(local_dp * local_probs, axis=-1)),
                jnp.zeros((rows, heads, share), jnp.float32),
            ],
            axis=2,
        )

        def delta_step(group, delta):
            probs = jnp.exp(group_scores(query, clean_k, group) - logsum[..., None])
            values = lax.dynamic_slice_in_dim(clean_v, group * share, share, 1)
            grad_probs = jnp.einsum(
                "rqhd,rkhd->rhqk", grad_ctx, values, preferred_element_type=jnp.float32
            )
            return delta + jnp.sum(grad_probs * probs, axis=-1)

        delta = lax.fori_loop(0, stop, delta_step, delta_start)
        local_ds = (local_probs * (local_dp - to_tiles(delta[:, :, :share]))).astype(jnp.bfloat16)
        local_dq = (
            jnp.einsum(
                "rthqk,rtkhd->rtqhd",
                local_ds,
                as_tiles(noisy_k),
                preferred_element_type=jnp.float32,
            )
            * scale
        )
        noisy_gk = (
            jnp.einsum(
                "rthqk,rtqhd->rtkhd",
                local_ds,
                as_tiles(query[:, :share]),
                preferred_element_type=jnp.float32,
            )
            * scale
        ).reshape(rows, share, heads, head_dim)
        noisy_gv = jnp.einsum(
            "rthqk,rtqhd->rtkhd",
            local_probs.astype(jnp.bfloat16),
            grad_tiles,
            preferred_element_type=jnp.float32,
        ).reshape(rows, share, heads, head_dim)
        dq_start = jnp.concatenate(
            [
                local_dq.reshape(rows, share, heads, head_dim),
                jnp.zeros((rows, share, heads, head_dim), jnp.float32),
            ],
            axis=1,
        )
        empty = jnp.zeros((rows, seq, heads, head_dim), jnp.float32)

        def grad_step(group, carry):
            grad_query, grad_key, grad_value = carry
            probs = jnp.exp(group_scores(query, clean_k, group) - logsum[..., None])
            keys = lax.dynamic_slice_in_dim(clean_k, group * share, share, 1)
            values = lax.dynamic_slice_in_dim(clean_v, group * share, share, 1)
            grad_probs = jnp.einsum(
                "rqhd,rkhd->rhqk", grad_ctx, values, preferred_element_type=jnp.float32
            )
            grad_score = (probs * (grad_probs - delta[..., None])).astype(jnp.bfloat16)
            grad_query = (
                grad_query
                + jnp.einsum(
                    "rhqk,rkhd->rqhd", grad_score, keys, preferred_element_type=jnp.float32
                )
                * scale
            )
            key_part = (
                jnp.einsum("rhqk,rqhd->rkhd", grad_score, query, preferred_element_type=jnp.float32)
                * scale
            )
            value_part = jnp.einsum(
                "rhqk,rqhd->rkhd",
                probs.astype(jnp.bfloat16),
                grad_ctx,
                preferred_element_type=jnp.float32,
            )
            grad_key = lax.dynamic_update_slice_in_dim(grad_key, key_part, group * share, 1)
            grad_value = lax.dynamic_update_slice_in_dim(grad_value, value_part, group * share, 1)
            return (grad_query, grad_key, grad_value)

        grad_query, clean_gk, clean_gv = lax.fori_loop(0, stop, grad_step, (dq_start, empty, empty))
        return (grad_query, clean_gk, clean_gv, noisy_gk, noisy_gv)

    hidden = tokens.astype(jnp.float32).reshape(count, width)
    saved = []
    for layer in range(layers):
        full = (
            lax.all_gather(w_qkv[layer], "narrow", axis=0, tiled=True),
            lax.all_gather(w_out[layer], "narrow", axis=0, tiled=True),
            lax.all_gather(w_up[layer], "narrow", axis=0, tiled=True),
            lax.all_gather(w_down[layer], "narrow", axis=0, tiled=True),
            lax.all_gather(norm_gains[layer], "narrow", axis=1, tiled=True),
            lax.all_gather(norm_biases[layer], "narrow", axis=1, tiled=True),
        )
        qkv_w, out_w, up_w, down_w, gains, biases = full
        normed_out, normed_one, inverse_one = norm_rows(
            hidden, gains[0].astype(jnp.float32), biases[0].astype(jnp.float32)
        )
        first = normed_out.astype(jnp.bfloat16)
        mixed = jnp.dot(first, qkv_w, preferred_element_type=jnp.float32).reshape(
            rows, 2, share, 3, heads, head_dim
        )
        query = rotate(mixed[:, :, :, 0], cosine, sine).astype(jnp.bfloat16)
        key = rotate(mixed[:, :, :, 1], cosine, sine).astype(jnp.bfloat16)
        value = mixed[:, :, :, 2].astype(jnp.bfloat16)
        clean_key, clean_value = (
            lax.all_gather(key[:, 1], "narrow", axis=1, tiled=True),
            lax.all_gather(value[:, 1], "narrow", axis=1, tiled=True),
        )
        head_items = (
            query.reshape(rows, 2 * share, heads, head_dim),
            clean_key,
            clean_value,
            key[:, 0],
            value[:, 0],
        )
        attended, logsum = attend_forward(*head_items)
        context = attended.reshape(count, width).astype(jnp.bfloat16)
        middle = hidden + jnp.dot(context, out_w, preferred_element_type=jnp.float32)
        normed_out, normed_two, inverse_two = norm_rows(
            middle, gains[1].astype(jnp.float32), biases[1].astype(jnp.float32)
        )
        second = normed_out.astype(jnp.bfloat16)
        upper = jnp.dot(second, up_w, preferred_element_type=jnp.float32)
        active = jax.nn.gelu(upper, approximate=True).astype(jnp.bfloat16)
        hidden = middle + jnp.dot(active, down_w, preferred_element_type=jnp.float32)
        stash = None
        saved.append(
            (
                stash,
                normed_one,
                inverse_one,
                first,
                head_items,
                logsum,
                context,
                normed_two,
                inverse_two,
                second,
                upper,
                active,
            )
        )
    result = hidden.reshape(tokens.shape).astype(jnp.bfloat16)
    valid = (local[None, :] < lengths[:, None]).astype(jnp.float32)
    grad = (cotangent.astype(jnp.float32) * valid[:, None, :, None]).reshape(count, width)
    grad_list = [None] * layers
    for layer in reversed(range(layers)):
        (
            stash,
            normed_one,
            inverse_one,
            first,
            head_items,
            logsum,
            context,
            normed_two,
            inverse_two,
            second,
            upper,
            active,
        ) = saved[layer]
        full = (
            lax.all_gather(w_qkv[layer], "narrow", axis=0, tiled=True),
            lax.all_gather(w_out[layer], "narrow", axis=0, tiled=True),
            lax.all_gather(w_up[layer], "narrow", axis=0, tiled=True),
            lax.all_gather(w_down[layer], "narrow", axis=0, tiled=True),
            lax.all_gather(norm_gains[layer], "narrow", axis=1, tiled=True),
            lax.all_gather(norm_biases[layer], "narrow", axis=1, tiled=True),
        )
        qkv_w, out_w, up_w, down_w, gains, biases = full
        branch = grad.astype(jnp.bfloat16)
        grad_down = outer_sum(active, branch)
        grad_active = times_back(branch, down_w)
        _, gelu_pull = jax.vjp(partial(jax.nn.gelu, approximate=True), upper)
        grad_upper = gelu_pull(grad_active)[0].astype(jnp.bfloat16)
        grad_up = outer_sum(second, grad_upper)
        grad_second = times_back(grad_upper, up_w)
        grad_norm, gain_two, bias_two = norm_back(
            grad_second, normed_two, inverse_two, gains[1].astype(jnp.float32)
        )
        grad_mid = grad + grad_norm
        branch = grad_mid.astype(jnp.bfloat16)
        grad_out = outer_sum(context, branch)
        grad_ctx = times_back(branch, out_w).astype(jnp.bfloat16)
        head_g = grad_ctx.reshape(rows, 2 * share, heads, head_dim)
        grad_q, clean_k_grad, clean_v_grad, noisy_k_grad, noisy_v_grad = attend_backward(
            *head_items + (head_g, logsum)
        )
        clean_gk, clean_gv = (
            lax.psum_scatter(
                clean_k_grad.astype(jnp.bfloat16), "narrow", scatter_dimension=1, tiled=True
            ).astype(jnp.float32),
            lax.psum_scatter(
                clean_v_grad.astype(jnp.bfloat16), "narrow", scatter_dimension=1, tiled=True
            ).astype(jnp.float32),
        )
        key_grad = jnp.stack([noisy_k_grad, clean_gk], axis=1)
        value_grad = jnp.stack([noisy_v_grad, clean_gv], axis=1)
        query_grad = grad_q.reshape(rows, 2, share, heads, head_dim)
        mixed_grad = jnp.stack(
            [
                rotate_back(query_grad, cosine, sine),
                rotate_back(key_grad, cosine, sine),
                value_grad,
            ],
            axis=3,
        )
        mixed_grad = mixed_grad.reshape(count, 3 * width).astype(jnp.bfloat16)
        grad_qkv = outer_sum(first, mixed_grad)
        grad_first = times_back(mixed_grad, qkv_w)
        grad_in, gain_one, bias_one = norm_back(
            grad_first, normed_one, inverse_one, gains[0].astype(jnp.float32)
        )
        grad = grad_mid + grad_in
        shards = (
            lax.psum_scatter(
                grad_qkv.astype(jnp.bfloat16), "narrow", scatter_dimension=0, tiled=True
            ).astype(jnp.float32),
            lax.psum_scatter(
                grad_out.astype(jnp.bfloat16), "narrow", scatter_dimension=0, tiled=True
            ).astype(jnp.float32),
            lax.psum_scatter(
                grad_up.astype(jnp.bfloat16), "narrow", scatter_dimension=0, tiled=True
            ).astype(jnp.float32),
            lax.psum_scatter(
                grad_down.astype(jnp.bfloat16), "narrow", scatter_dimension=0, tiled=True
            ).astype(jnp.float32),
            lax.psum_scatter(
                jnp.stack([gain_one, gain_two]).astype(jnp.bfloat16),
                "narrow",
                scatter_dimension=1,
                tiled=True,
            ).astype(jnp.float32),
            lax.psum_scatter(
                jnp.stack([bias_one, bias_two]).astype(jnp.bfloat16),
                "narrow",
                scatter_dimension=1,
                tiled=True,
            ).astype(jnp.float32),
        )
        shards = lax.psum(
            (shards[0], shards[1], shards[2], shards[3], shards[4], shards[5]), "wide"
        )
        grad_list[layer] = shards
    stacked = tuple(
        (jnp.stack([grad_list[layer][kind] for layer in range(layers)]) for kind in range(6))
    )
    grad_tokens = grad.reshape(tokens.shape).astype(jnp.bfloat16)
    return (
        result,
        grad_tokens,
        stacked[0],
        stacked[1],
        stacked[2],
        stacked[3],
        stacked[4],
        stacked[5][:, 0],
        stacked[5][:, 1],
    )


def solution(mesh):
    return jax.shard_map(
        on_device,
        mesh=mesh,
        in_specs=(
            P("wide", None, "narrow", None),
            P("wide"),
            P(None, "narrow", None),
            P(None, "narrow", None),
            P(None, "narrow", None),
            P(None, "narrow", None),
            P(None, None, "narrow"),
            P(None, None, "narrow"),
            P("wide", None, "narrow", None),
        ),
        out_specs=(
            P("wide", None, "narrow", None),
            P("wide", None, "narrow", None),
            P(None, "narrow", None),
            P(None, "narrow", None),
            P(None, "narrow", None),
            P(None, "narrow", None),
            P(None, None, "narrow"),
            P(None, "narrow"),
            P(None, "narrow"),
        ),
        check_vma=False,
    )
```

profile of v0, /device:TPU:0, one launch (start us, length us, event | category | flops | bytes accessed | tf_op | source)
XLA Modules:
  0.0 1759.0 jit_solution(2183330541820631966)
XLA Ops:
  10.5 11.0 all-gather
  21.4 13.1 all-gather.1
  36.3 4.6 fusion.267
  40.9 4.6 fusion.266
  46.7 16.3 all-gather.29.cloned.1.call-done
  63.1 5.7 copy.281
  68.8 4.1 convolution_bitcast_fusion
  89.1 9.6 all-gather.8
  98.7 4.6 fusion.263
  103.3 9.9 all-gather.9
  113.3 5.2 fusion.262
  124.0 4.6 while.116
  133.9 9.3 all-gather.33.cloned.1.call-done
  147.9 24.8 %all-gather.35.cloned.1.call-done = bf16[1,768,768]{2,1,0:T(8,128)(2,1)} async-done(((bf16[1,192,768]{2,1,0:T(8,128)(2,1)}), bf16[1,768,768]{2,1,0:T(8,128)(2,1)}) %all-gather.35.cloned.1.call-update) | async-done | bytes 1179664 | tf_op jit(solution)/shard_map/all_gather | solution.py:259
  175.5 56.6 %all-gather.37.cloned.1.call-done = bf16[1,768,3072]{2,1,0:T(8,128)(2,1)} async-done(((bf16[1,192,3072]{2,1,0:T(8,128)(2,1)}), bf16[1,768,3072]{2,1,0:T(8,128)(2,1)}) %all-gather.37.cloned.1.call-update) | async-done | bytes 4718608 | tf_op jit(solution)/shard_map/all_gather | solution.py:260
  232.1 7.5 fusion.204
  239.6 51.8 %all-gather.39.cloned.1.call-done = bf16[1,3072,768]{2,1,0:T(8,128)(2,1)} async-done(((bf16[1,768,768]{2,1,0:T(8,128)(2,1)}), bf16[1,3072,768]{2,1,0:T(8,128)(2,1)}) %all-gather.39.cloned.1.call-update) | async-done | bytes 4718608 | tf_op jit(solution)/shard_map/all_gather | solution.py:261
  291.4 8.4 fusion.318
  300.2 40.9 %all-gather.41.cloned.1.call-done = bf16[1,768,2304]{2,1,0:T(8,128)(2,1)} async-done(((bf16[1,192,2304]{2,1,0:T(8,128)(2,1)}), bf16[1,768,2304]{2,1,0:T(8,128)(2,1)}) %all-gather.41.cloned.1.call-update) | async-done | bytes 3538960 | tf_op jit(solution)/shard_map/all_gather | solution.py:258
  341.1 6.4 fusion.208
  347.5 6.8 reshape.2060
  371.4 19.8 %all-gather.43.cloned.1.call-done = bf16[1,1,1024,12,64]{2,4,3,1,0:T(8,128)(2,1)} async-done(((bf16[1,1,256,12,64]{2,4,3,1,0:T(8,128)(2,1)}), bf16[1,1,1024,12,64]{2,4,3,1,0:T(8,128)(2,1)}) %all-gather.43.cloned.1.call-update) | async-done | bytes 1572880 | tf_op jit(solution)/shard_map/all_gather | solution.py:277
  391.2 3.7 while.118
  398.7 64.0 %all-gather.45.cloned.1.call-done = bf16[1,1,1024,12,64]{2,1,4,3,0:T(2,128)(2,1)} async-done(((bf16[1,1,256,12,64]{2,1,4,3,0:T(2,128)(2,1)}), bf16[1,1,1024,12,64]{2,1,4,3,0:T(2,128)(2,1)}) %all-gather.45.cloned.1.call-update) | async-done | bytes 1572880 | tf_op jit(solution)/shard_map/all_gather | solution.py:278
  466.3 5.2 while.119
  466.5 5.0 bitcast_add_fusion.15
  473.1 19.0 %all-gather.47.cloned.1.call-done = bf16[1,768,768]{2,1,0:T(8,128)(2,1)} async-done(((bf16[1,192,768]{2,1,0:T(8,128)(2,1)}), bf16[1,768,768]{2,1,0:T(8,128)(2,1)}) %all-gather.47.cloned.1.call-update) | async-done | bytes 1179664 | tf_op jit(solution)/shard_map/all_gather | solution.py:259
  496.3 54.8 %all-gather.49.cloned.1.call-done = bf16[1,768,3072]{2,1,0:T(8,128)(2,1)} async-done(((bf16[1,192,3072]{2,1,0:T(8,128)(2,1)}), bf16[1,768,3072]{2,1,0:T(8,128)(2,1)}) %all-gather.49.cloned.1.call-update) | async-done | bytes 4718608 | tf_op jit(solution)/shard_map/all_gather | solution.py:260
  551.1 8.2 fusion.196
  559.2 51.2 %all-gather.51.cloned.1.call-done = bf16[1,3072,768]{2,1,0:T(8,128)(2,1)} async-done(((bf16[1,768,768]{2,1,0:T(8,128)(2,1)}), bf16[1,3072,768]{2,1,0:T(8,128)(2,1)}) %all-gather.51.cloned.1.call-update) | async-done | bytes 4718608 | tf_op jit(solution)/shard_map/all_gather | solution.py:261
  610.4 9.0 fusion.189
  634.0 5.8 while.120
  646.3 10.9 while.121
  668.5 68.6 %reduce-scatter.27.cloned.1.call-done = bf16[1,256,12,64]{1,3,2,0:T(8,128)(2,1)} async-done(((bf16[1,1024,12,64]{1,3,2,0:T(8,128)(2,1)}), bf16[1,256,12,64]{1,3,2,0:T(8,128)(2,1)}) %reduce-scatter.27.cloned.1.call-update) | async-done | bytes 393232 | tf_op jit(solution)/shard_map/reduce_scatter | solution.py:364
  738.2 33.3 %reduce-scatter.25.cloned.1.call-done = bf16[1,256,12,64]{1,3,2,0:T(8,128)(2,1)} async-done(((bf16[1,1024,12,64]{1,3,2,0:T(8,128)(2,1)}), bf16[1,256,12,64]{1,3,2,0:T(8,128)(2,1)}) %reduce-scatter.25.cloned.1.call-update) | async-done | bytes 393232 | tf_op jit(solution)/shard_map/reduce_scatter | solution.py:361
  782.0 6.4 fusion.182
  798.7 5.4 while.122
  810.6 11.2 while.123
  815.0 3.7 fusion.448
  829.2 7.4 convolution_convert_fusion.2
  837.8 8.3 convolution_convert_fusion
  847.5 5.8 convolution_convert_fusion.4
  854.6 6.4 convolution_convert_fusion.3
  862.5 8.4 convolution_convert_fusion.1
  879.7 21.9 %reduce-scatter.31.cloned.1.call-done = bf16[1,256,12,64]{1,3,2,0:T(8,128)(2,1)} async-done(((bf16[1,1024,12,64]{1,3,2,0:T(8,128)(2,1)}), bf16[1,256,12,64]{1,3,2,0:T(8,128)(2,1)}) %reduce-scatter.31.cloned.1.call-update) | async-done | bytes 393232 | tf_op jit(solution)/shard_map/reduce_scatter | solution.py:364
  902.7 32.7 %reduce-scatter.29.cloned.1.call-done = bf16[1,256,12,64]{1,3,2,0:T(8,128)(2,1)} async-done(((bf16[1,1024,12,64]{1,3,2,0:T(8,128)(2,1)}), bf16[1,256,12,64]{1,3,2,0:T(8,128)(2,1)}) %reduce-scatter.29.cloned.1.call-update) | async-done | bytes 393232 | tf_op jit(solution)/shard_map/reduce_scatter | solution.py:361
  941.8 3.9 convolution_convert_fusion.5
  946.4 20.9 %reduce-scatter.39.cloned.1.call-done = bf16[192,768]{1,0:T(8,128)(2,1)} async-done(((bf16[768,768]{1,0:T(8,128)(2,1)}), bf16[192,768]{1,0:T(8,128)(2,1)}) %reduce-scatter.39.cloned.1.call-update) | async-done | bytes 294928 | tf_op jit(solution)/shard_map/reduce_scatter | solution.py:390
  971.4 27.3 %reduce-scatter.37.cloned.1.call-done = bf16[192,768]{1,0:T(8,128)(2,1)} async-done(((bf16[768,768]{1,0:T(8,128)(2,1)}), bf16[192,768]{1,0:T(8,128)(2,1)}) %reduce-scatter.37.cloned.1.call-update) | async-done | bytes 294928 | tf_op jit(solution)/shard_map/reduce_scatter | solution.py:390
  1000.6 5.6 fusion.231
  1008.0 51.3 %reduce-scatter.43.cloned.1.call-done = bf16[192,3072]{1,0:T(8,128)(2,1)} async-done(((bf16[768,3072]{1,0:T(8,128)(2,1)}), bf16[192,3072]{1,0:T(8,128)(2,1)}) %reduce-scatter.43.cloned.1.call-update) | async-done | bytes 1179664 | tf_op jit(solution)/shard_map/reduce_scatter | solution.py:393
  1062.3 57.0 %reduce-scatter.47.cloned.1.call-done = bf16[768,768]{1,0:T(8,128)(2,1)} async-done(((bf16[3072,768]{1,0:T(8,128)(2,1)}), bf16[768,768]{1,0:T(8,128)(2,1)}) %reduce-scatter.47.cloned.1.call-update) | async-done | bytes 1179664 | tf_op jit(solution)/shard_map/reduce_scatter | solution.py:396
  1122.2 48.1 %reduce-scatter.35.cloned.1.call-done = bf16[192,2304]{1,0:T(8,128)(2,1)} async-done(((bf16[768,2304]{1,0:T(8,128)(2,1)}), bf16[192,2304]{1,0:T(8,128)(2,1)}) %reduce-scatter.35.cloned.1.call-update) | async-done | bytes 884752 | tf_op jit(solution)/shard_map/reduce_scatter | solution.py:387
  1172.8 58.2 %reduce-scatter.41.cloned.1.call-done = bf16[192,3072]{1,0:T(8,128)(2,1)} async-done(((bf16[768,3072]{1,0:T(8,128)(2,1)}), bf16[192,3072]{1,0:T(8,128)(2,1)}) %reduce-scatter.41.cloned.1.call-update) | async-done | bytes 1179664 | tf_op jit(solution)/shard_map/reduce_scatter | solution.py:393
  1233.9 57.2 %reduce-scatter.45.cloned.1.call-done = bf16[768,768]{1,0:T(8,128)(2,1)} async-done(((bf16[3072,768]{1,0:T(8,128)(2,1)}), bf16[768,768]{1,0:T(8,128)(2,1)}) %reduce-scatter.45.cloned.1.call-update) | async-done | bytes 1179664 | tf_op jit(solution)/shard_map/reduce_scatter | solution.py:396
  1293.9 47.4 %reduce-scatter.33.cloned.1.call-done = bf16[192,2304]{1,0:T(8,128)(2,1)} async-done(((bf16[768,2304]{1,0:T(8,128)(2,1)}), bf16[192,2304]{1,0:T(8,128)(2,1)}) %reduce-scatter.33.cloned.1.call-update) | async-done | bytes 884752 | tf_op jit(solution)/shard_map/reduce_scatter | solution.py:387
  1345.2 8.9 add_convert_fusion
  1354.1 14.0 reduce-scatter.55.cloned.1.call-done
  1368.9 26.3 %reduce-scatter.51.cloned.1.call-done = bf16[192,2]{1,0:T(8,128)(2,1)} async-done(((bf16[768,2]{1,0:T(8,128)(2,1)}), bf16[192,2]{1,0:T(8,128)(2,1)}) %reduce-scatter.51.cloned.1.call-update) | async-done | bytes 784
  1399.3 22.6 %reduce-scatter.53.cloned.1.call-done = bf16[192,2]{1,0:T(8,128)(2,1)} async-done(((bf16[768,2]{1,0:T(8,128)(2,1)}), bf16[192,2]{1,0:T(8,128)(2,1)}) %reduce-scatter.53.cloned.1.call-update) | async-done | bytes 784
  1422.7 25.9 %reduce-scatter.49.cloned.1.call-done = bf16[192,2]{1,0:T(8,128)(2,1)} async-done(((bf16[768,2]{1,0:T(8,128)(2,1)}), bf16[192,2]{1,0:T(8,128)(2,1)}) %reduce-scatter.49.cloned.1.call-update) | async-done | bytes 784
  1449.5 16.4 all-reduce.10
  1467.7 271.4 %all-reduce.14.cloned.1.call-done = (f32[1,192,2304]{2,1,0:T(8,128)}, f32[1,192,2304]{2,1,0:T(8,128)}, f32[1,192,768]{2,1,0:T(8,128)}, f32[1,192,768]{2,1,0:T(8,...) async-done(((f32[1,192,2304]{2,1,0:T(8,128)}, f32[1,192,2304]{2,1,0:T(8,128)}, ...) | async-done | bytes 14155792 | tf_op jit(solution)/shard_map/psum | solution.py:412
  1739.2 4.2 pad_maximum_fusion.2
  (630 shorter events, 241.7 us)
Async XLA Ops:
  7.2 55.9 %all-gather.29.cloned.1.call-start = ((), (), s32[]{:S(2)}) async-start(), calls=%async_computation.28 | async-start | bytes 4423680 | tf_op jit(solution)/shard_map/all_gather | solution.py:258
  10.0 25.1 %copy-start.19 = (bf16[1,2,256,768]{3,2,1,0:T(8,128)(2,1)S(1)}, bf16[1,2,256,768]{3,2,1,0:T(8,128)(2,1)}, u32[]{:S(2)}) copy-start(bf16[1,2,256,768]{3,2,1,0:T(8,128)(2,1)} %param.25) | copy-start | bytes 2359300
  10.0 114.0 %all-gather.31.cloned.1.call-start = ((), (), s32[]{:S(2)}) async-start(), calls=%async_computation.29 | async-start | bytes 1966080 | tf_op jit(solution)/shard_map/all_gather | solution.py:277
  40.9 27.9 %copy-start.102 = (f32[768]{0:T(1024)}, f32[768]{0:T(1024)S(1)}, u32[]{:S(2)}) copy-start(f32[768]{0:T(1024)S(1)} %get-tuple-element.1596) | copy-start | bytes 9220
  40.9 191.1 %copy-start.110 = (f32[768]{0:T(1024)}, f32[768]{0:T(1024)S(1)}, u32[]{:S(2)}) copy-start(f32[768]{0:T(1024)S(1)} %get-tuple-element.1595) | copy-start | bytes 9220
  46.3 28.8 %copy-start.78 = (f32[256,32]{0,1:T(8,128)}, f32[256,32]{0,1:T(8,128)S(1)}, u32[]{:S(2)}) copy-start(f32[256,32]{0,1:T(8,128)S(1)} %get-tuple-element.1829) | copy-start | bytes 98308
  46.3 28.8 %copy-start.80 = (f32[256,32]{0,1:T(8,128)}, f32[256,32]{0,1:T(8,128)S(1)}, u32[]{:S(2)}) copy-start(f32[256,32]{0,1:T(8,128)S(1)} %get-tuple-element.1830) | copy-start | bytes 98308
  77.4 65.8 %all-gather.33.cloned.1.call-start = ((), (), s32[]{:S(2)}) async-start(), calls=%async_computation.30 | async-start | bytes 1966080 | tf_op jit(solution)/shard_map/all_gather | solution.py:278
  80.0 92.7 %all-gather.35.cloned.1.call-start = ((), (), s32[]{:S(2)}) async-start(), calls=%async_computation.31 | async-start | bytes 1474560 | tf_op jit(solution)/shard_map/all_gather | solution.py:259
  82.0 150.1 %all-gather.37.cloned.1.call-start = ((), (), s32[]{:S(2)}) async-start(), calls=%async_computation.32 | async-start | bytes 5898240 | tf_op jit(solution)/shard_map/all_gather | solution.py:260
  83.6 207.8 %all-gather.39.cloned.1.call-start = ((), (), s32[]{:S(2)}) async-start(), calls=%async_computation.33 | async-start | bytes 5898240 | tf_op jit(solution)/shard_map/all_gather | solution.py:261
  87.2 253.9 %all-gather.41.cloned.1.call-start = ((), (), s32[]{:S(2)}) async-start(), calls=%async_computation.34 | async-start | bytes 4423680 | tf_op jit(solution)/shard_map/all_gather | solution.py:258
  87.9 303.2 %all-gather.43.cloned.1.call-start = ((), (), s32[]{:S(2)}) async-start(), calls=%async_computation.35 | async-start | bytes 1966080 | tf_op jit(solution)/shard_map/all_gather | solution.py:277
  89.1 29.4 %copy-start.64 = (bf16[1,1,256,12,64]{2,4,3,1,0:T(8,128)(2,1)S(1)}, bf16[1,1,256,12,64]{2,4,3,1,0:T(8,128)(2,1)}, u32[]{:S(2)}) copy-start(bf16[1,1,256,12,64]{2,4,3,1,0:T(8,128)(2,1)} %get-tuple-element.1798) | copy-start | bytes 1179652
  103.3 237.8 %copy-start.113 = (f32[768]{0:T(1024)}, f32[768]{0:T(1024)S(1)}, u32[]{:S(2)}) copy-start(f32[768]{0:T(1024)S(1)} %get-tuple-element.1592) | copy-start | bytes 9220
  146.9 28.2 %copy-start = (bf16[1,512,12,64]{1,3,2,0:T(8,128)(2,1)}, bf16[1,512,12,64]{1,3,2,0:T(8,128)(2,1)S(1)}, u32[]{:S(2)}) copy-start(bf16[1,512,12,64]{1,3,2,0:T(8,128)(2,1)S(1)} %get-tuple-element.2696) | copy-start | bytes 2359300
  175.1 64.5 %copy-start.32 = (f32[512,768]{1,0:T(8,128)}, f32[512,768]{1,0:T(8,128)S(1)}, u32[]{:S(2)}) copy-start(f32[512,768]{1,0:T(8,128)S(1)} %get-tuple-element.1834) | copy-start | bytes 4718596
  175.1 56.9 %copy-start.127 = (f32[768]{0:T(1024)S(1)}, f32[768]{0:T(1024)}, u32[]{:S(2)}) copy-start(f32[768]{0:T(1024)} %get-tuple-element.1597) | copy-start | bytes 9220
  175.1 64.4 %copy-start.104 = (f32[512]{0:T(512)}, f32[512]{0:T(512)S(1)}, u32[]{:S(2)}) copy-start(f32[512]{0:T(512)S(1)} %broadcast_multiply_fusion.10) | copy-start | bytes 6148
  175.5 64.1 %copy-start.118 = (f32[512]{0:T(512)}, f32[512]{0:T(512)S(1)}, u32[]{:S(2)}) copy-start(f32[512]{0:T(512)S(1)} %add_rsqrt_fusion.2) | copy-start | bytes 6148
  299.9 47.6 %copy-start.13 = (f32[512,768]{1,0:T(8,128)}, f32[512,768]{1,0:T(8,128)S(1)}, u32[]{:S(2)}) copy-start(f32[512,768]{1,0:T(8,128)S(1)} %get-tuple-element.1836) | copy-start | bytes 4718596
  299.9 41.2 %copy-start.129 = (f32[768]{0:T(1024)S(1)}, f32[768]{0:T(1024)}, u32[]{:S(2)}) copy-start(f32[768]{0:T(1024)} %get-tuple-element.1594) | copy-start | bytes 9220
  299.9 47.6 %copy-start.106 = (f32[512]{0:T(512)}, f32[512]{0:T(512)S(1)}, u32[]{:S(2)}) copy-start(f32[512]{0:T(512)S(1)} %broadcast_multiply_fusion.9) | copy-start | bytes 6148
  300.2 47.3 %copy-start.121 = (f32[512]{0:T(512)}, f32[512]{0:T(512)S(1)}, u32[]{:S(2)}) copy-start(f32[512]{0:T(512)S(1)} %add_rsqrt_fusion.1) | copy-start | bytes 6148
  360.2 102.5 %all-gather.45.cloned.1.call-start = ((), (), s32[]{:S(2)}) async-start(), calls=%async_computation.36 | async-start | bytes 3932160 | tf_op jit(solution)/shard_map/all_gather | solution.py:278
  365.0 30.6 %copy-start.39 = (bf16[256,12,64]{0,2,1:T(8,128)(2,1)}, bf16[256,12,64]{0,2,1:T(8,128)(2,1)S(1)}, u32[]{:S(2)}) copy-start(bf16[256,12,64]{0,2,1:T(8,128)(2,1)S(1)} %get-tuple-element.1794) | copy-start | bytes 1179652
  365.0 127.1 %all-gather.47.cloned.1.call-start = ((), (), s32[]{:S(2)}) async-start(), calls=%async_computation.37 | async-start | bytes 1474560 | tf_op jit(solution)/shard_map/all_gather | solution.py:259
  365.6 185.4 %all-gather.49.cloned.1.call-start = ((), (), s32[]{:S(2)}) async-start(), calls=%async_computation.38 | async-start | bytes 5898240 | tf_op jit(solution)/shard_map/all_gather | solution.py:260
  366.4 244.1 %all-gather.51.cloned.1.call-start = ((), (), s32[]{:S(2)}) async-start(), calls=%async_computation.39 | async-start | bytes 5898240 | tf_op jit(solution)/shard_map/all_gather | solution.py:261
  366.9 370.2 %reduce-scatter.27.cloned.1.call-start = ((), (), s32[]{:S(2)}) async-start(), calls=%async_computation.17 | async-start | bytes 1966080 | tf_op jit(solution)/shard_map/reduce_scatter | solution.py:364
  371.0 269.5 %copy-start.5 = (f32[2,12,128,128]{2,3,1,0:T(8,128)}, f32[2,12,128,128]{2,3,1,0:T(8,128)S(1)}, u32[]{:S(2)}) copy-start(f32[2,12,128,128]{2,3,1,0:T(8,128)S(1)} %get-tuple-element.1838) | copy-start | bytes 4718596
  398.7 67.6 %copy-start.98 = (f32[1,12,512]{2,1,0:T(8,128)S(1)}, f32[1,12,512]{2,1,0:T(8,128)}, u32[]{:S(2)}) copy-start(f32[1,12,512]{2,1,0:T(8,128)} %copy-done.97) | copy-start | bytes 73732
  494.8 56.3 %copy-start.116 = (f32[768]{0:T(1024)S(1)}, f32[768]{0:T(1024)}, u32[]{:S(2)}) copy-start(f32[768]{0:T(1024)} %get-tuple-element.1591) | copy-start | bytes 9220
  494.8 56.3 %copy-start.130 = (f32[768]{0:T(1024)S(1)}, f32[768]{0:T(1024)}, u32[]{:S(2)}) copy-start(f32[768]{0:T(1024)} %get-tuple-element.1593) | copy-start | bytes 9220
  494.8 128.2 %copy-start.108 = (f32[512]{0:T(512)}, f32[512]{0:T(512)S(1)}, u32[]{:S(2)}) copy-start(f32[512]{0:T(512)S(1)} %broadcast_multiply_fusion.8) | copy-start | bytes 6148
  496.3 123.2 %copy-start.124 = (f32[512]{0:T(512)}, f32[512]{0:T(512)S(1)}, u32[]{:S(2)}) copy-start(f32[512]{0:T(512)S(1)} %add_rsqrt_fusion) | copy-start | bytes 6148
  551.1 59.4 %copy-start.85 = (bf16[512,768]{1,0:T(8,128)(2,1)S(1)}, bf16[512,768]{1,0:T(8,128)(2,1)}, u32[]{:S(2)}) copy-start(bf16[512,768]{1,0:T(8,128)(2,1)} %bitcast_convert_fusion) | copy-start | bytes 2359300
  657.2 114.3 %reduce-scatter.25.cloned.1.call-start = ((), (), s32[]{:S(2)}) async-start(), calls=%async_computation.16 | async-start | bytes 1966080 | tf_op jit(solution)/shard_map/reduce_scatter | solution.py:361
  657.8 243.8 %reduce-scatter.31.cloned.1.call-start = ((), (), s32[]{:S(2)}) async-start(), calls=%async_computation.19 | async-start | bytes 1966080 | tf_op jit(solution)/shard_map/reduce_scatter | solution.py:364
  665.5 71.6 %copy-start.65 = (bf16[1,1,256,12,64]{2,4,3,1,0:T(8,128)(2,1)S(1)}, bf16[1,1,256,12,64]{2,4,3,1,0:T(8,128)(2,1)}, u32[]{:S(2)}) copy-start(bf16[1,1,256,12,64]{2,4,3,1,0:T(8,128)(2,1)} %stack_reshape.14) | copy-start | bytes 1179652
  821.8 113.6 %reduce-scatter.29.cloned.1.call-start = ((), (), s32[]{:S(2)}) async-start(), calls=%async_computation.18 | async-start | bytes 1966080 | tf_op jit(solution)/shard_map/reduce_scatter | solution.py:361
  822.4 145.0 %reduce-scatter.39.cloned.1.call-start = ((), (), s32[]{:S(2)}) async-start(), calls=%async_computation.23 | async-start | bytes 1474560 | tf_op jit(solution)/shard_map/reduce_scatter | solution.py:390
  826.0 172.7 %reduce-scatter.37.cloned.1.call-start = ((), (), s32[]{:S(2)}) async-start(), calls=%async_computation.22 | async-start | bytes 1474560 | tf_op jit(solution)/shard_map/reduce_scatter | solution.py:390
  829.1 230.2 %reduce-scatter.43.cloned.1.call-start = ((), (), s32[]{:S(2)}) async-start(), calls=%async_computation.25 | async-start | bytes 5898240 | tf_op jit(solution)/shard_map/reduce_scatter | solution.py:393
  836.6 282.7 %reduce-scatter.47.cloned.1.call-start = ((), (), s32[]{:S(2)}) async-start(), calls=%async_computation.27 | async-start | bytes 5898240 | tf_op jit(solution)/shard_map/reduce_scatter | solution.py:396
  846.1 324.2 %reduce-scatter.35.cloned.1.call-start = ((), (), s32[]{:S(2)}) async-start(), calls=%async_computation.21 | async-start | bytes 4423680 | tf_op jit(solution)/shard_map/reduce_scatter | solution.py:387
  853.3 377.7 %reduce-scatter.41.cloned.1.call-start = ((), (), s32[]{:S(2)}) async-start(), calls=%async_computation.24 | async-start | bytes 5898240 | tf_op jit(solution)/shard_map/reduce_scatter | solution.py:393
  861.1 430.0 %reduce-scatter.45.cloned.1.call-start = ((), (), s32[]{:S(2)}) async-start(), calls=%async_computation.26 | async-start | bytes 5898240 | tf_op jit(solution)/shard_map/reduce_scatter | solution.py:396
  870.9 470.4 %reduce-scatter.33.cloned.1.call-start = ((), (), s32[]{:S(2)}) async-start(), calls=%async_computation.20 | async-start | bytes 4423680 | tf_op jit(solution)/shard_map/reduce_scatter | solution.py:387
  879.7 56.8 %copy-start.42 = (f32[1,1,256,12,64]{2,4,3,1,0:T(8,128)S(1)}, f32[1,1,256,12,64]{2,4,3,1,0:T(8,128)}, u32[]{:S(2)}) copy-start(f32[1,1,256,12,64]{2,4,3,1,0:T(8,128)} %stack_reshape.15) | copy-start | bytes 2359300
  879.7 56.8 %copy-start.43 = (f32[1,2,256,12,32]{2,1,4,3,0:T(2,128)S(1)}, f32[1,2,256,12,32]{2,1,4,3,0:T(2,128)}, u32[]{:S(2)}) copy-start(f32[1,2,256,12,32]{2,1,4,3,0:T(2,128)} %get-tuple-element.1789) | copy-start | bytes 2359300
  879.7 56.8 %copy-start.44 = (f32[1,2,256,12,32]{2,1,4,3,0:T(2,128)S(1)}, f32[1,2,256,12,32]{2,1,4,3,0:T(2,128)}, u32[]{:S(2)}) copy-start(f32[1,2,256,12,32]{2,1,4,3,0:T(2,128)} %get-tuple-element.1790) | copy-start | bytes 2359300
  945.7 23.5 %copy-start.139 = (bf16[768]{0:T(1024)(128)(2,1)S(1)}, bf16[768]{0:T(1024)(128)(2,1)}, u32[]{:S(2)}) copy-start(bf16[768]{0:T(1024)(128)(2,1)} %get-tuple-element.1577) | copy-start | bytes 4612
  945.7 23.5 %copy-start.138 = (bf16[768]{0:T(1024)(128)(2,1)S(1)}, bf16[768]{0:T(1024)(128)(2,1)}, u32[]{:S(2)}) copy-start(bf16[768]{0:T(1024)(128)(2,1)} %get-tuple-element.1587) | copy-start | bytes 4612
  945.7 24.5 %copy-start.137 = (bf16[768]{0:T(1024)(128)(2,1)S(1)}, bf16[768]{0:T(1024)(128)(2,1)}, u32[]{:S(2)}) copy-start(bf16[768]{0:T(1024)(128)(2,1)} %get-tuple-element.1575) | copy-start | bytes 4612
  945.7 24.5 %copy-start.136 = (bf16[768]{0:T(1024)(128)(2,1)S(1)}, bf16[768]{0:T(1024)(128)(2,1)}, u32[]{:S(2)}) copy-start(bf16[768]{0:T(1024)(128)(2,1)} %get-tuple-element.1590) | copy-start | bytes 4612
  945.8 54.8 %copy-start.20 = (bf16[1,2,256,768]{3,2,1,0:T(8,128)(2,1)S(1)}, bf16[1,2,256,768]{3,2,1,0:T(8,128)(2,1)}, u32[]{:S(2)}) copy-start(bf16[1,2,256,768]{3,2,1,0:T(8,128)(2,1)} %param.25) | copy-start | bytes 2359300
  945.8 54.8 %copy-start.103 = (f32[768]{0:T(1024)S(1)}, f32[768]{0:T(1024)}, u32[]{:S(2)}) copy-start(f32[768]{0:T(1024)} %copy-done.102) | copy-start | bytes 9220
  945.8 422.3 %reduce-scatter.55.cloned.1.call-start = ((), (), s32[]{:S(2)}) async-start(), calls=%async_computation.43 | async-start | bytes 245760
  970.1 425.2 %reduce-scatter.51.cloned.1.call-start = ((), (), s32[]{:S(2)}) async-start(), calls=%async_computation.41 | async-start | bytes 245760
  971.1 450.8 %reduce-scatter.53.cloned.1.call-start = ((), (), s32[]{:S(2)}) async-start(), calls=%async_computation.42 | async-start | bytes 245760
  1007.0 441.6 %reduce-scatter.49.cloned.1.call-start = ((), (), s32[]{:S(2)}) async-start(), calls=%async_computation.40 | async-start | bytes 245760
  1008.0 731.1 %all-reduce.14.cloned.1.call-start = ((), (), s32[]{:S(2)}) async-start(), calls=%async_computation.44 | async-start | bytes 28311552 | tf_op jit(solution)/shard_map/psum | solution.py:412
  1345.2 51.0 %copy-start.8 = (f32[512,768]{1,0:T(8,128)S(1)}, f32[512,768]{1,0:T(8,128)}, u32[]{:S(2)}) copy-start(f32[512,768]{1,0:T(8,128)} %copy-done.6) | copy-start | bytes 4718596
  (116 other events, 378.0 us)
Sparse Core Ops, SparseCore 0:
  10.5 52.5 all-gather.28
  77.6 31.9 all-gather.30
  112.0 31.2 all-gather.32
  144.9 27.7 all-gather.34
  175.0 57.0 all-gather.36
  234.3 57.0 all-gather.38
  293.8 47.2 all-gather.40
  360.3 30.8 all-gather.42
  393.6 69.0 all-gather.44
  464.4 27.7 all-gather.46
  494.0 57.0 all-gather.48
  553.3 57.0 all-gather.50
  657.3 79.7 reduce-scatter.26
  740.5 30.9 reduce-scatter.24
  821.9 79.6 reduce-scatter.30
  904.4 30.9 reduce-scatter.28
  938.7 28.5 reduce-scatter.38
  970.1 28.5 reduce-scatter.36
  1002.2 57.0 reduce-scatter.42
  1062.2 57.0 reduce-scatter.46
  1123.0 47.2 reduce-scatter.34
  1173.8 57.0 reduce-scatter.40
  1233.9 57.0 reduce-scatter.44
  1294.0 47.2 reduce-scatter.32
  1344.0 23.9 reduce-scatter.54
  1371.2 23.9 reduce-scatter.50
  1397.8 23.9 reduce-scatter.52
  1424.6 23.9 reduce-scatter.48
  1452.2 286.9 all-reduce.13
where the time goes:
time: 1770 us; the launch traced here: 1760 us
  waiting for transfers between devices  1300 us (73%)
  matrix products  187 us (11%)
  local copies, waits for them, and re-layouts  108 us (6%)
  other arithmetic  85.5 us (5%)
  blocking collectives  60 us (3%)
    psum x1, waiting for transfers between devices, on_device(): lax.psum((shards[0], shards[1], shards[2], shards[3], shards[4], shards[5...  271 us
    reduce_scatter x2, waiting for transfers between devices, on_device(): lax.psum_scatter(grad_down.astype(jnp.bfloat16), 'narrow', scatter_dimens...  114 us
    all_gather x2, waiting for transfers between devices, on_device(): lax.all_gather(w_up[layer], 'narrow', axis=0, tiled=True)  111 us
    reduce_scatter x2, waiting for transfers between devices, on_device(): lax.psum_scatter(grad_up.astype(jnp.bfloat16), 'narrow', scatter_dimensio...  109 us
    all_gather x2, waiting for transfers between devices, on_device(): lax.all_gather(w_down[layer], 'narrow', axis=0, tiled=True)  103 us
    reduce_scatter x2, waiting for transfers between devices, on_device(): lax.psum_scatter(grad_qkv.astype(jnp.bfloat16), 'narrow', scatter_dimensi...  95.5 us
    unnamed x33, waiting for transfers between devices  92.6 us
    reduce_scatter x2, waiting for transfers between devices, on_device(): lax.psum_scatter(clean_v_grad.astype(jnp.bfloat16), 'narrow', scatter_dim...  90.5 us
  transfers between devices with their start and end apart: 29, of which 28 were waited for; matrix products, arithmetic and copies ran while one was open for 13% of the time, Pallas kernels for 0%

commit v1 on v0

--- a/solution.py
+++ b/solution.py
@@ -3,10 +3,469 @@
 import jax
 import jax.numpy as jnp
 from jax import lax
+from jax.experimental import pallas as pl
+from jax.experimental.pallas import tpu as pltpu
 from jax.sharding import PartitionSpec as P
 
 H = 12
 BLOCK = 16
+NEG = -1e30
+EPS = 1e-05
+MESH = pl.DeviceIdType.MESH
+F32 = jnp.float32
+BF16 = jnp.bfloat16
+GELU_C = 0.7978845608028654
+GELU_A = 0.044715
+
+
+def dot(a, b):
+    return jnp.dot(a, b, preferred_element_type=F32)
+
+
+def dot_nt(a, b):
+    return lax.dot_general(a, b, (((1,), (1,)), ((), ())), preferred_element_type=F32)
+
+
+def dot_tn(a, b):
+    return lax.dot_general(a, b, (((0,), (0,)), ((), ())), preferred_element_type=F32)
+
+
+def tile_at(index, size):
+    return pl.ds(pl.multiple_of(index * size, size), size)
+
+
+def loop(count, body):
+    lax.fori_loop(0, count, lambda i, _: (body(i), None)[1], None)
+
+
+def swap_halves(x, first):
+    return jnp.where(first, pltpu.roll(x, 96, 1), pltpu.roll(x, 32, 1))
+
+
+def lane_masks(rows):
+    lane = lax.broadcasted_iota(jnp.int32, (rows, 128), 1)
+    return lane % 64 < 32
+
+
+def head_masks():
+    lane = lax.broadcasted_iota(jnp.int32, (1, 128), 1)
+    low = (lane < 64).astype(F32)
+    return low, 1.0 - low
+
+
+def norm_into(src, dst, gain, bias, rows):
+    step = 32
+
+    def body(i):
+        at = tile_at(i, step)
+        x = src[at, :].astype(F32)
+        c = x - jnp.mean(x, axis=-1, keepdims=True)
+        inv = lax.rsqrt(jnp.mean(c * c, axis=-1, keepdims=True) + EPS)
+        dst[at, :] = (c * inv * gain + bias).astype(BF16)
+
+    loop(rows // step, body)
+
+
+class Gather:
+    def __init__(self, here, shard, full, send, recv, base, lsem):
+        self.n, self.w = here
+        self.core = lax.rem(self.w, 2)
+        self.shard, self.full, self.send, self.recv, self.base, self.lsem = (
+            shard, full, send, recv, base, lsem)
+        self.rows = shard.shape[0]
+        self.half = self.rows // 2
+        self.quarter = self.rows // 4
+        self.x, self.y, self.d, self.s = (
+            (self.n ^ 1, self.w), (self.n ^ 2, self.w), (self.n ^ 3, self.w), (self.n, self.w ^ 1))
+
+    def region(self, owner, core, quarter=None):
+        start = owner * self.rows + core * self.half
+        if quarter is None:
+            return self.full.at[pl.ds(pl.multiple_of(start, 16), self.half)]
+        return self.full.at[pl.ds(pl.multiple_of(start + quarter * self.quarter, 16), self.quarter)]
+
+    def copy(self, slot, src, dst, device):
+        k = self.base + slot
+        return pltpu.make_async_remote_copy(
+            src_ref=src, dst_ref=dst, send_sem=self.send.at[k], recv_sem=self.recv.at[k],
+            device_id=device, device_id_type=MESH)
+
+    def own(self):
+        return pltpu.make_async_copy(
+            self.shard, self.full.at[pl.ds(pl.multiple_of(self.n * self.rows, 16), self.rows)], self.lsem)
+
+    def plain(self, slot, region, device):
+        return self.copy(slot, region, region, device)
+
+    def issue(self):
+        src = self.shard.at[pl.ds(pl.multiple_of(self.core * self.half, 16), self.half)]
+        dst = self.region(self.n, self.core)
+        self.copy(0, src, dst, self.x).start()
+        self.copy(1, src, dst, self.y).start()
+        self.own().start()
+
+    def forward(self):
+        nx, ny = self.x[0], self.y[0]
+        self.plain(0, self.region(nx, self.core), self.x).wait_recv()
+        self.plain(2, self.region(nx, self.core, 0), self.y).start()
+        self.plain(4, self.region(nx, self.core), self.s).start()
+        self.plain(1, self.region(ny, self.core), self.y).wait_recv()
+        self.plain(3, self.region(ny, self.core, 1), self.x).start()
+        self.plain(5, self.region(ny, self.core), self.s).start()
+
+    def finish(self):
+        nd = self.d[0]
+        self.plain(2, self.region(nd, self.core, 0), self.y).wait_recv()
+        self.plain(3, self.region(nd, self.core, 1), self.x).wait_recv()
+        self.plain(6, self.region(nd, self.core), self.s).start()
+
+    def use(self):
+        other = 1 - self.core
+        for slot, who in ((4, self.x), (5, self.y), (6, self.d)):
+            self.plain(slot, self.region(who[0], other), self.s).wait_recv()
+        self.own().wait()
+
+    def drain(self):
+        src = self.shard.at[pl.ds(pl.multiple_of(self.core * self.half, 16), self.half)]
+        dst = self.region(self.n, self.core)
+        self.copy(0, src, dst, self.x).wait_send()
+        self.copy(1, src, dst, self.y).wait_send()
+        nx, ny, nd = self.x[0], self.y[0], self.d[0]
+        self.plain(2, self.region(nx, self.core, 0), self.y).wait_send()
+        self.plain(3, self.region(ny, self.core, 1), self.x).wait_send()
+        self.plain(4, self.region(nx, self.core), self.s).wait_send()
+        self.plain(5, self.region(ny, self.core), self.s).wait_send()
+        self.plain(6, self.region(nd, self.core), self.s).wait_send()
+
+
+def forward_kernel(
+    layers,
+    tok, prm, cosr, sinr, bias_c, bias_n, wq, wo, wu, wd,
+    result, fq, fo, fu, fd, prm_out, h_out, q_out, nkv_out, kv_out, lse_out, ctx_out, mid_out, u_out,
+    gq, go, gu, gd, prm_buf, par, hid, a, q, nkv, kv, score, top, lse, ctx, mid, u, act,
+    send, recv, lsem, psend, precv, ksend, krecv, ssem,
+):
+    n = lax.axis_index("narrow")
+    w = lax.axis_index("wide")
+    rows, width = tok.shape
+    share = rows // 2
+    group = share
+    pairs = width // 128
+    ff = wu.shape[2]
+    peers = ((n ^ 1, w), (n ^ 2, w), (n ^ 3, w))
+
+    barrier = pltpu.get_barrier_semaphore()
+    for device in peers + ((n, w ^ 1),):
+        pl.semaphore_signal(barrier, inc=1, device_id=device, device_id_type=MESH)
+    pl.semaphore_wait(barrier, 4)
+
+    tensors = []
+    for layer in range(layers):
+        for kind, (shard, full) in enumerate(((wq, gq), (wo, go), (wu, gu), (wd, gd))):
+            k = layer * 4 + kind
+            tensors.append(Gather((n, w), shard.at[layer], full.at[layer], send, recv, 7 * k, lsem.at[k]))
+
+    def params(i):
+        return pltpu.make_async_remote_copy(
+            src_ref=prm, dst_ref=prm_buf.at[i], send_sem=psend.at[i], recv_sem=precv.at[i],
+            device_id=peers[i], device_id_type=MESH)
+
+    def share_kv(layer, i):
+        region = kv.at[layer, tile_at(n, share)]
+        return pltpu.make_async_remote_copy(
+            src_ref=region, dst_ref=region, send_sem=ksend.at[3 * layer + i],
+            recv_sem=krecv.at[3 * layer + i], device_id=peers[i], device_id_type=MESH)
+
+    def recv_kv(layer, i):
+        region = kv.at[layer, tile_at(peers[i][0], share)]
+        return pltpu.make_async_remote_copy(
+            src_ref=region, dst_ref=region, send_sem=ksend.at[3 * layer + i],
+            recv_sem=krecv.at[3 * layer + i], device_id=peers[i], device_id_type=MESH)
+
+    gives = (n % 2 == 0, n < 2, n < 2)
+    takes = (n % 2 == 1, n >= 2, n >= 2)
+
+    for i in range(3):
+        params(i).start()
+    tensors[0].issue()
+    tensors[1].issue()
+
+    def saves(layer):
+        pieces = [
+            (q, q_out.at[layer]), (nkv, nkv_out.at[layer]), (kv.at[layer], kv_out.at[layer]),
+            (lse, lse_out.at[layer]), (ctx, ctx_out.at[layer]), (mid, mid_out.at[layer]), (u, u_out.at[layer]),
+            (hid, h_out.at[layer]),
+        ]
+        return [pltpu.make_async_copy(s, d, ssem.at[layer * 8 + k]) for k, (s, d) in enumerate(pieces)]
+
+    def weight_saves():
+        pieces = ((gq, fq), (go, fo), (gu, fu), (gd, fd))
+        out = []
+        for layer in range(layers):
+            for kind, (s, d) in enumerate(pieces):
+                k = layer * 4 + kind
+                out.append(pltpu.make_async_copy(s.at[layer], d.at[layer], ssem.at[8 * layers + k]))
+        return out
+
+    for i in range(3):
+        params(i).wait_recv()
+    par[...] = prm[...] + prm_buf[0] + prm_buf[1] + prm_buf[2]
+    prm_out[...] = par[...]
+
+    first = lane_masks(rows)
+    masks = head_masks()
+    lanes = lax.broadcasted_iota(jnp.int32, (rows, 128), 1)
+
+    for layer in range(layers):
+        t_qkv, t_out, t_up, t_down = tensors[4 * layer:4 * layer + 4]
+        later = tensors[4 * layer + 4:]
+        gain1, gain2 = par[2 * layer:2 * layer + 1, :], par[2 * layer + 1:2 * layer + 2, :]
+        at = 2 * layers + 2 * layer
+        bias1, bias2 = par[at:at + 1, :], par[at + 1:at + 2, :]
+        saved = saves(layer)
+        before = saves(layer - 1) if layer else None
+        if layer == 0:
+            norm_into(tok, a, gain1, bias1, rows)
+        else:
+            norm_into(hid, a, gain1, bias1, rows)
+        if layer == 0:
+            t_qkv.forward()
+        t_qkv.finish()
+        t_qkv.use()
+        if before:
+            before[0].wait()
+            before[1].wait()
+
+        wqkv = gq.at[layer]
+
+        def query_tile(j):
+            x = dot(a[...], wqkv[:, tile_at(j, 256)])
+            for part in range(2):
+                v = x[:, 128 * part:128 * part + 128]
+                v = v * cosr[...] + swap_halves(v, first) * sinr[...]
+                q[:, tile_at(2 * j + part, 128)] = (v.astype(BF16).astype(F32) * 0.125).astype(BF16)
+
+        def key_tile(j):
+            x = dot(a[...], wqkv[:, tile_at(j + 3, 256)])
+            for part in range(2):
+                v = x[:, 128 * part:128 * part + 128]
+                v = (v * cosr[...] + swap_halves(v, first) * sinr[...]).astype(BF16)
+                nkv[:, tile_at(2 * j + part, 128)] = v[:share]
+                kv[layer, tile_at(n, share), tile_at(2 * j + part, 128)] = v[share:]
+
+        def value_tile(j):
+            v = dot(a[...], wqkv[:, tile_at(j + 6, 256)]).astype(BF16)
+            nkv[:, tile_at(j + 3, 256)] = v[:share]
+            kv[layer, tile_at(n, share), tile_at(j + 3, 256)] = v[share:]
+
+        loop(3, key_tile)
+        loop(3, value_tile)
+        for i in range(3):
+            @pl.when(gives[i])
+            def _():
+                share_kv(layer, i).start()
+        loop(3, query_tile)
+        saved[0].start()
+        saved[1].start()
+        t_out.forward()
+        t_up.issue()
+        t_down.issue()
+        for i in range(3):
+            @pl.when(takes[i])
+            def _():
+                recv_kv(layer, i).wait_recv()
+        saved[2].start()
+        if before:
+            before[3].wait()
+            before[4].wait()
+
+        def pair_step(pair):
+            at_pair = tile_at(pair, 128)
+            at_value = tile_at(pair + pairs, 128)
+            q2 = q[:, at_pair].astype(F32)
+            outs = []
+            for h in range(2):
+                qm = (q2 * masks[h]).astype(BF16)
+                s = dot_nt(qm, kv[layer, tile_at(n, group), at_pair]) + bias_c[...]
+                score[:, tile_at(n, group)] = s
+                top[...] = jnp.maximum(s[:, :128], s[:, 128:])
+                s = dot_nt(qm[:share], nkv[:, at_pair]) + bias_n[...]
+                score[:share, 4 * group:5 * group] = s
+                top[:share] = jnp.maximum(top[:share], jnp.maximum(s[:, :128], s[:, 128:]))
+
+                def scores_of(g):
+                    s = dot_nt(qm, kv[layer, tile_at(g, group), at_pair])
+                    score[:, tile_at(g, group)] = s
+                    top[...] = jnp.maximum(top[...], jnp.maximum(s[:, :128], s[:, 128:]))
+
+                loop(n, scores_of)
+                most = jnp.max(top[...], axis=-1, keepdims=True)
+                p = jnp.exp(score[:share, 4 * group:5 * group] - most[:share])
+                part = p[:, :128] + p[:, 128:]
+                add = dot(p.astype(BF16), nkv[:, at_value])
+                zeros = jnp.zeros((share, 128), F32)
+
+                def probs_of(g, carry):
+                    total, out = carry
+                    p = jnp.exp(score[:, tile_at(g, group)] - most)
+                    total = total + p[:, :128] + p[:, 128:]
+                    out = out + dot(p.astype(BF16), kv[layer, tile_at(g, group), at_value])
+                    return total, out
+
+                total, out = lax.fori_loop(
+                    0, n + 1, probs_of,
+                    (jnp.concatenate([part, zeros], axis=0), jnp.concatenate([add, zeros], axis=0)))
+                total = jnp.sum(total, axis=-1, keepdims=True)
+                outs.append(out * (masks[h] / total))
+                lse[...] = jnp.where(lanes == 2 * pair + h, most + jnp.log(total), lse[...])
+            ctx[:, at_pair] = (outs[0] + outs[1]).astype(BF16)
+
+        loop(pairs, pair_step)
+        saved[3].start()
+        saved[4].start()
+        t_out.finish()
+        t_out.use()
+        t_up.forward()
+        if later:
+            later[0].issue()
+            later[1].issue()
+        if before:
+            before[5].wait()
+            before[6].wait()
+            before[7].wait()
+
+        def out_tile(j):
+            at = tile_at(j, 256)
+            base = (tok if layer == 0 else hid)[:, at].astype(F32)
+            mid[:, at] = base + dot(ctx[...], go[layer, :, at])
+
+        loop(width // 256, out_tile)
+        saved[5].start()
+        norm_into(mid, a, gain2, bias2, rows)
+        t_up.finish()
+        t_up.use()
+
+        def up_tile(j):
+            at = tile_at(j, 256)
+            x = dot(a[...], gu[layer, :, at])
+            u[:, at] = x
+            t = jnp.tanh(GELU_C * (x + GELU_A * (x * x * x)))
+            act[:, at] = (0.5 * x * (1.0 + t)).astype(BF16)
+
+        loop(ff // 256, up_tile)
+        saved[6].start()
+        t_down.forward()
+        if later:
+            later[0].forward()
+        t_down.finish()
+        t_down.use()
+
+        def down_tile(j):
+            at = tile_at(j, 256)
+            out = mid[:, at] + dot(act[...], gd[layer, :, at])
+            hid[:, at] = out
+            if layer == layers - 1:
+                result[:, at] = out.astype(BF16)
+
+        loop(width // 256, down_tile)
+        saved[7].start()
+
+    for c in weight_saves():
+        c.start()
+    for c in saves(layers - 1):
+        c.wait()
+    for layer in range(layers - 1):
+        saves(layer)[2].wait()
+    for c in weight_saves():
+        c.wait()
+    for t in tensors:
+        t.drain()
+    for i in range(3):
+        params(i).wait_send()
+        for layer in range(layers):
+            @pl.when(gives[i])
+            def _():
+                share_kv(layer, i).wait_send()
+
+
+def forward(tokens, prm, cosr, sinr, bias_c, bias_n, w_qkv, w_out, w_up, w_down):
+    rows, width = tokens.shape
+    share = rows // 2
+    layers = w_qkv.shape[0]
+    seq = share * 4
+    qw, ff = w_qkv.shape[2], w_up.shape[2]
+    full = [
+        jax.ShapeDtypeStruct((layers, width, qw), BF16),
+        jax.ShapeDtypeStruct((layers, width, width), BF16),
+        jax.ShapeDtypeStruct((layers, width, ff), BF16),
+        jax.ShapeDtypeStruct((layers, ff, width), BF16),
+    ]
+    hbm = pl.BlockSpec(memory_space=pltpu.HBM)
+    vmem = pl.BlockSpec(memory_space=pltpu.VMEM)
+    shape = jax.ShapeDtypeStruct
+    kept = [
+        shape((layers, rows, width), F32),
+        shape((layers, rows, width), BF16),
+        shape((layers, share, 2 * width), BF16),
+        shape((layers, seq, 2 * width), BF16),
+        shape((layers, rows, 128), F32),
+        shape((layers, rows, width), BF16),
+        shape((layers, rows, width), F32),
+        shape((layers, rows, ff), F32),
+    ]
+    dma, count = pltpu.SemaphoreType.DMA, 7 * 4 * layers
+    return pl.pallas_call(
+        partial(forward_kernel, layers),
+        out_shape=[shape((rows, width), BF16)] + full + [shape(prm.shape, F32)] + kept,
+        in_specs=[vmem] * 6 + [hbm] * 4,
+        out_specs=[vmem] + [hbm] * 4 + [vmem] + [hbm] * 8,
+        scratch_shapes=[pltpu.VMEM(f.shape, BF16) for f in full] + [
+            pltpu.VMEM((3,) + prm.shape, F32),
+            pltpu.VMEM(prm.shape, F32),
+            pltpu.VMEM((rows, width), F32),
+            pltpu.VMEM((rows, width), BF16),
+            pltpu.VMEM((rows, width), BF16),
+            pltpu.VMEM((share, 2 * width), BF16),
+            pltpu.VMEM((layers, seq, 2 * width), BF16),
+            pltpu.VMEM((rows, seq + share), F32),
+            pltpu.VMEM((rows, 128), F32),
+            pltpu.VMEM((rows, 128), F32),
+            pltpu.VMEM((rows, width), BF16),
+            pltpu.VMEM((rows, width), F32),
+            pltpu.VMEM((rows, ff), F32),
+            pltpu.VMEM((rows, ff), BF16),
+            dma((count,)), dma((count,)), dma((4 * layers,)),
+            dma((3,)), dma((3,)), dma((3 * layers,)), dma((3 * layers,)),
+            dma((8 * layers + 4 * layers,)),
+        ],
+        compiler_params=pltpu.CompilerParams(
+            collective_id=0, has_side_effects=True, vmem_limit_bytes=62 * 2**20),
+        cost_estimate=pl.CostEstimate(flops=20 * 10**9, bytes_accessed=10**8, transcendentals=10**7),
+        name="forward",
+    )(tokens, prm, cosr, sinr, bias_c, bias_n, w_qkv, w_out, w_up, w_down)
+
+
+def shared_params(norm_gains, norm_biases):
+    layers, _, part = norm_gains.shape
+    mine = jnp.concatenate([norm_gains.reshape(2 * layers, part), norm_biases.reshape(2 * layers, part)]).astype(F32)
+    parts = lax.axis_size("narrow")
+    owner = jnp.arange(parts) == lax.axis_index("narrow")
+    return jnp.where(owner[None, :, None], mine[:, None, :], 0.0).reshape(4 * layers, parts * part)
+
+
+def attend_tables(share, head_dim):
+    local = lax.axis_index("narrow") * share + jnp.arange(share, dtype=jnp.int32)
+    half = head_dim // 2
+    freq = jnp.exp(-jnp.log(10000.0) * jnp.arange(half, dtype=F32) * 2.0 / head_dim)
+    angle = local.astype(F32)[:, None] * freq[None, :]
+    cosine, sine = jnp.cos(angle), jnp.sin(angle)
+    cosr = jnp.tile(jnp.concatenate([cosine, cosine], axis=1), (2, 2))
+    sinr = jnp.tile(jnp.concatenate([-sine, sine], axis=1), (2, 2))
+    block = jnp.arange(share, dtype=jnp.int32) // BLOCK
+    same = block[:, None] == block[None, :]
+    below = block[None, :] < block[:, None]
+    bias = lambda allow: jnp.where(allow, 0.0, NEG).astype(F32)
+    return cosr, sinr, jnp.concatenate([bias(below), bias(below | same)]), bias(same)
 
 
 def norm_rows(hidden, gain, bias):
@@ -117,48 +576,6 @@
             * scale
         )
         return jnp.where(same_block[None, None, None], score, -jnp.inf)
-
-    def attend_forward(query, clean_k, clean_v, noisy_k, noisy_v):
-        local_score = noisy_scores(query[:, :share], noisy_k)
-        local_top = jnp.max(local_score, axis=-1)
-        local_total = jnp.sum(jnp.exp(local_score - local_top[..., None]), axis=-1)
-        top_start = jnp.concatenate(
-            [to_rows(local_top), jnp.full((rows, heads, share), -jnp.inf, jnp.float32)], axis=2
-        )
-        total_start = jnp.concatenate(
-            [to_rows(local_total), jnp.zeros((rows, heads, share), jnp.float32)], axis=2
-        )
-
-        def stat_step(group, carry):
-            top, total = carry
-            score = group_scores(query, clean_k, group)
-            group_top = safe_top(jnp.max(score, axis=-1))
-            group_total = jnp.sum(jnp.exp(score - group_top[..., None]), axis=-1)
-            joined = safe_top(jnp.maximum(top, group_top))
-            total = total * jnp.exp(top - joined) + group_total * jnp.exp(group_top - joined)
-            return (joined, total)
-
-        top, total = lax.fori_loop(0, stop, stat_step, (top_start, total_start))
-        logsum = top + jnp.log(total)
-        local_probs = jnp.exp(local_score - to_tiles(logsum[:, :, :share])).astype(jnp.bfloat16)
-        local_out = jnp.einsum(
-            "rthqk,rtkhd->rtqhd", local_probs, as_tiles(noisy_v), preferred_element_type=jnp.float32
-        ).reshape(rows, share, heads, head_dim)
-        out_start = jnp.concatenate(
-            [local_out, jnp.zeros((rows, share, heads, head_dim), jnp.float32)], axis=1
-        )
-
-        def out_step(group, attended):
-            probs = jnp.exp(group_scores(query, clean_k, group) - logsum[..., None]).astype(
-                jnp.bfloat16
-            )
-            values = lax.dynamic_slice_in_dim(clean_v, group * share, share, 1)
-            return attended + jnp.einsum(
-                "rhqk,rkhd->rqhd", probs, values, preferred_element_type=jnp.float32
-            )
-
-        attended = lax.fori_loop(0, stop, out_step, out_start)
-        return (attended, logsum)
 
     def attend_backward(query, clean_k, clean_v, noisy_k, noisy_v, grad_ctx, logsum):
         local_score = noisy_scores(query[:, :share], noisy_k)
@@ -251,66 +668,28 @@
         grad_query, clean_gk, clean_gv = lax.fori_loop(0, stop, grad_step, (dq_start, empty, empty))
         return (grad_query, clean_gk, clean_gv, noisy_gk, noisy_gv)
 
-    hidden = tokens.astype(jnp.float32).reshape(count, width)
+    prm = shared_params(norm_gains, norm_biases)
+    cosr, sinr, bias_c, bias_n = attend_tables(share, head_dim)
+    (result, fq, fo, fu, fd, prm, h_out, q_out, nkv_out, kv_out, lse_out, ctx_out, mid_out, u_out) = forward(
+        tokens.reshape(count, width), prm, cosr, sinr, bias_c, bias_n, w_qkv, w_out, w_up, w_down)
     saved = []
     for layer in range(layers):
-        full = (
-            lax.all_gather(w_qkv[layer], "narrow", axis=0, tiled=True),
-            lax.all_gather(w_out[layer], "narrow", axis=0, tiled=True),
-            lax.all_gather(w_up[layer], "narrow", axis=0, tiled=True),
-            lax.all_gather(w_down[layer], "narrow", axis=0, tiled=True),
-            lax.all_gather(norm_gains[layer], "narrow", axis=1, tiled=True),
-            lax.all_gather(norm_biases[layer], "narrow", axis=1, tiled=True),
-        )
-        qkv_w, out_w, up_w, down_w, gains, biases = full
-        normed_out, normed_one, inverse_one = norm_rows(
-            hidden, gains[0].astype(jnp.float32), biases[0].astype(jnp.float32)
-        )
-        first = normed_out.astype(jnp.bfloat16)
-        mixed = jnp.dot(first, qkv_w, preferred_element_type=jnp.float32).reshape(
-            rows, 2, share, 3, heads, head_dim
-        )
-        query = rotate(mixed[:, :, :, 0], cosine, sine).astype(jnp.bfloat16)
-        key = rotate(mixed[:, :, :, 1], cosine, sine).astype(jnp.bfloat16)
-        value = mixed[:, :, :, 2].astype(jnp.bfloat16)
-        clean_key, clean_value = (
-            lax.all_gather(key[:, 1], "narrow", axis=1, tiled=True),
-            lax.all_gather(value[:, 1], "narrow", axis=1, tiled=True),
-        )
-        head_items = (
-            query.reshape(rows, 2 * share, heads, head_dim),
-            clean_key,
-            clean_value,
-            key[:, 0],
-            value[:, 0],
-        )
-        attended, logsum = attend_forward(*head_items)
-        context = attended.reshape(count, width).astype(jnp.bfloat16)
-        middle = hidden + jnp.dot(context, out_w, preferred_element_type=jnp.float32)
-        normed_out, normed_two, inverse_two = norm_rows(
-            middle, gains[1].astype(jnp.float32), biases[1].astype(jnp.float32)
-        )
-        second = normed_out.astype(jnp.bfloat16)
-        upper = jnp.dot(second, up_w, preferred_element_type=jnp.float32)
-        active = jax.nn.gelu(upper, approximate=True).astype(jnp.bfloat16)
-        hidden = middle + jnp.dot(active, down_w, preferred_element_type=jnp.float32)
-        stash = None
-        saved.append(
-            (
-                stash,
-                normed_one,
-                inverse_one,
-                first,
-                head_items,
-                logsum,
-                context,
-                normed_two,
-                inverse_two,
-                second,
-                upper,
-                active,
-            )
-        )
+        h_in = tokens.astype(jnp.float32).reshape(count, width) if layer == 0 else h_out[layer - 1]
+        o, n1, i1 = norm_rows(h_in, prm[2 * layer], prm[2 * layers + 2 * layer])
+        f = o.astype(BF16)
+        o, n2, i2 = norm_rows(mid_out[layer], prm[2 * layer + 1], prm[2 * layers + 2 * layer + 1])
+        s = o.astype(BF16)
+        act = jax.nn.gelu(u_out[layer], approximate=True).astype(BF16)
+        mixed = jnp.dot(f, fq[layer], preferred_element_type=F32).reshape(rows, 2, share, 3, heads, head_dim)
+        query = rotate(mixed[:, :, :, 0], cosine, sine).astype(BF16)
+        key = rotate(mixed[:, :, :, 1], cosine, sine).astype(BF16)
+        value = mixed[:, :, :, 2].astype(BF16)
+        items = (query.reshape(rows, 2 * share, heads, head_dim),
+                 lax.all_gather(key[:, 1], "narrow", axis=1, tiled=True),
+                 lax.all_gather(value[:, 1], "narrow", axis=1, tiled=True), key[:, 0], value[:, 0])
+        ls = lse_out[layer][:, :heads].T[None]
+        saved.append((None, n1, i1, f, items, ls, ctx_out[layer], n2, i2, s, u_out[layer], act))
+    hidden = result
     result = hidden.reshape(tokens.shape).astype(jnp.bfloat16)
     valid = (local[None, :] < lengths[:, None]).astype(jnp.float32)
     grad = (cotangent.astype(jnp.float32) * valid[:, None, :, None]).reshape(count, width)
@@ -330,15 +709,8 @@
             upper,
             active,
         ) = saved[layer]
-        full = (
-            lax.all_gather(w_qkv[layer], "narrow", axis=0, tiled=True),
-            lax.all_gather(w_out[layer], "narrow", axis=0, tiled=True),
-            lax.all_gather(w_up[layer], "narrow", axis=0, tiled=True),
-            lax.all_gather(w_down[layer], "narrow", axis=0, tiled=True),
-            lax.all_gather(norm_gains[layer], "narrow", axis=1, tiled=True),
-            lax.all_gather(norm_biases[layer], "narrow", axis=1, tiled=True),
-        )
-        qkv_w, out_w, up_w, down_w, gains, biases = full
+        qkv_w, out_w, up_w, down_w = fq[layer], fo[layer], fu[layer], fd[layer]
+        gains = prm[2 * layer:2 * layer + 2]
         branch = grad.astype(jnp.bfloat16)
         grad_down = outer_sum(active, branch)
         grad_active = times_back(branch, down_w)

time: 1770 us -> 1530 us (0.86)
  waiting for transfers between devices: 1300 us -> 920 us
  Pallas kernels: 0 us -> 243 us
  matrix products: 187 us -> 138 us
  blocking collectives: 60 us -> 16.4 us
    all_gather x8 -> x0, waiting for transfers between devices: 315 us -> none  [the longest x2 111 us: on_device(): lax.all_gather(w_up[layer], 'narrow', axis=0, tiled=True)]
    pallas_call x0 -> x1, Pallas kernels: none -> 243 us  [forward(): pl.pallas_call(partial(forward_kernel, layers), out_shape=[shape((rows, w...]
    all_gather x2, waiting for transfers between devices: 73.3 us -> 0.04 us  [on_device(): lax.all_gather(value[:, 1], 'narrow', axis=1, tiled=True)]
    dot_general x12 -> x2, matrix products: 59.2 us -> 6.51 us  [on_device(): jnp.dot(f, fq[layer], preferred_element_type=F32)]
    all_gather x4 -> x0, blocking collectives: 43.6 us -> none  [the longest x2 23 us: on_device(): lax.all_gather(norm_biases[layer], 'narrow', axis=1, tiled=True)]
    all_gather x2, waiting for transfers between devices: 19.8 us -> 47.1 us  [on_device(): lax.all_gather(key[:, 1], 'narrow', axis=1, tiled=True)]
    reduce_scatter x2, waiting for transfers between devices: 90.5 us -> 68.7 us  [on_device(): lax.psum_scatter(clean_v_grad.astype(jnp.bfloat16), 'narrow', scatter_dim...]
    unnamed x33 -> x25, waiting for transfers between devices: 92.6 us -> 101 us
  transfers between devices with their start and end apart: 29 -> 21, of which waited for: 28 -> 19; matrix products, arithmetic and copies ran while one was open for 13% -> 14% of each run, Pallas kernels for 0% -> 0%
where the time goes in v1:
time: 1530 us; the launch traced here: 1520 us
  waiting for transfers between devices  920 us (60%)
  Pallas kernels  243 us (16%)
  matrix products  138 us (9%)
  local copies, waits for them, and re-layouts  109 us (7%)
  other arithmetic  71.1 us (5%)
  between operations  17.4 us (1%)
  blocking collectives  16.4 us (1%)
    psum x1, waiting for transfers between devices, on_device(): lax.psum((shards[0], shards[1], shards[2], shards[3], shards[4], shards[5...  271 us
    pallas_call x1, Pallas kernels, forward(): pl.pallas_call(partial(forward_kernel, layers), out_shape=[shape((rows, w...  243 us
    reduce_scatter x2, waiting for transfers between devices, on_device(): lax.psum_scatter(grad_down.astype(jnp.bfloat16), 'narrow', scatter_dimens...  114 us
    reduce_scatter x2, waiting for transfers between devices, on_device(): lax.psum_scatter(grad_up.astype(jnp.bfloat16), 'narrow', scatter_dimensio...  109 us
    unnamed x25, waiting for transfers between devices  101 us
    reduce_scatter x2, waiting for transfers between devices, on_device(): lax.psum_scatter(grad_qkv.astype(jnp.bfloat16), 'narrow', scatter_dimensi...  95.4 us
    reduce_scatter x2, waiting for transfers between devices, on_device(): lax.psum_scatter(clean_v_grad.astype(jnp.bfloat16), 'narrow', scatter_dim...  68.7 us
    reduce_scatter x2, waiting for transfers between devices, on_device(): lax.psum_scatter(clean_k_grad.astype(jnp.bfloat16), 'narrow', scatter_dim...  66.2 us
  transfers between devices with their start and end apart: 21, of which 19 were waited for; matrix products, arithmetic and copies ran while one was open for 14% of the time, Pallas kernels for 0%

profile of v1, /device:TPU:0, one launch (start us, length us, event | category | flops | bytes accessed | tf_op | source)
XLA Modules:
  0.0 1517.8 jit_solution(1857596160403029954)
XLA Ops:
  14.4 243.4 %forward.1 = (bf16[512,768]{1,0:T(8,128)(2,1)}, bf16[2,768,2304]{2,1,0:T(8,128)(2,1)}, bf16[2,768,768]{2,1,0:T(8,128)(2,1)}, bf16[2,768,3072]{2,1,0:T(8,128)(2,1...) custom-call(bf16[512,768]{1,0:T(8,128)(2,1)} %bitcast.690, ...), custom_call_target="tpu_custom_call" | custom-call | flops 20000000000 | bytes 100000000 | tf_op jit(solution)/shard_map/forward/pallas_call | solution.py:417
  261.8 5.3 slice_bitcast_fusion
  267.1 5.9 copy.124
  274.8 4.4 convolution_bitcast_fusion.1
  284.5 3.6 copy.152
  299.2 2.5 fusion.192
  309.6 9.1 fusion.106
  318.8 3.5 multiply_reduce_fusion
  331.5 15.9 %all-gather.11.cloned.1.call-done = bf16[1,1,1024,12,64]{2,4,3,1,0:T(8,128)(2,1)} async-done(((bf16[1,1,256,12,64]{2,4,3,1,0:T(8,128)(2,1)}), bf16[1,1,1024,12,64]{2,4,3,1,0:T(8,128)(2,1)}) %all-gather.11.cloned.1.call-update) | async-done | bytes 1572880 | tf_op jit(solution)/shard_map/all_gather | solution.py:688
  347.4 5.8 while.60
  349.8 3.0 fusion.309
  359.5 10.9 while.61
  363.6 3.7 fusion.321
  374.9 2.8 fusion.167
  396.9 2.8 subtract_exponential_fusion
  405.8 3.4 fusion.234
  409.1 41.3 %reduce-scatter.27.cloned.1.call-done = bf16[1,256,12,64]{1,3,2,0:T(8,128)(2,1)} async-done(((bf16[1,1024,12,64]{1,3,2,0:T(8,128)(2,1)}), bf16[1,256,12,64]{1,3,2,0:T(8,128)(2,1)}) %reduce-scatter.27.cloned.1.call-update) | async-done | bytes 393232 | tf_op jit(solution)/shard_map/reduce_scatter | solution.py:736
  451.5 33.3 %reduce-scatter.25.cloned.1.call-done = bf16[1,256,12,64]{1,3,2,0:T(8,128)(2,1)} async-done(((bf16[1,1024,12,64]{1,3,2,0:T(8,128)(2,1)}), bf16[1,256,12,64]{1,3,2,0:T(8,128)(2,1)}) %reduce-scatter.25.cloned.1.call-update) | async-done | bytes 393232 | tf_op jit(solution)/shard_map/reduce_scatter | solution.py:733
  488.3 2.5 copy.151
  493.6 3.2 multiply_reduce_fusion.1
  497.5 8.6 fusion.113
  506.2 3.6 multiply_reduce_fusion.2
  518.7 31.2 %all-gather.15.cloned.1.call-done = bf16[1,1,1024,12,64]{2,4,3,1,0:T(8,128)(2,1)} async-done(((bf16[1,1,256,12,64]{2,4,3,1,0:T(8,128)(2,1)}), bf16[1,1,1024,12,64]{2,4,3,1,0:T(8,128)(2,1)}) %all-gather.15.cloned.1.call-update) | async-done | bytes 1572880 | tf_op jit(solution)/shard_map/all_gather | solution.py:688
  550.0 5.6 while.62
  552.2 3.3 fusion.329
  561.9 12.7 while.63
  564.7 2.7 fusion.343
  567.4 4.1 fusion.341
  575.4 3.5 convolution_convert_fusion.6
  579.0 3.5 convolution_convert_fusion.7
  582.6 7.4 convolution_convert_fusion.2
  591.2 8.2 convolution_convert_fusion
  600.5 5.5 convolution_convert_fusion.4
  606.7 7.4 convolution_convert_fusion.3
  614.2 8.8 convolution_convert_fusion.1
  632.1 27.4 %reduce-scatter.31.cloned.1.call-done = bf16[1,256,12,64]{1,3,2,0:T(8,128)(2,1)} async-done(((bf16[1,1024,12,64]{1,3,2,0:T(8,128)(2,1)}), bf16[1,256,12,64]{1,3,2,0:T(8,128)(2,1)}) %reduce-scatter.31.cloned.1.call-update) | async-done | bytes 393232 | tf_op jit(solution)/shard_map/reduce_scatter | solution.py:736
  660.5 32.9 %reduce-scatter.29.cloned.1.call-done = bf16[1,256,12,64]{1,3,2,0:T(8,128)(2,1)} async-done(((bf16[1,1024,12,64]{1,3,2,0:T(8,128)(2,1)}), bf16[1,256,12,64]{1,3,2,0:T(8,128)(2,1)}) %reduce-scatter.29.cloned.1.call-update) | async-done | bytes 393232 | tf_op jit(solution)/shard_map/reduce_scatter | solution.py:733
  696.1 2.5 copy.179
  700.4 3.8 convolution_convert_fusion.5
  705.0 20.5 %reduce-scatter.39.cloned.1.call-done = bf16[192,768]{1,0:T(8,128)(2,1)} async-done(((bf16[768,768]{1,0:T(8,128)(2,1)}), bf16[192,768]{1,0:T(8,128)(2,1)}) %reduce-scatter.39.cloned.1.call-update) | async-done | bytes 294928 | tf_op jit(solution)/shard_map/reduce_scatter | solution.py:762
  729.5 27.3 %reduce-scatter.37.cloned.1.call-done = bf16[192,768]{1,0:T(8,128)(2,1)} async-done(((bf16[768,768]{1,0:T(8,128)(2,1)}), bf16[192,768]{1,0:T(8,128)(2,1)}) %reduce-scatter.37.cloned.1.call-update) | async-done | bytes 294928 | tf_op jit(solution)/shard_map/reduce_scatter | solution.py:762
  758.6 6.2 multiply_reduce_fusion.3
  766.8 50.7 %reduce-scatter.43.cloned.1.call-done = bf16[192,3072]{1,0:T(8,128)(2,1)} async-done(((bf16[768,3072]{1,0:T(8,128)(2,1)}), bf16[192,3072]{1,0:T(8,128)(2,1)}) %reduce-scatter.43.cloned.1.call-update) | async-done | bytes 1179664 | tf_op jit(solution)/shard_map/reduce_scatter | solution.py:765
  817.5 2.9 bitcast_convert_fusion.2
  820.4 57.0 %reduce-scatter.47.cloned.1.call-done = bf16[768,768]{1,0:T(8,128)(2,1)} async-done(((bf16[3072,768]{1,0:T(8,128)(2,1)}), bf16[768,768]{1,0:T(8,128)(2,1)}) %reduce-scatter.47.cloned.1.call-update) | async-done | bytes 1179664 | tf_op jit(solution)/shard_map/reduce_scatter | solution.py:768
  877.5 2.9 bitcast_convert_fusion
  880.4 48.0 %reduce-scatter.35.cloned.1.call-done = bf16[192,2304]{1,0:T(8,128)(2,1)} async-done(((bf16[768,2304]{1,0:T(8,128)(2,1)}), bf16[192,2304]{1,0:T(8,128)(2,1)}) %reduce-scatter.35.cloned.1.call-update) | async-done | bytes 884752 | tf_op jit(solution)/shard_map/reduce_scatter | solution.py:759
  928.4 2.5 bitcast_convert_fusion.4
  930.9 58.0 %reduce-scatter.41.cloned.1.call-done = bf16[192,3072]{1,0:T(8,128)(2,1)} async-done(((bf16[768,3072]{1,0:T(8,128)(2,1)}), bf16[192,3072]{1,0:T(8,128)(2,1)}) %reduce-scatter.41.cloned.1.call-update) | async-done | bytes 1179664 | tf_op jit(solution)/shard_map/reduce_scatter | solution.py:765
  988.9 2.9 bitcast_convert_fusion.3
  991.9 57.0 %reduce-scatter.45.cloned.1.call-done = bf16[768,768]{1,0:T(8,128)(2,1)} async-done(((bf16[3072,768]{1,0:T(8,128)(2,1)}), bf16[768,768]{1,0:T(8,128)(2,1)}) %reduce-scatter.45.cloned.1.call-update) | async-done | bytes 1179664 | tf_op jit(solution)/shard_map/reduce_scatter | solution.py:768
  1048.9 2.8 bitcast_convert_fusion.1
  1051.7 47.4 %reduce-scatter.33.cloned.1.call-done = bf16[192,2304]{1,0:T(8,128)(2,1)} async-done(((bf16[768,2304]{1,0:T(8,128)(2,1)}), bf16[192,2304]{1,0:T(8,128)(2,1)}) %reduce-scatter.33.cloned.1.call-update) | async-done | bytes 884752 | tf_op jit(solution)/shard_map/reduce_scatter | solution.py:759
  1099.1 2.5 bitcast_convert_fusion.5
  1101.7 24.1 %reduce-scatter.55.cloned.1.call-done = bf16[192,2]{1,0:T(8,128)(2,1)} async-done(((bf16[768,2]{1,0:T(8,128)(2,1)}), bf16[192,2]{1,0:T(8,128)(2,1)}) %reduce-scatter.55.cloned.1.call-update) | async-done | bytes 784
  1126.6 26.3 %reduce-scatter.51.cloned.1.call-done = bf16[192,2]{1,0:T(8,128)(2,1)} async-done(((bf16[768,2]{1,0:T(8,128)(2,1)}), bf16[192,2]{1,0:T(8,128)(2,1)}) %reduce-scatter.51.cloned.1.call-update) | async-done | bytes 784
  1153.9 2.8 add_convert_fusion.2
  1156.7 23.0 %reduce-scatter.53.cloned.1.call-done = bf16[192,2]{1,0:T(8,128)(2,1)} async-done(((bf16[768,2]{1,0:T(8,128)(2,1)}), bf16[192,2]{1,0:T(8,128)(2,1)}) %reduce-scatter.53.cloned.1.call-update) | async-done | bytes 784
  1180.6 25.7 %reduce-scatter.49.cloned.1.call-done = bf16[192,2]{1,0:T(8,128)(2,1)} async-done(((bf16[768,2]{1,0:T(8,128)(2,1)}), bf16[192,2]{1,0:T(8,128)(2,1)}) %reduce-scatter.49.cloned.1.call-update) | async-done | bytes 784
  1207.2 16.4 %all-reduce.4 = (f32[1,2,192]{2,1,0:T(2,128)S(1)}, f32[1,2,192]{2,1,0:T(2,128)S(1)}, f32[1,2,192]{2,1,0:T(2,128)S(1)}, f32[1,2,192]{2,1,0:T(2,128)S(1)}) all-reduce(f32[1,2,192]{2,1,0:T(2,128)S(1)} %bitcast_convert_fusion.12, f32[1,2,192]{2,1,0:T(2,128)S(1)} %bitcast_convert_fusion.13, ...), channel_id=1, replica_groups=mesh['narrow'=4,'wide'=8] {'wide'}, use_global_device_ids=true, to_apply=%region_55.56 | all-reduce | flops 1536 | bytes 12288 | tf_op jit(solution)/shard_map/psum | solution.py:784
  1225.4 271.4 %all-reduce.8.cloned.1.call-done = (f32[1,192,2304]{2,1,0:T(8,128)}, f32[1,192,2304]{2,1,0:T(8,128)}, f32[1,192,768]{2,1,0:T(8,128)}, f32[1,192,768]{2,1,0:T(8,1...) async-done(((f32[1,192,2304]{2,1,0:T(8,128)}, f32[1,192,2304]{2,1,0:T(8,128)}, ...) | async-done | bytes 14155792 | tf_op jit(solution)/shard_map/psum | solution.py:784
  1496.8 4.2 pad_maximum_fusion.2
  1503.1 2.9 pad_maximum_fusion
  1507.2 2.5 pad_maximum_fusion.1
  (506 shorter events, 156.9 us)
Async XLA Ops:
  7.2 324.4 %all-gather.9.cloned.1.call-start = ((), (), s32[]{:S(2)}) async-start(), calls=%async_computation.28 | async-start | bytes 1966080 | tf_op jit(solution)/shard_map/all_gather | solution.py:689
  259.4 13.6 copy-start.73
  261.1 11.9 copy-start.82
  261.8 11.3 copy-start.71
  261.8 28.3 %copy-start.69 = (f32[768]{0:T(1024)}, f32[768]{0:T(1024)S(1)}, u32[]{:S(2)}) copy-start(f32[768]{0:T(1024)S(1)} %get-tuple-element.875) | copy-start | bytes 9220
  274.8 4.5 copy-start.61
  282.5 64.9 %all-gather.11.cloned.1.call-start = ((), (), s32[]{:S(2)}) async-start(), calls=%async_computation.29 | async-start | bytes 1966080 | tf_op jit(solution)/shard_map/all_gather | solution.py:688
  284.5 5.7 copy-start.84
  299.2 4.2 copy-start
  302.7 147.7 %reduce-scatter.27.cloned.1.call-start = ((), (), s32[]{:S(2)}) async-start(), calls=%async_computation.17 | async-start | bytes 1966080 | tf_op jit(solution)/shard_map/reduce_scatter | solution.py:736
  303.7 15.0 copy-start.89
  303.7 18.6 %copy-start.80 = (f32[512]{0:T(512)}, f32[512]{0:T(512)S(1)}, u32[]{:S(2)}) copy-start(f32[512]{0:T(512)S(1)} %broadcast_multiply_fusion.11) | copy-start | bytes 6148
  304.0 18.3 %copy-start.91 = (f32[512]{0:T(512)}, f32[512]{0:T(512)S(1)}, u32[]{:S(2)}) copy-start(f32[512]{0:T(512)S(1)} %add_rsqrt_fusion.3) | copy-start | bytes 6148
  308.0 10.7 slice-start.2
  309.5 9.2 copy-start.63
  309.5 9.2 copy-start.87
  309.5 9.2 slice-start.3
  309.6 9.2 slice-start.4
  329.8 24.1 %copy-start.7 = (f32[2,12,128,128]{2,3,1,0:T(8,128)}, f32[2,12,128,128]{2,3,1,0:T(8,128)S(1)}, u32[]{:S(2)}) copy-start(f32[2,12,128,128]{2,3,1,0:T(8,128)S(1)} %subtract_exponential_fusion.1) | copy-start | bytes 4718596
  329.8 17.6 %copy-start.68 = (pred[512]{0:T(512)(128)(4,1)S(1)}, pred[512]{0:T(512)(128)(4,1)}, u32[]{:S(2)}) copy-start(pred[512]{0:T(512)(128)(4,1)} %constant.301.clone.2) | copy-start | bytes 1540
  370.4 114.4 %reduce-scatter.25.cloned.1.call-start = ((), (), s32[]{:S(2)}) async-start(), calls=%async_computation.16 | async-start | bytes 1966080 | tf_op jit(solution)/shard_map/reduce_scatter | solution.py:733
  371.0 147.7 %all-gather.13.cloned.1.call-start = ((), (), s32[]{:S(2)}) async-start(), calls=%async_computation.30 | async-start | bytes 1966080 | tf_op jit(solution)/shard_map/all_gather | solution.py:689
  373.6 176.3 %all-gather.15.cloned.1.call-start = ((), (), s32[]{:S(2)}) async-start(), calls=%async_computation.31 | async-start | bytes 1966080 | tf_op jit(solution)/shard_map/all_gather | solution.py:688
  374.7 284.8 %reduce-scatter.31.cloned.1.call-start = ((), (), s32[]{:S(2)}) async-start(), calls=%async_computation.19 | async-start | bytes 1966080 | tf_op jit(solution)/shard_map/reduce_scatter | solution.py:736
  377.7 11.4 copy-start.41
  377.7 12.2 copy-start.33
  377.7 12.3 copy-start.32
  390.0 4.5 copy-start.38
  486.1 5.2 slice-start
  487.9 9.4 slice-start.8
  490.8 6.6 slice-start.9
  491.3 5.5 copy-start.23
  496.8 9.3 slice-start.5
  497.4 12.3 copy-start.18
  497.4 8.7 copy-start.1
  497.4 8.7 copy-start.86
  497.4 8.7 copy-start.90
  497.4 8.7 copy-start.93
  497.4 8.7 slice-start.6
  497.5 8.7 slice-start.7
  517.1 32.9 %copy-start.75 = (f32[12,512]{1,0:T(8,128)S(1)}, f32[12,512]{1,0:T(8,128)}, u32[]{:S(2)}) copy-start(f32[12,512]{1,0:T(8,128)} %copy.165) | copy-start | bytes 73732
  574.6 118.8 %reduce-scatter.29.cloned.1.call-start = ((), (), s32[]{:S(2)}) async-start(), calls=%async_computation.18 | async-start | bytes 1966080 | tf_op jit(solution)/shard_map/reduce_scatter | solution.py:733
  575.4 150.1 %reduce-scatter.39.cloned.1.call-start = ((), (), s32[]{:S(2)}) async-start(), calls=%async_computation.23 | async-start | bytes 1474560 | tf_op jit(solution)/shard_map/reduce_scatter | solution.py:762
  579.0 177.9 %reduce-scatter.37.cloned.1.call-start = ((), (), s32[]{:S(2)}) async-start(), calls=%async_computation.22 | async-start | bytes 1474560 | tf_op jit(solution)/shard_map/reduce_scatter | solution.py:762
  582.5 235.0 %reduce-scatter.43.cloned.1.call-start = ((), (), s32[]{:S(2)}) async-start(), calls=%async_computation.25 | async-start | bytes 5898240 | tf_op jit(solution)/shard_map/reduce_scatter | solution.py:765
  590.1 287.4 %reduce-scatter.47.cloned.1.call-start = ((), (), s32[]{:S(2)}) async-start(), calls=%async_computation.27 | async-start | bytes 5898240 | tf_op jit(solution)/shard_map/reduce_scatter | solution.py:768
  599.4 329.0 %reduce-scatter.35.cloned.1.call-start = ((), (), s32[]{:S(2)}) async-start(), calls=%async_computation.21 | async-start | bytes 4423680 | tf_op jit(solution)/shard_map/reduce_scatter | solution.py:759
  606.1 382.9 %reduce-scatter.41.cloned.1.call-start = ((), (), s32[]{:S(2)}) async-start(), calls=%async_computation.24 | async-start | bytes 5898240 | tf_op jit(solution)/shard_map/reduce_scatter | solution.py:765
  614.2 434.7 %reduce-scatter.45.cloned.1.call-start = ((), (), s32[]{:S(2)}) async-start(), calls=%async_computation.26 | async-start | bytes 5898240 | tf_op jit(solution)/shard_map/reduce_scatter | solution.py:768
  623.1 476.0 %reduce-scatter.33.cloned.1.call-start = ((), (), s32[]{:S(2)}) async-start(), calls=%async_computation.20 | async-start | bytes 4423680 | tf_op jit(solution)/shard_map/reduce_scatter | solution.py:759
  704.3 23.0 %copy-start.105 = (bf16[768]{0:T(1024)(128)(2,1)S(1)}, bf16[768]{0:T(1024)(128)(2,1)}, u32[]{:S(2)}) copy-start(bf16[768]{0:T(1024)(128)(2,1)} %get-tuple-element.855) | copy-start | bytes 4612
  704.3 23.0 %copy-start.104 = (bf16[768]{0:T(1024)(128)(2,1)S(1)}, bf16[768]{0:T(1024)(128)(2,1)}, u32[]{:S(2)}) copy-start(bf16[768]{0:T(1024)(128)(2,1)} %get-tuple-element.868) | copy-start | bytes 4612
  704.3 24.0 %copy-start.103 = (bf16[768]{0:T(1024)(128)(2,1)S(1)}, bf16[768]{0:T(1024)(128)(2,1)}, u32[]{:S(2)}) copy-start(bf16[768]{0:T(1024)(128)(2,1)} %get-tuple-element.853) | copy-start | bytes 4612
  704.3 24.0 %copy-start.102 = (bf16[768]{0:T(1024)(128)(2,1)S(1)}, bf16[768]{0:T(1024)(128)(2,1)}, u32[]{:S(2)}) copy-start(bf16[768]{0:T(1024)(128)(2,1)} %get-tuple-element.871) | copy-start | bytes 4612
  704.3 54.3 %copy-start.9 = (bf16[1,2,256,768]{3,2,1,0:T(8,128)(2,1)S(1)}, bf16[1,2,256,768]{3,2,1,0:T(8,128)(2,1)}, u32[]{:S(2)}) copy-start(bf16[1,2,256,768]{3,2,1,0:T(8,128)(2,1)} %param.17) | copy-start | bytes 2359300
  704.3 54.3 %copy-start.70 = (f32[768]{0:T(1024)S(1)}, f32[768]{0:T(1024)}, u32[]{:S(2)}) copy-start(f32[768]{0:T(1024)} %copy-done.69) | copy-start | bytes 9220
  704.4 421.4 %reduce-scatter.55.cloned.1.call-start = ((), (), s32[]{:S(2)}) async-start(), calls=%async_computation.35 | async-start | bytes 245760
  728.2 424.7 %reduce-scatter.51.cloned.1.call-start = ((), (), s32[]{:S(2)}) async-start(), calls=%async_computation.33 | async-start | bytes 245760
  729.2 450.5 %reduce-scatter.53.cloned.1.call-start = ((), (), s32[]{:S(2)}) async-start(), calls=%async_computation.34 | async-start | bytes 245760
  765.8 440.5 %reduce-scatter.49.cloned.1.call-start = ((), (), s32[]{:S(2)}) async-start(), calls=%async_computation.32 | async-start | bytes 245760
  766.7 730.1 %all-reduce.8.cloned.1.call-start = ((), (), s32[]{:S(2)}) async-start(), calls=%async_computation.36 | async-start | bytes 28311552 | tf_op jit(solution)/shard_map/psum | solution.py:784
  1101.6 52.2 %copy-start.5 = (f32[512,768]{1,0:T(8,128)S(1)}, f32[512,768]{1,0:T(8,128)}, u32[]{:S(2)}) copy-start(f32[512,768]{1,0:T(8,128)} %copy-done.4) | copy-start | bytes 4718596
  1496.8 4.2 copy-start.66
  1496.8 5.3 copy-start.28
  (78 other events, 176.9 us)
Sparse Core Ops, SparseCore 0:
  282.6 32.0 all-gather.8
  316.6 30.8 all-gather.10
  370.6 79.8 reduce-scatter.26
  453.9 30.9 reduce-scatter.24
  486.5 30.8 all-gather.12
  519.1 30.8 all-gather.14
  574.7 84.6 reduce-scatter.30
  662.5 30.8 reduce-scatter.28
  696.9 28.5 reduce-scatter.38
  728.2 28.5 reduce-scatter.36
  760.4 57.0 reduce-scatter.42
  820.3 57.0 reduce-scatter.46
  881.1 47.2 reduce-scatter.34
  931.8 57.0 reduce-scatter.40
  991.8 57.0 reduce-scatter.44
  1051.8 47.2 reduce-scatter.32
  1101.7 23.9 reduce-scatter.54
  1128.9 23.9 reduce-scatter.50
  1155.7 23.9 reduce-scatter.52
  1182.3 23.9 reduce-scatter.48
  1209.9 286.9 all-reduce.7

commit v2 on v1

v2 whole, which is shorter than its diff:
```python
from functools import partial

import jax
import jax.numpy as jnp
from jax import lax
from jax.experimental import pallas as pl
from jax.experimental.pallas import tpu as pltpu
from jax.sharding import PartitionSpec as P

H = 12
BLOCK = 16
NEG = -1e30
EPS = 1e-05
MESH = pl.DeviceIdType.MESH
F32 = jnp.float32
BF16 = jnp.bfloat16
GELU_C = 0.7978845608028654
GELU_A = 0.044715


def dot(a, b):
    return jnp.dot(a, b, preferred_element_type=F32)


def dot_nt(a, b):
    return lax.dot_general(a, b, (((1,), (1,)), ((), ())), preferred_element_type=F32)


def dot_tn(a, b):
    return lax.dot_general(a, b, (((0,), (0,)), ((), ())), preferred_element_type=F32)


def tile_at(index, size):
    return pl.ds(pl.multiple_of(index * size, size), size)


def loop(count, body):
    lax.fori_loop(0, count, lambda i, _: (body(i), None)[1], None)


def swap_halves(x, first):
    return jnp.where(first, pltpu.roll(x, 96, 1), pltpu.roll(x, 32, 1))


def lane_masks(rows):
    lane = lax.broadcasted_iota(jnp.int32, (rows, 128), 1)
    return lane % 64 < 32


def head_masks():
    lane = lax.broadcasted_iota(jnp.int32, (1, 128), 1)
    low = (lane < 64).astype(F32)
    return low, 1.0 - low


def norm_into(src, dst, gain, bias, rows):
    step = 32

    def body(i):
        at = tile_at(i, step)
        x = src[at, :].astype(F32)
        c = x - jnp.mean(x, axis=-1, keepdims=True)
        inv = lax.rsqrt(jnp.mean(c * c, axis=-1, keepdims=True) + EPS)
        dst[at, :] = (c * inv * gain + bias).astype(BF16)

    loop(rows // step, body)


class Gather:
    def __init__(self, here, shard, full, send, recv, base, lsem):
        self.n, self.w = here
        self.core = lax.rem(self.w, 2)
        self.shard, self.full, self.send, self.recv, self.base, self.lsem = (
            shard, full, send, recv, base, lsem)
        self.rows = shard.shape[0]
        self.half = self.rows // 2
        self.quarter = self.rows // 4
        self.x, self.y, self.d, self.s = (
            (self.n ^ 1, self.w), (self.n ^ 2, self.w), (self.n ^ 3, self.w), (self.n, self.w ^ 1))

    def region(self, owner, core, quarter=None):
        start = owner * self.rows + core * self.half
        if quarter is None:
            return self.full.at[pl.ds(pl.multiple_of(start, 16), self.half)]
        return self.full.at[pl.ds(pl.multiple_of(start + quarter * self.quarter, 16), self.quarter)]

    def copy(self, slot, src, dst, device):
        k = self.base + slot
        return pltpu.make_async_remote_copy(
            src_ref=src, dst_ref=dst, send_sem=self.send.at[k], recv_sem=self.recv.at[k],
            device_id=device, device_id_type=MESH)

    def own(self):
        return pltpu.make_async_copy(
            self.shard, self.full.at[pl.ds(pl.multiple_of(self.n * self.rows, 16), self.rows)], self.lsem)

    def plain(self, slot, region, device):
        return self.copy(slot, region, region, device)

    def issue(self):
        src = self.shard.at[pl.ds(pl.multiple_of(self.core * self.half, 16), self.half)]
        dst = self.region(self.n, self.core)
        self.copy(0, src, dst, self.x).start()
        self.copy(1, src, dst, self.y).start()
        self.own().start()

    def forward(self):
        nx, ny = self.x[0], self.y[0]
        self.plain(0, self.region(nx, self.core), self.x).wait_recv()
        self.plain(2, self.region(nx, self.core, 0), self.y).start()
        self.plain(4, self.region(nx, self.core), self.s).start()
        self.plain(1, self.region(ny, self.core), self.y).wait_recv()
        self.plain(3, self.region(ny, self.core, 1), self.x).start()
        self.plain(5, self.region(ny, self.core), self.s).start()

    def finish(self):
        nd = self.d[0]
        self.plain(2, self.region(nd, self.core, 0), self.y).wait_recv()
        self.plain(3, self.region(nd, self.core, 1), self.x).wait_recv()
        self.plain(6, self.region(nd, self.core), self.s).start()

    def use(self):
        other = 1 - self.core
        for slot, who in ((4, self.x), (5, self.y), (6, self.d)):
            self.plain(slot, self.region(who[0], other), self.s).wait_recv()
        self.own().wait()

    def drain(self):
        src = self.shard.at[pl.ds(pl.multiple_of(self.core * self.half, 16), self.half)]
        dst = self.region(self.n, self.core)
        self.copy(0, src, dst, self.x).wait_send()
        self.copy(1, src, dst, self.y).wait_send()
        nx, ny, nd = self.x[0], self.y[0], self.d[0]
        self.plain(2, self.region(nx, self.core, 0), self.y).wait_send()
        self.plain(3, self.region(ny, self.core, 1), self.x).wait_send()
        self.plain(4, self.region(nx, self.core), self.s).wait_send()
        self.plain(5, self.region(ny, self.core), self.s).wait_send()
        self.plain(6, self.region(nd, self.core), self.s).wait_send()


def forward_kernel(
    layers,
    tok, prm, cosr, sinr, bias_c, bias_n, wq, wo, wu, wd,
    result, fq, fo, fu, fd, prm_out, h_out, q_out, nkv_out, kv_out, lse_out, ctx_out, mid_out, act_out, dg_out,
    gq, go, gu, gd, prm_buf, par, hid, a, q, nkv, kv, score, top, lse, ctx, mid, dg, act,
    send, recv, lsem, psend, precv, ksend, krecv, ssem,
):
    n = lax.axis_index("narrow")
    w = lax.axis_index("wide")
    rows, width = tok.shape
    share = rows // 2
    group = share
    pairs = width // 128
    ff = wu.shape[2]
    peers = ((n ^ 1, w), (n ^ 2, w), (n ^ 3, w))

    barrier = pltpu.get_barrier_semaphore()
    for device in peers + ((n, w ^ 1),):
        pl.semaphore_signal(barrier, inc=1, device_id=device, device_id_type=MESH)
    pl.semaphore_wait(barrier, 4)

    tensors = []
    for layer in range(layers):
        for kind, (shard, full) in enumerate(((wq, gq), (wo, go), (wu, gu), (wd, gd))):
            k = layer * 4 + kind
            tensors.append(Gather((n, w), shard.at[layer], full.at[layer], send, recv, 7 * k, lsem.at[k]))

    def params(i):
        return pltpu.make_async_remote_copy(
            src_ref=prm, dst_ref=prm_buf.at[i], send_sem=psend.at[i], recv_sem=precv.at[i],
            device_id=peers[i], device_id_type=MESH)

    def share_kv(layer, i):
        region = kv.at[layer, tile_at(n, share)]
        return pltpu.make_async_remote_copy(
            src_ref=region, dst_ref=region, send_sem=ksend.at[3 * layer + i],
            recv_sem=krecv.at[3 * layer + i], device_id=peers[i], device_id_type=MESH)

    def recv_kv(layer, i):
        region = kv.at[layer, tile_at(peers[i][0], share)]
        return pltpu.make_async_remote_copy(
            src_ref=region, dst_ref=region, send_sem=ksend.at[3 * layer + i],
            recv_sem=krecv.at[3 * layer + i], device_id=peers[i], device_id_type=MESH)

    gives = (n % 2 == 0, n < 2, n < 2)
    takes = (n % 2 == 1, n >= 2, n >= 2)

    for i in range(3):
        params(i).start()
    tensors[0].issue()
    tensors[1].issue()

    def saves(layer):
        pieces = [
            (q, q_out.at[layer]), (nkv, nkv_out.at[layer]), (kv.at[layer], kv_out.at[layer]),
            (lse, lse_out.at[layer]), (ctx, ctx_out.at[layer]), (mid, mid_out.at[layer]), (act, act_out.at[layer]),
            (dg, dg_out.at[layer]), (hid, h_out.at[layer]),
        ]
        return [pltpu.make_async_copy(s, d, ssem.at[layer * 9 + k]) for k, (s, d) in enumerate(pieces)]

    def weight_saves():
        pieces = ((gq, fq), (go, fo), (gu, fu), (gd, fd))
        out = []
        for layer in range(layers):
            for kind, (s, d) in enumerate(pieces):
                k = layer * 4 + kind
                out.append(pltpu.make_async_copy(s.at[layer], d.at[layer], ssem.at[9 * layers + k]))
        return out

    for i in range(3):
        params(i).wait_recv()
    par[...] = prm[...] + prm_buf[0] + prm_buf[1] + prm_buf[2]
    prm_out[...] = par[...]

    first = lane_masks(rows)
    masks = head_masks()
    lanes = lax.broadcasted_iota(jnp.int32, (rows, 128), 1)

    for layer in range(layers):
        t_qkv, t_out, t_up, t_down = tensors[4 * layer:4 * layer + 4]
        later = tensors[4 * layer + 4:]
        gain1, gain2 = par[2 * layer:2 * layer + 1, :], par[2 * layer + 1:2 * layer + 2, :]
        at = 2 * layers + 2 * layer
        bias1, bias2 = par[at:at + 1, :], par[at + 1:at + 2, :]
        saved = saves(layer)
        before = saves(layer - 1) if layer else None
        if layer == 0:
            norm_into(tok, a, gain1, bias1, rows)
        else:
            norm_into(hid, a, gain1, bias1, rows)
        if layer == 0:
            t_qkv.forward()
        t_qkv.finish()
        t_qkv.use()
        if before:
            before[0].wait()
            before[1].wait()

        wqkv = gq.at[layer]

        def query_tile(j):
            x = dot(a[...], wqkv[:, tile_at(j, 256)])
            for part in range(2):
                v = x[:, 128 * part:128 * part + 128]
                v = v * cosr[...] + swap_halves(v, first) * sinr[...]
                q[:, tile_at(2 * j + part, 128)] = (v.astype(BF16).astype(F32) * 0.125).astype(BF16)

        def key_tile(j):
            x = dot(a[...], wqkv[:, tile_at(j + 3, 256)])
            for part in range(2):
                v = x[:, 128 * part:128 * part + 128]
                v = (v * cosr[...] + swap_halves(v, first) * sinr[...]).astype(BF16)
                nkv[:, tile_at(2 * j + part, 128)] = v[:share]
                kv[layer, tile_at(n, share), tile_at(2 * j + part, 128)] = v[share:]

        def value_tile(j):
            v = dot(a[...], wqkv[:, tile_at(j + 6, 256)]).astype(BF16)
            nkv[:, tile_at(j + 3, 256)] = v[:share]
            kv[layer, tile_at(n, share), tile_at(j + 3, 256)] = v[share:]

        loop(3, key_tile)
        loop(3, value_tile)
        for i in range(3):
            @pl.when(gives[i])
            def _():
                share_kv(layer, i).start()
        loop(3, query_tile)
        saved[0].start()
        saved[1].start()
        t_out.forward()
        t_up.issue()
        t_down.issue()
        for i in range(3):
            @pl.when(takes[i])
            def _():
                recv_kv(layer, i).wait_recv()
        saved[2].start()
        if before:
            before[3].wait()
            before[4].wait()

        def pair_step(pair):
            at_pair = tile_at(pair, 128)
            at_value = tile_at(pair + pairs, 128)
            q2 = q[:, at_pair].astype(F32)
            outs = []
            for h in range(2):
                qm = (q2 * masks[h]).astype(BF16)
                s = dot_nt(qm, kv[layer, tile_at(n, group), at_pair]) + bias_c[...]
                score[:, tile_at(n, group)] = s
                top[...] = jnp.maximum(s[:, :128], s[:, 128:])
                s = dot_nt(qm[:share], nkv[:, at_pair]) + bias_n[...]
                score[:share, 4 * group:5 * group] = s
                top[:share] = jnp.maximum(top[:share], jnp.maximum(s[:, :128], s[:, 128:]))

                def scores_of(g):
                    s = dot_nt(qm, kv[layer, tile_at(g, group), at_pair])
                    score[:, tile_at(g, group)] = s
                    top[...] = jnp.maximum(top[...], jnp.maximum(s[:, :128], s[:, 128:]))

                loop(n, scores_of)
                most = jnp.max(top[...], axis=-1, keepdims=True)
                p = jnp.exp(score[:share, 4 * group:5 * group] - most[:share])
                part = p[:, :128] + p[:, 128:]
                add = dot(p.astype(BF16), nkv[:, at_value])
                zeros = jnp.zeros((share, 128), F32)

                def probs_of(g, carry):
                    total, out = carry
                    p = jnp.exp(score[:, tile_at(g, group)] - most)
                    total = total + p[:, :128] + p[:, 128:]
                    out = out + dot(p.astype(BF16), kv[layer, tile_at(g, group), at_value])
                    return total, out

                total, out = lax.fori_loop(
                    0, n + 1, probs_of,
                    (jnp.concatenate([part, zeros], axis=0), jnp.concatenate([add, zeros], axis=0)))
                total = jnp.sum(total, axis=-1, keepdims=True)
                outs.append(out * (masks[h] / total))
                lse[...] = jnp.where(lanes == 2 * pair + h, most + jnp.log(total), lse[...])
            ctx[:, at_pair] = (outs[0] + outs[1]).astype(BF16)

        loop(pairs, pair_step)
        saved[3].start()
        saved[4].start()
        t_out.finish()
        t_out.use()
        t_up.forward()
        if later:
            later[0].issue()
            later[1].issue()
        if before:
            before[5].wait()
            before[6].wait()
            before[7].wait()
            before[8].wait()

        def out_tile(j):
            at = tile_at(j, 256)
            base = (tok if layer == 0 else hid)[:, at].astype(F32)
            mid[:, at] = base + dot(ctx[...], go[layer, :, at])

        loop(width // 256, out_tile)
        saved[5].start()
        norm_into(mid, a, gain2, bias2, rows)
        t_up.finish()
        t_up.use()

        def up_tile(j):
            at = tile_at(j, 256)
            x = dot(a[...], gu[layer, :, at])
            x2 = x * x
            t = jnp.tanh(GELU_C * (x + GELU_A * (x * x2)))
            cdf = 0.5 + 0.5 * t
            act[:, at] = (x * cdf).astype(BF16)
            slope = GELU_C * (1.0 + 3.0 * GELU_A * x2)
            dg[:, at] = (cdf + 0.5 * x * (1.0 - t * t) * slope).astype(BF16)

        loop(ff // 256, up_tile)
        saved[6].start()
        saved[7].start()
        t_down.forward()
        if later:
            later[0].forward()
        t_down.finish()
        t_down.use()

        def down_tile(j):
            at = tile_at(j, 256)
            out = mid[:, at] + dot(act[...], gd[layer, :, at])
            hid[:, at] = out
            if layer == layers - 1:
                result[:, at] = out.astype(BF16)

        loop(width // 256, down_tile)
        saved[8].start()

    for c in weight_saves():
        c.start()
    for c in saves(layers - 1):
        c.wait()
    for layer in range(layers - 1):
        saves(layer)[2].wait()
    for c in weight_saves():
        c.wait()
    for t in tensors:
        t.drain()
    for i in range(3):
        params(i).wait_send()
        for layer in range(layers):
            @pl.when(gives[i])
            def _():
                share_kv(layer, i).wait_send()


def forward(tokens, prm, cosr, sinr, bias_c, bias_n, w_qkv, w_out, w_up, w_down):
    rows, width = tokens.shape
    share = rows // 2
    layers = w_qkv.shape[0]
    seq = share * 4
    qw, ff = w_qkv.shape[2], w_up.shape[2]
    full = [
        jax.ShapeDtypeStruct((layers, width, qw), BF16),
        jax.ShapeDtypeStruct((layers, width, width), BF16),
        jax.ShapeDtypeStruct((layers, width, ff), BF16),
        jax.ShapeDtypeStruct((layers, ff, width), BF16),
    ]
    hbm = pl.BlockSpec(memory_space=pltpu.HBM)
    vmem = pl.BlockSpec(memory_space=pltpu.VMEM)
    shape = jax.ShapeDtypeStruct
    kept = [
        shape((layers, rows, width), F32),
        shape((layers, rows, width), BF16),
        shape((layers, share, 2 * width), BF16),
        shape((layers, seq, 2 * width), BF16),
        shape((layers, rows, 128), F32),
        shape((layers, rows, width), BF16),
        shape((layers, rows, width), F32),
        shape((layers, rows, ff), BF16),
        shape((layers, rows, ff), BF16),
    ]
    dma, count = pltpu.SemaphoreType.DMA, 7 * 4 * layers
    return pl.pallas_call(
        partial(forward_kernel, layers),
        out_shape=[shape((rows, width), BF16)] + full + [shape(prm.shape, F32)] + kept,
        in_specs=[vmem] * 6 + [hbm] * 4,
        out_specs=[vmem] + [hbm] * 4 + [vmem] + [hbm] * 9,
        scratch_shapes=[pltpu.VMEM(f.shape, BF16) for f in full] + [
            pltpu.VMEM((3,) + prm.shape, F32),
            pltpu.VMEM(prm.shape, F32),
            pltpu.VMEM((rows, width), F32),
            pltpu.VMEM((rows, width), BF16),
            pltpu.VMEM((rows, width), BF16),
            pltpu.VMEM((share, 2 * width), BF16),
            pltpu.VMEM((layers, seq, 2 * width), BF16),
            pltpu.VMEM((rows, seq + share), F32),
            pltpu.VMEM((rows, 128), F32),
            pltpu.VMEM((rows, 128), F32),
            pltpu.VMEM((rows, width), BF16),
            pltpu.VMEM((rows, width), F32),
            pltpu.VMEM((rows, ff), BF16),
            pltpu.VMEM((rows, ff), BF16),
            dma((count,)), dma((count,)), dma((4 * layers,)),
            dma((3,)), dma((3,)), dma((3 * layers,)), dma((3 * layers,)),
            dma((9 * layers + 4 * layers,)),
        ],
        compiler_params=pltpu.CompilerParams(
            collective_id=0, has_side_effects=True, vmem_limit_bytes=62 * 2**20),
        cost_estimate=pl.CostEstimate(flops=20 * 10**9, bytes_accessed=10**8, transcendentals=10**7),
        name="forward",
    )(tokens, prm, cosr, sinr, bias_c, bias_n, w_qkv, w_out, w_up, w_down)


def add_rows(dst, at, left, left_at, right, right_at, rows):
    def body(i):
        step = lambda base: pl.ds(pl.multiple_of(base + 16 * i, 16), 16)
        dst[step(at), :] = left[step(left_at), :] + right[step(right_at), :]

    loop(rows // 16, body)


class Reduce:
    def __init__(self, here, turn, turns, grad, bufs, out, send, recv, base, credit, cbase, lsem):
        self.n, self.w = here
        self.turn, self.turns = turn, turns
        self.grad, self.out = grad, out
        self.s1, self.r2, self.r3, self.r4, self.r5, self.zb = bufs
        self.send, self.recv, self.base = send, recv, base
        self.credit, self.cbase, self.lsem = credit, cbase, lsem
        self.core = lax.rem(self.w, 2)
        self.rows = grad.shape[0] // 4
        self.half, self.quarter = self.rows // 2, self.rows // 4
        n, w = here
        self.x, self.y, self.d, self.s = (n ^ 1, w), (n ^ 2, w), (n ^ 3, w), (n, w ^ 1)
        chips = lax.axis_size("wide") // 2
        z = w // 2
        left = z < chips // 2
        step = jnp.where(left, 2, -2)
        self.inner, self.outer = (n, w + step), (n, w - step)
        self.has_outer = jnp.logical_and(z > 0, z < chips - 1)
        self.is_mid = jnp.logical_or(z == chips // 2 - 1, z == chips // 2)
        self.mine = jnp.where(left, 0, 1)

    def at(self, owner, core, quarter=0):
        return pl.multiple_of(owner * self.rows + core * self.half + quarter * self.quarter, 16)

    def part(self, ref, start, count):
        return ref.at[pl.ds(pl.multiple_of(start, 16), count)]

    def copy(self, slot, src, dst, device):
        k = self.base + slot
        return pltpu.make_async_remote_copy(
            src_ref=src, dst_ref=dst, send_sem=self.send.at[k], recv_sem=self.recv.at[k],
            device_id=device, device_id_type=MESH)

    def take(self, slot):
        if self.turn > 0:
            pl.semaphore_wait(self.credit.at[self.cbase + slot], 1)

    def give(self, slot, device):
        if self.turn < self.turns - 1:
            pl.semaphore_signal(
                self.credit.at[self.cbase + slot], inc=1, device_id=device, device_id_type=MESH)

    def to_sibling(self):
        out = []
        for m in range(4):
            src = self.part(self.grad, self.at(m, 1 - self.core), self.half)
            out.append(self.copy(m, src, self.part(self.s1, m * self.half, self.half), self.s))
        return out

    def first_hop(self):
        q, g, c = self.quarter, self.grad, self.core
        nx, ny, nd = self.x[0], self.y[0], self.d[0]
        plan = ((4, nx, 0, 0, self.x), (5, nd, 0, 1, self.x), (6, ny, 1, 2, self.y), (7, nd, 1, 3, self.y))
        return [
            self.copy(slot, self.part(g, self.at(owner, c, quarter), q), self.part(self.r2, place * q, q), device)
            for slot, owner, quarter, place, device in plan]

    def second_hop(self):
        q, g, c = self.quarter, self.grad, self.core
        return [
            self.copy(8, self.part(g, self.at(self.y[0], c, 0), q), self.part(self.r3, 0, q), self.y),
            self.copy(9, self.part(g, self.at(self.x[0], c, 1), q), self.part(self.r3, q, q), self.x)]

    def inward(self):
        return self.copy(10, self.zb, self.r4, self.inner)

    def across(self):
        src = self.part(self.zb, (1 - self.mine) * self.quarter, self.quarter)
        return self.copy(11, src, self.r5, self.inner)

    def done_at(self, core, quarter):
        start = core * self.half + quarter * self.quarter
        return self.part(self.out, start, self.quarter)

    def final(self, quarter, device, slot, from_zb):
        dst = self.done_at(self.core, quarter)
        src = self.part(self.zb, quarter * self.quarter, self.quarter) if from_zb else dst
        return self.copy(slot, src, dst, device)

    def keep(self):
        src = self.part(self.zb, self.mine * self.quarter, self.quarter)
        return pltpu.make_async_copy(src, self.done_at(self.core, self.mine), self.lsem)

    def p1(self):
        self.take(0)
        for c in self.to_sibling():
            c.start()

    def p2(self):
        g = self.grad
        for m, c in enumerate(self.to_sibling()):
            c.wait_recv()
            add_rows(g, self.at(m, self.core), g, self.at(m, self.core), self.s1, m * self.half, self.half)
        self.give(0, self.s)
        self.take(1)
        self.take(2)
        for c in self.first_hop():
            c.start()

    def p3(self):
        g, q = self.grad, self.quarter
        hops = self.first_hop()
        hops[1].wait_recv()
        at = self.at(self.y[0], self.core, 0)
        add_rows(g, at, g, at, self.r2, q, q)
        self.take(3)
        self.second_hop()[0].start()
        hops[3].wait_recv()
        at = self.at(self.x[0], self.core, 1)
        add_rows(g, at, g, at, self.r2, 3 * q, q)
        self.take(4)
        self.second_hop()[1].start()
        for k in range(2):
            hops[2 * k].wait_recv()
            at = self.at(self.n, self.core, k)
            add_rows(g, at, g, at, self.r2, 2 * k * q, q)
        self.give(1, self.x)
        self.give(2, self.y)

    def p4(self):
        g, q = self.grad, self.quarter
        for k, c in enumerate(self.second_hop()):
            c.wait_recv()
            add_rows(self.zb, k * q, g, self.at(self.n, self.core, k), self.r3, k * q, q)
        self.give(3, self.y)
        self.give(4, self.x)

        @pl.when(jnp.logical_not(jnp.logical_or(self.has_outer, self.is_mid)))
        def _():
            self.take(5)
            self.inward().start()

    def p5(self):
        @pl.when(self.has_outer)
        def _():
            self.inward().wait_recv()
            add_rows(self.zb, 0, self.zb, 0, self.r4, 0, self.half)
            self.give(5, self.outer)

        @pl.when(self.is_mid)
        def _():
            self.take(6)
            self.across().start()

        @pl.when(jnp.logical_and(self.has_outer, jnp.logical_not(self.is_mid)))
        def _():
            self.take(5)
            self.inward().start()

    def p6(self):
        @pl.when(self.is_mid)
        def _():
            self.across().wait_recv()
            at = self.mine * self.quarter
            add_rows(self.zb, at, self.zb, at, self.r5, 0, self.quarter)
            self.give(6, self.inner)
            self.keep().start()
            self.final(self.mine, self.inner, 12, True).start()
            self.final(self.mine, self.s, 13, True).start()

        @pl.when(jnp.logical_and(self.is_mid, self.has_outer))
        def _():
            self.final(self.mine, self.outer, 15, True).start()

    def p7(self):
        other = 1 - self.mine

        @pl.when(self.is_mid)
        def _():
            self.final(other, self.inner, 12, False).wait_recv()
            self.final(other, self.s, 14, False).start()

        @pl.when(jnp.logical_and(self.is_mid, self.has_outer))
        def _():
            self.final(other, self.outer, 16, False).start()

        @pl.when(jnp.logical_not(self.is_mid))
        def _():
            self.final(self.mine, self.inner, 15, False).wait_recv()
            self.final(self.mine, self.s, 13, False).start()
            self.final(other, self.inner, 16, False).wait_recv()
            self.final(other, self.s, 14, False).start()

        @pl.when(jnp.logical_and(jnp.logical_not(self.is_mid), self.has_outer))
        def _():
            self.final(self.mine, self.outer, 15, False).start()
            self.final(other, self.outer, 16, False).start()

    def p8(self):
        for k, quarter in ((13, self.mine), (14, 1 - self.mine)):
            region = self.done_at(1 - self.core, quarter)
            self.copy(k, region, region, self.s).wait_recv()

    def free_grad(self):
        for c in self.to_sibling() + self.first_hop() + self.second_hop():
            c.wait_send()

    def free_zb(self):
        @pl.when(jnp.logical_not(self.is_mid))
        def _():
            self.inward().wait_send()

        @pl.when(self.is_mid)
        def _():
            self.across().wait_send()
            self.final(self.mine, self.inner, 12, True).wait_send()
            self.keep().wait()

        other = 1 - self.mine
        self.final(self.mine, self.s, 13, False).wait_send()
        self.final(other, self.s, 14, False).wait_send()

        @pl.when(self.has_outer)
        def _():
            self.final(self.mine, self.outer, 15, False).wait_send()
            self.final(other, self.outer, 16, False).wait_send()


SLOTS = 17


class SmallSum:
    def __init__(self, here, acc, buf, send, recv):
        n, w = here
        self.acc, self.buf, self.send, self.recv = acc, buf, send, recv
        chips = lax.axis_size("wide") // 2
        z = w // 2
        left = z < chips // 2
        step = jnp.where(left, 2, -2)
        self.inner, self.outer = (n, w + step), (n, w - step)
        self.has_outer = jnp.logical_and(z > 0, z < chips - 1)
        self.is_mid = jnp.logical_or(z == chips // 2 - 1, z == chips // 2)
        self.others = ((n, w ^ 1), (n ^ 1, w), (n ^ 2, w))

    def copy(self, slot, device):
        return pltpu.make_async_remote_copy(
            src_ref=self.buf.at[0, slot], dst_ref=self.buf.at[1, slot], send_sem=self.send.at[slot],
            recv_sem=self.recv.at[slot], device_id=device, device_id_type=MESH)

    def begin(self):
        self.buf[0, 0] = self.acc[...]
        self.copy(0, self.others[0]).start()

    def swap(self, slot):
        self.copy(slot, self.others[slot]).wait_recv()
        self.buf[0, slot + 1] = self.buf[0, slot] + self.buf[1, slot]
        if slot < 2:
            self.copy(slot + 1, self.others[slot + 1]).start()

    def chain(self):
        @pl.when(self.has_outer)
        def _():
            self.copy(3, self.outer).wait_recv()
            self.buf[0, 3] = self.buf[0, 3] + self.buf[1, 3]

        @pl.when(jnp.logical_not(self.is_mid))
        def _():
            self.copy(3, self.inner).start()

        @pl.when(self.is_mid)
        def _():
            self.buf[0, 4] = self.buf[0, 3]
            self.copy(4, self.inner).start()

    def settle(self):
        @pl.when(self.is_mid)
        def _():
            self.copy(4, self.inner).wait_recv()
            self.buf[0, 5] = self.buf[0, 4] + self.buf[1, 4]

        @pl.when(jnp.logical_not(self.is_mid))
        def _():
            self.copy(5, self.inner).wait_recv()
            self.buf[0, 5] = self.buf[1, 5]

        @pl.when(self.has_outer)
        def _():
            self.copy(5, self.outer).start()

    def finish(self, out):
        out[...] = self.buf[0, 5]
        for k in range(3):
            self.copy(k, self.others[k]).wait_send()

        @pl.when(jnp.logical_not(self.is_mid))
        def _():
            self.copy(3, self.inner).wait_send()

        @pl.when(self.is_mid)
        def _():
            self.copy(4, self.inner).wait_send()

        @pl.when(self.has_outer)
        def _():
            self.copy(5, self.outer).wait_send()


TILE = 512


def backward_kernel(
    layers,
    lens, cot, tok, par, cosr, sinr, bias_c, bias_n,
    fq, fo, fu, fd, h_in, q_in, nkv_in, kv_in, lse_in, ctx_in, mid_in, act_in, dg_in,
    grad_tok, oq, oo, ou, od, small,
    gq, go, gu, gd, *rest,
):
    bufs, rest = [rest[6 * k:6 * k + 6] for k in range(4)], rest[24:]
    (wd_s, wu_s, act_s, dg_s, wo, wq, dh, mid, da, at_, db, q, kv, nkv, ctx, dctx, lse, lset, delta, dqkv, xfer,
     gacc, sbuf, send, recv, credit, lsem, ksend, krecv, kcredit, stsem, ldsem, ssend, srecv) = rest
    n = lax.axis_index("narrow")
    w = lax.axis_index("wide")
    here = (n, w)
    rows, width = cot.shape
    share = rows // 2
    group = share
    pairs = width // 128
    ff = act_in.shape[2]
    tiles = ff // TILE
    peers = ((n ^ 1, w), (n ^ 2, w), (n ^ 3, w))
    gives = (n % 2 == 0, n < 2, n < 2)
    takes = (n % 2 == 1, n >= 2, n >= 2)
    order = list(reversed(range(layers)))

    def reducers(turn):
        layer = order[turn]
        made = []
        for kind, (g, o) in enumerate(((gq, oq), (go, oo), (gu, ou), (gd, od))):
            k = turn * 4 + kind
            made.append(Reduce(here, turn, layers, g, bufs[kind], o.at[layer], send, recv, SLOTS * k,
                               credit, 7 * kind, lsem.at[k]))
        return made

    every = [reducers(turn) for turn in range(layers)]

    barrier = pltpu.get_barrier_semaphore()
    zdev = every[0][0]
    hello = peers + ((n, w ^ 1), zdev.inner)
    for device in hello:
        pl.semaphore_signal(barrier, inc=1, device_id=device, device_id_type=MESH)

    @pl.when(zdev.has_outer)
    def _():
        pl.semaphore_signal(barrier, inc=1, device_id=zdev.outer, device_id_type=MESH)

    def stream(layer, j, slot):
        cols = tile_at(j, TILE)
        return [
            pltpu.make_async_copy(fd.at[layer, cols], wd_s.at[slot], stsem.at[slot, 0]),
            pltpu.make_async_copy(fu.at[layer, :, cols], wu_s.at[slot], stsem.at[slot, 1]),
            pltpu.make_async_copy(act_in.at[layer, :, cols], act_s.at[slot], stsem.at[slot, 2]),
            pltpu.make_async_copy(dg_in.at[layer, :, cols], dg_s.at[slot], stsem.at[slot, 3]),
        ]

    def loads(layer):
        pieces = ((mid_in, mid), (ctx_in, ctx), (q_in, q), (nkv_in, nkv), (kv_in, kv), (lse_in, lse), (fo, wo), (fq, wq))
        return [pltpu.make_async_copy(s.at[layer], d, ldsem.at[k]) for k, (s, d) in enumerate(pieces)]

    def load_h(layer):
        if layer == 0:
            return pltpu.make_async_copy(tok, db, ldsem.at[8])
        return pltpu.make_async_copy(h_in.at[layer - 1], mid, ldsem.at[8])

    for c in stream(order[0], 0, 0):
        c.start()
    for c in loads(order[0]):
        c.start()

    local = lax.broadcasted_iota(jnp.int32, (share, 1), 0) + n * share
    valid = (local < lens[0]).astype(F32)
    first_load = pltpu.make_async_copy(cot, db, ldsem.at[9])
    first_load.start()
    first_load.wait()
    for k in range(2):
        dh[k * share:(k + 1) * share] = db[k * share:(k + 1) * share, :].astype(F32) * valid
    gacc[...] = jnp.zeros_like(gacc)
    first = lane_masks(rows)
    masks = head_masks()

    def to_bf16(dst):
        def body(i):
            at = tile_at(i, 64)
            dst[at, :] = dh[at, :].astype(BF16)

        loop(rows // 64, body)

    def norm_of(src, at):
        x = src[at, :].astype(F32)
        c = x - jnp.mean(x, axis=-1, keepdims=True)
        inv = lax.rsqrt(jnp.mean(c * c, axis=-1, keepdims=True) + EPS)
        return c * inv, inv

    def normed_transposed(src, gain, bias):
        for i in range(rows // 128):
            normed, _ = norm_of(src, slice(128 * i, 128 * i + 128))
            at_[:, 128 * i:128 * i + 128] = (normed * gain + bias).astype(BF16).T

    def norm_back(src, gain, row_gain, row_bias):
        step = 32

        def body(i, carry):
            at = tile_at(i, step)
            normed, inv = norm_of(src, at)
            g = da[at, :]
            e = g * gain
            dv = inv * (e - jnp.mean(e, axis=-1, keepdims=True)
                        - normed * jnp.mean(e * normed, axis=-1, keepdims=True))
            dh[at, :] = dh[at, :] + dv
            fold = lambda v: v.reshape(step // 8, 8, width).sum(axis=0)
            return carry[0] + fold(g * normed), carry[1] + fold(g)

        zero = jnp.zeros((8, width), F32)
        one, two = lax.fori_loop(0, rows // step, body, (zero, zero))
        gacc[row_gain:row_gain + 1, :] = jnp.sum(one, axis=0, keepdims=True)
        gacc[row_bias:row_bias + 1, :] = jnp.sum(two, axis=0, keepdims=True)

    def block(pair, k2, v2, at, bias):
        at_pair = tile_at(pair, 128)
        q2 = q[at, at_pair].astype(F32)
        d2 = dctx[at, at_pair].astype(F32)
        k2f = k2.astype(F32)
        dk = dv = dq = None
        for h in range(2):
            row = pl.ds(2 * pair + h, 1)
            qm = (q2 * masks[h]).astype(BF16)
            dm = (d2 * masks[h]).astype(BF16)
            km = (k2f * masks[h]).astype(BF16)
            s = dot_nt(k2, qm)
            if bias is not None:
                s = s + bias
            p = jnp.exp(s - lset[row, at])
            dp = dot_nt(v2, dm)
            ds = (p * (dp - delta[row, at])).astype(BF16)
            ak, av, aq = dot(ds, qm), dot(p.astype(BF16), dm), dot_tn(ds, km)
            dk, dv, dq = (ak, av, aq) if dk is None else (dk + ak, dv + av, dq + aq)
        return dk, dv, dq

    everyone = slice(0, rows)

    def kv_copy(i):
        region = xfer.at[i]
        return pltpu.make_async_remote_copy(
            src_ref=region, dst_ref=region, send_sem=ksend.at[i], recv_sem=krecv.at[i],
            device_id=peers[i], device_id_type=MESH)

    def attend_remote(i):
        @pl.when(takes[i])
        def _():
            rows_of = tile_at(peers[i][0], group)

            def pair_step(pair):
                at_k, at_v = tile_at(pair, 128), tile_at(pair + pairs, 128)
                dk, dv, dq = block(pair, kv[rows_of, at_k], kv[rows_of, at_v], everyone, None)
                xfer[i, :, at_k] = dk.astype(BF16)
                xfer[i, :, at_v] = dv.astype(BF16)
                da[:, at_k] = da[:, at_k] + dq

            loop(pairs, pair_step)

    def attend_own():
        rows_of = tile_at(n, group)

        def pair_step(pair):
            at_k, at_v = tile_at(pair, 128), tile_at(pair + pairs, 128)
            dk, dv, dq = block(pair, kv[rows_of, at_k], kv[rows_of, at_v], everyone, bias_c[...])
            dqkv[share:, tile_at(pair + pairs, 128)] = dk.astype(BF16)
            dqkv[share:, tile_at(pair + 2 * pairs, 128)] = dv.astype(BF16)
            da[:, at_k] = da[:, at_k] + dq
            dk, dv, dq = block(pair, nkv[:, at_k], nkv[:, at_v], slice(0, share), bias_n[...])
            dqkv[:share, tile_at(pair + pairs, 128)] = dk.astype(BF16)
            dqkv[:share, tile_at(pair + 2 * pairs, 128)] = dv.astype(BF16)
            da[:share, at_k] = da[:share, at_k] + dq

        loop(pairs, pair_step)

    pl.semaphore_wait(barrier, jnp.where(zdev.has_outer, 6, 5))

    for turn, layer in enumerate(order):
        last = turn == layers - 1
        r_qkv, r_out, r_up, r_down = every[turn]
        prev = every[turn - 1] if turn else None
        gain1, gain2 = par[2 * layer:2 * layer + 1, :], par[2 * layer + 1:2 * layer + 2, :]
        at = 2 * layers + 2 * layer
        bias1, bias2 = par[at:at + 1, :], par[at + 1:at + 2, :]
        load = loads(layer)
        load[0].wait()
        normed_transposed(mid, gain2, bias2)
        to_bf16(db)
        da[...] = jnp.zeros_like(da)
        if prev:
            prev[0].p2()
            prev[3].p4()
            prev[2].p4()
            prev[3].free_grad()
            prev[2].free_grad()

        def ff_step(j):
            slot = lax.rem(j, 2)
            for c in stream(layer, j, slot):
                c.wait()

            @pl.when(j + 1 < tiles)
            def _():
                for c in stream(layer, j + 1, 1 - slot):
                    c.start()

            dact = dot_nt(db[...], wd_s[slot])
            gd[tile_at(j, TILE), :] = dot_tn(act_s[slot], db[...]).astype(BF16)
            du = (dact * dg_s[slot].astype(F32)).astype(BF16)
            dg_s[slot] = du
            gu[:, tile_at(j, TILE)] = dot(at_[...], dg_s[slot]).astype(BF16)
            da[...] = da[...] + dot_nt(dg_s[slot], wu_s[slot])

        loop(tiles, ff_step)
        r_down.p1()
        r_up.p1()
        norm_back(mid, gain2, 2 * layer + 1, 2 * layers + 2 * layer + 1)
        if layer:
            load_h(layer).start()
        to_bf16(db)
        if prev:
            prev[3].p5()
            prev[1].p4()
            prev[2].p5()
            prev[0].p3()
            prev[1].free_grad()
        load[1].wait()
        load[6].wait()

        def out_tile(j):
            at = tile_at(j, 256)
            go[:, at] = dot_tn(ctx[...], db[:, at]).astype(BF16)
            dctx[:, at] = dot_nt(db[...], wo[at, :]).astype(BF16)

        loop(width // 256, out_tile)
        r_out.p1()
        if layer == 0:
            load_h(layer).start()
        load[5].wait()
        lset[...] = lse[...].T

        def delta_step(pair):
            at = tile_at(pair, 128)
            both = (dctx[:, at].astype(F32) * ctx[:, at].astype(F32)).T
            for h in range(2):
                delta[pl.ds(2 * pair + h, 1), :] = jnp.sum(both[64 * h:64 * h + 64], axis=0, keepdims=True)

        loop(pairs, delta_step)
        da[...] = jnp.zeros_like(da)
        r_down.p2()
        if prev:
            prev[3].p6()
            prev[1].p5()
            prev[2].p6()
        for k in (2, 3, 4):
            load[k].wait()
        for i in (2, 1, 0):
            if turn:
                @pl.when(takes[i])
                def _():
                    kv_copy(i).wait_send()
            attend_remote(i)

            @pl.when(takes[i])
            def _():
                if turn:
                    pl.semaphore_wait(kcredit.at[i], 1)
                kv_copy(i).start()
        r_up.p2()
        r_out.p2()
        attend_own()
        r_down.p3()
        if prev:
            prev[0].p4()
            prev[3].p7()
            prev[1].p6()
            prev[2].p7()
        load_h(layer).wait()
        entry = mid if layer else db
        normed_transposed(entry, gain1, bias1)

        def query_tile(t):
            v = da[:, tile_at(t, 128)] * 0.125
            dqkv[:, tile_at(t, 128)] = (v * cosr[...] - swap_halves(v, first) * sinr[...]).astype(BF16)

        loop(pairs, query_tile)
        if prev:
            prev[0].free_grad()

        def grad_tile(j):
            at = tile_at(j, 256)
            gq[:, at] = dot(at_[...], dqkv[:, at]).astype(BF16)

        loop(width // 256, grad_tile)
        r_up.p3()
        for i in range(3):
            @pl.when(gives[i])
            def _():
                kv_copy(i).wait_recv()

        def arrived(cols):
            total = dqkv[share:, pl.ds(pl.multiple_of(width + cols, 128), 128)].astype(F32)
            for i in range(3):
                total = total + jnp.where(gives[i], xfer[i, :, pl.ds(pl.multiple_of(cols, 128), 128)].astype(F32), 0.0)
            return total

        def key_tile(t):
            at = tile_at(pairs + t, 128)
            v = jnp.concatenate([dqkv[:share, at].astype(F32), arrived(128 * t)], axis=0)
            dqkv[:, at] = (v * cosr[...] - swap_halves(v, first) * sinr[...]).astype(BF16)

        def value_tile(t):
            dqkv[share:, tile_at(2 * pairs + t, 128)] = arrived(128 * t + width).astype(BF16)

        loop(pairs, key_tile)
        loop(pairs, value_tile)
        if not last:
            for i in range(3):
                @pl.when(gives[i])
                def _():
                    pl.semaphore_signal(kcredit.at[i], inc=1, device_id=peers[i], device_id_type=MESH)

        def grad_tile_kv(j):
            grad_tile(j + width // 256)

        loop(2 * width // 256, grad_tile_kv)
        r_qkv.p1()
        load[7].wait()

        def first_tile(j):
            at = tile_at(j, 256)
            da[:, at] = dot_nt(dqkv[...], wq[at, :])

        loop(width // 256, first_tile)
        r_out.p3()
        norm_back(entry, gain1, 2 * layer, 2 * layers + 2 * layer)
        if not last:
            for c in stream(order[turn + 1], 0, 0):
                c.start()
            for c in loads(order[turn + 1]):
                c.start()
        if prev:
            prev[0].p5()
            prev[1].p7()

    prev = every[-2] if layers > 1 else None
    r_qkv, r_out, r_up, r_down = every[-1]
    tot = SmallSum(here, gacc, sbuf, ssend, srecv)
    tot.begin()
    to_bf16(grad_tok)
    r_qkv.p2()
    tot.swap(0)
    if prev:
        prev[0].p6()
        prev[3].free_zb()
        prev[2].free_zb()
    r_down.p4()
    r_up.p4()
    tot.swap(1)
    if prev:
        prev[0].p7()
        prev[1].free_zb()
    r_out.p4()
    r_qkv.p3()
    tot.swap(2)
    r_down.p5()
    r_up.p5()
    r_out.p5()
    tot.chain()
    r_down.p6()
    if prev:
        prev[0].free_zb()
    r_qkv.p4()
    r_up.p6()
    r_out.p6()
    tot.settle()
    r_down.p7()
    r_qkv.p5()
    r_up.p7()
    r_out.p7()
    r_qkv.p6()
    r_qkv.p7()
    tot.finish(small)
    for turn in every:
        for r in turn:
            r.p8()
    for r in every[-1]:
        r.free_grad()
        r.free_zb()
    for i in range(3):
        @pl.when(takes[i])
        def _():
            kv_copy(i).wait_send()


def backward(lengths, cot, tok, par, tabs, full, kept):
    cosr, sinr, bias_c, bias_n = tabs
    rows, width = cot.shape
    share = rows // 2
    layers = full[0].shape[0]
    ff = full[2].shape[2]
    hbm = pl.BlockSpec(memory_space=pltpu.HBM)
    vmem = pl.BlockSpec(memory_space=pltpu.VMEM)
    shape = jax.ShapeDtypeStruct
    v = pltpu.VMEM
    dma, regular = pltpu.SemaphoreType.DMA, pltpu.SemaphoreType.REGULAR
    outs = [shape((layers, f.shape[1] // 4, f.shape[2]), BF16) for f in full]
    scratch = [v(f.shape[1:], BF16) for f in full]
    for f in full:
        total, cols = f.shape[1:]
        quarter = total // 16
        scratch += [v((8 * quarter, cols), BF16), v((4 * quarter, cols), BF16), v((2 * quarter, cols), BF16),
                    v((2 * quarter, cols), BF16), v((quarter, cols), BF16), v((2 * quarter, cols), BF16)]
    scratch += [
        v((2, TILE, width), BF16), v((2, width, TILE), BF16), v((2, rows, TILE), BF16), v((2, rows, TILE), BF16),
        v((width, width), BF16), v((width, 3 * width), BF16),
        v((rows, width), F32), v((rows, width), F32), v((rows, width), F32),
        v((width, rows), BF16), v((rows, width), BF16),
        v((rows, width), BF16), v((4 * share, 2 * width), BF16), v((share, 2 * width), BF16),
        v((rows, width), BF16), v((rows, width), BF16),
        v((rows, 128), F32), v((128, rows), F32), v((16, rows), F32),
        v((rows, 3 * width), BF16), v((3, share, 2 * width), BF16),
        v(par.shape, F32), v((2, 6) + par.shape, F32),
        dma((SLOTS * 4 * layers,)), dma((SLOTS * 4 * layers,)), regular((7 * 4,)), dma((4 * layers,)),
        dma((3,)), dma((3,)), regular((3,)), dma((2, 4)), dma((10,)), dma((6,)), dma((6,)),
    ]
    return pl.pallas_call(
        partial(backward_kernel, layers),
        out_shape=[shape((rows, width), BF16)] + outs + [shape(par.shape, F32)],
        in_specs=[pl.BlockSpec(memory_space=pltpu.SMEM)] + [hbm] * 2 + [vmem] * 5 + [hbm] * 13,
        out_specs=[vmem] + [hbm] * 4 + [vmem],
        scratch_shapes=scratch,
        compiler_params=pltpu.CompilerParams(
            collective_id=1, has_side_effects=True, vmem_limit_bytes=63 * 2**20),
        cost_estimate=pl.CostEstimate(flops=40 * 10**9, bytes_accessed=10**8, transcendentals=10**7),
        name="backward",
    )(lengths, cot, tok, par, cosr, sinr, bias_c.T, bias_n.T, *full, *kept)


def shared_params(norm_gains, norm_biases):
    layers, _, part = norm_gains.shape
    mine = jnp.concatenate([norm_gains.reshape(2 * layers, part), norm_biases.reshape(2 * layers, part)]).astype(F32)
    parts = lax.axis_size("narrow")
    owner = jnp.arange(parts) == lax.axis_index("narrow")
    return jnp.where(owner[None, :, None], mine[:, None, :], 0.0).reshape(4 * layers, parts * part)


def attend_tables(share, head_dim):
    local = lax.axis_index("narrow") * share + jnp.arange(share, dtype=jnp.int32)
    half = head_dim // 2
    freq = jnp.exp(-jnp.log(10000.0) * jnp.arange(half, dtype=F32) * 2.0 / head_dim)
    angle = local.astype(F32)[:, None] * freq[None, :]
    cosine, sine = jnp.cos(angle), jnp.sin(angle)
    cosr = jnp.tile(jnp.concatenate([cosine, cosine], axis=1), (2, 2))
    sinr = jnp.tile(jnp.concatenate([-sine, sine], axis=1), (2, 2))
    block = jnp.arange(share, dtype=jnp.int32) // BLOCK
    same = block[:, None] == block[None, :]
    below = block[None, :] < block[:, None]
    bias = lambda allow: jnp.where(allow, 0.0, NEG).astype(F32)
    return cosr, sinr, jnp.concatenate([bias(below), bias(below | same)]), bias(same)


def on_device(tokens, lengths, w_qkv, w_out, w_up, w_down, norm_gains, norm_biases, cotangent):
    _, _, share, width = tokens.shape
    layers, _, part = norm_gains.shape
    tok = tokens.reshape(2 * share, width)
    tabs = attend_tables(share, width // H)
    outs = forward(tok, shared_params(norm_gains, norm_biases), *tabs, w_qkv, w_out, w_up, w_down)
    result, full, par, kept = outs[0], outs[1:5], outs[5], outs[6:]
    grad_tok, gq, go, gu, gd, small = backward(
        lengths, cotangent.reshape(2 * share, width), tok, par, tabs, full, kept)
    mine = lax.dynamic_slice_in_dim(small, lax.axis_index("narrow") * part, part, 1)
    gains = mine[:2 * layers].reshape(layers, 2, part)
    biases = mine[2 * layers:].reshape(layers, 2, part)
    return (
        result.reshape(tokens.shape), grad_tok.reshape(tokens.shape),
        gq.astype(F32), go.astype(F32), gu.astype(F32), gd.astype(F32),
        gains, biases[:, 0], biases[:, 1],
    )


def solution(mesh):
    return jax.shard_map(
        on_device,
        mesh=mesh,
        in_specs=(
            P("wide", None, "narrow", None),
            P("wide"),
            P(None, "narrow", None),
            P(None, "narrow", None),
            P(None, "narrow", None),
            P(None, "narrow", None),
            P(None, None, "narrow"),
            P(None, None, "narrow"),
            P("wide", None, "narrow", None),
        ),
        out_specs=(
            P("wide", None, "narrow", None),
            P("wide", None, "narrow", None),
            P(None, "narrow", None),
            P(None, "narrow", None),
            P(None, "narrow", None),
            P(None, "narrow", None),
            P(None, None, "narrow"),
            P(None, "narrow"),
            P(None, "narrow"),
        ),
        check_vma=False,
    )
```

time: 1530 us -> 558 us (0.36)
  waiting for transfers between devices: 920 us -> 0 us
  Pallas kernels: 243 us -> 535 us
  matrix products: 138 us -> 0 us
  local copies, waits for them, and re-layouts: 109 us -> 8.92 us
  other arithmetic: 71.1 us -> 12.7 us
  blocking collectives: 16.4 us -> 0 us
  between operations: 17.4 us -> 1.39 us
    reduce_scatter x12 -> x0, waiting for transfers between devices: 501 us -> none  [the longest x2 114 us: on_device(): lax.psum_scatter(grad_down.astype(jnp.bfloat16), 'narrow', scatter_dimens...]
    pallas_call x0 -> x1, Pallas kernels: none -> 289 us  [backward(): pl.pallas_call(partial(backward_kernel, layers), out_shape=[shape((rows,...]
    psum x1 -> x0, waiting for transfers between devices: 271 us -> none  [on_device(): lax.psum((shards[0], shards[1], shards[2], shards[3], shards[4], shards[5...]
    dot_general x42 -> x0, matrix products: 138 us -> none  [the longest x8 48.2 us: outer_sum(): lax.dot_general(left, right, (((0,), (0,)), ((), ())), preferred_element_...]
    unnamed x25 -> x0, waiting for transfers between devices: 101 us -> none
    all_gather x4 -> x0, waiting for transfers between devices: 47.2 us -> none  [the longest x2 47.1 us: on_device(): lax.all_gather(key[:, 1], 'narrow', axis=1, tiled=True)]
    another operation x37 -> x0, other arithmetic: 41 us -> none  [the longest x17 31.6 us: on_device(): jnp.stack([grad_list[layer][kind] for layer in range(layers)])]
    unnamed x238 -> x16, local copies, waits for them, and re-layouts: 33.1 us -> 2.97 us
  transfers between devices with their start and end apart: 21 -> 0, of which waited for: 19 -> 0; matrix products, arithmetic and copies ran while one was open for 14% -> 0% of each run, Pallas kernels for 0% -> 0%
where the time goes in v2:
time: 558 us
  Pallas kernels  535 us (96%)
  other arithmetic  12.7 us (2%)
  local copies, waits for them, and re-layouts  8.92 us (2%)
    pallas_call x1, Pallas kernels, backward(): pl.pallas_call(partial(backward_kernel, layers), out_shape=[shape((rows,...  289 us
    pallas_call x1, Pallas kernels, forward(): pl.pallas_call(partial(forward_kernel, layers), out_shape=[shape((rows, w...  246 us

profile of v2, /device:TPU:0, one launch (start us, length us, event | category | flops | bytes accessed | tf_op | source)
XLA Modules:
  0.0 557.8 jit_solution(13204557662085386738)
XLA Ops:
  0.6 0.7 concatenate.21
  1.3 0.7 concatenate.20
  2.1 0.1 broadcast_in_dim.50
  2.2 0.1 broadcast_in_dim.46
  2.2 0.1 broadcast_in_dim.47
  2.3 0.6 broadcast_select_fusion.prm
  3.0 0.2 fusion.1
  3.2 0.1 tile.8
  3.3 0.8 copy.21.cosr
  4.1 0.1 tile.20
  4.2 0.8 copy.22.sinr
  5.1 0.9 compare_select_fusion.2
  6.0 0.9 fusion.2
  6.9 245.6 %forward.1 = (bf16[512,768]{1,0:T(8,128)(2,1)}, bf16[2,768,2304]{2,1,0:T(8,128)(2,1)}, bf16[2,768,768]{2,1,0:T(8,128)(2,1)}, bf16[2,768,3072]{2,1,0:T(8,128)(2,1...) custom-call(bf16[512,768]{1,0:T(8,128)(2,1)} %bitcast.30, ...), custom_call_target="tpu_custom_call" | custom-call | flops 20000000000 | bytes 100000000 | tf_op jit(solution)/shard_map/forward/pallas_call | solution.py:423
  253.2 1.0 copy.25.bias_c
  254.2 289.1 %backward.1 = (bf16[512,768]{1,0:T(8,128)(2,1)}, bf16[2,192,2304]{2,1,0:T(8,128)(2,1)}, bf16[2,192,768]{2,1,0:T(8,128)(2,1)}, bf16[2,192,3072]{2,1,0:T(8,128)(2,...) custom-call(s32[1]{0:T(128)S(6)} %copy.38.lens, bf16[512,768]{1,0:T(8,128)(2,1)} %bitcast.32, ...), custom_call_target="tpu_custom_call" | custom-call | flops 40000000000 | bytes 100000000 | tf_op jit(solution)/shard_map/backward/pallas_call | solution.py:1189
  543.3 0.0 copy-start.4
  543.3 0.0 copy-start.1
  543.3 3.7 convert_element_type.28
  546.9 0.0 copy-done.4
  546.9 1.1 convert_element_type.29
  548.0 0.0 copy-done.1
  548.0 0.0 copy-start
  548.0 2.8 convert_element_type.30
  550.8 0.0 copy-done
  550.8 0.0 copy-start.2
  550.8 0.0 copy-start.3
  550.8 2.5 convert_element_type.31
  553.4 0.9 fusion.3
  554.2 0.6 reshape.104
  554.8 0.6 copy.35
  555.4 0.6 copy.34
  556.0 0.0 copy-done.2
  556.0 0.9 copy.39
  556.9 0.0 copy-done.3
  556.9 0.9 copy.40
  (11 shorter events, 0.1 us)
Async XLA Ops:
  543.3 3.7 copy-start.4
  543.3 4.8 copy-start.1
  548.0 2.8 copy-start
  550.8 5.2 copy-start.2
  550.8 6.1 %copy-start.3 = (bf16[512,768]{1,0:T(8,128)(2,1)S(1)}, bf16[512,768]{1,0:T(8,128)(2,1)}, u32[]{:S(2)}) copy-start(bf16[512,768]{1,0:T(8,128)(2,1)} %get-tuple-element.45) | copy-start | bytes 2359300

commit v3 on v2

--- a/solution.py
+++ b/solution.py
@@ -2,6 +2,7 @@
 
 import jax
 import jax.numpy as jnp
+import numpy as np
 from jax import lax
 from jax.experimental import pallas as pl
 from jax.experimental.pallas import tpu as pltpu
@@ -38,13 +39,24 @@
     lax.fori_loop(0, count, lambda i, _: (body(i), None)[1], None)
 
 
-def swap_halves(x, first):
-    return jnp.where(first, pltpu.roll(x, 96, 1), pltpu.roll(x, 32, 1))
-
-
-def lane_masks(rows):
-    lane = lax.broadcasted_iota(jnp.int32, (rows, 128), 1)
-    return lane % 64 < 32
+def rotary(x, cosine, sine):
+    lane = lax.broadcasted_iota(jnp.int32, x.shape, 1)
+    swapped = jnp.where(lane % 64 < 32, pltpu.roll(x, 96, 1), pltpu.roll(x, 32, 1))
+    return x * cosine + swapped * sine
+
+
+def rotary_halves(x, cosine, sine):
+    half = x.shape[0] // 2
+    return jnp.concatenate([rotary(x[:half], cosine, sine), rotary(x[half:], cosine, sine)], axis=0)
+
+
+def block_bias(query, key, strict):
+    allow = key < query if strict else key <= query
+    return jnp.where(allow, 0.0, NEG).astype(F32)
+
+
+def blocks_of(shape, dim):
+    return lax.broadcasted_iota(jnp.int32, shape, dim) // BLOCK
 
 
 def head_masks():
@@ -140,9 +152,11 @@
 
 def forward_kernel(
     layers,
-    tok, prm, cosr, sinr, bias_c, bias_n, wq, wo, wu, wd,
-    result, fq, fo, fu, fd, prm_out, h_out, q_out, nkv_out, kv_out, lse_out, ctx_out, mid_out, act_out, dg_out,
-    gq, go, gu, gd, prm_buf, par, hid, a, q, nkv, kv, score, top, lse, ctx, mid, dg, act,
+    tok, prm, cosr, sinr, wq, wo, wu, wd,
+    result, fq, fo, fu, fd, prm_out,
+    h_out, q_out, nkv_out, kv_out, lse_out, ctx_out, mid_out, act_out, dg_out, near_out, all_out, post_out,
+    gq, go, gu, gd, prm_buf, par, hid, a, ag, post, q, nkv, kv, bias_c, bias_n,
+    score, top, lse, lset, ctx, mid, dg, act,
     send, recv, lsem, psend, precv, ksend, krecv, ssem,
 ):
     n = lax.axis_index("narrow")
@@ -170,14 +184,14 @@
             src_ref=prm, dst_ref=prm_buf.at[i], send_sem=psend.at[i], recv_sem=precv.at[i],
             device_id=peers[i], device_id_type=MESH)
 
-    def share_kv(layer, i):
-        region = kv.at[layer, tile_at(n, share)]
+    def share_a(layer, i):
+        region = ag.at[layer, tile_at(n, share)]
         return pltpu.make_async_remote_copy(
             src_ref=region, dst_ref=region, send_sem=ksend.at[3 * layer + i],
             recv_sem=krecv.at[3 * layer + i], device_id=peers[i], device_id_type=MESH)
 
-    def recv_kv(layer, i):
-        region = kv.at[layer, tile_at(peers[i][0], share)]
+    def recv_a(layer, i):
+        region = ag.at[layer, tile_at(peers[i][0], share)]
         return pltpu.make_async_remote_copy(
             src_ref=region, dst_ref=region, send_sem=ksend.at[3 * layer + i],
             recv_sem=krecv.at[3 * layer + i], device_id=peers[i], device_id_type=MESH)
@@ -188,15 +202,15 @@
     for i in range(3):
         params(i).start()
     tensors[0].issue()
-    tensors[1].issue()
 
     def saves(layer):
         pieces = [
-            (q, q_out.at[layer]), (nkv, nkv_out.at[layer]), (kv.at[layer], kv_out.at[layer]),
-            (lse, lse_out.at[layer]), (ctx, ctx_out.at[layer]), (mid, mid_out.at[layer]), (act, act_out.at[layer]),
-            (dg, dg_out.at[layer]), (hid, h_out.at[layer]),
+            (q, q_out.at[layer]), (nkv, nkv_out.at[layer]), (kv, kv_out.at[layer]),
+            (lset, lse_out.at[layer]), (ctx, ctx_out.at[layer]), (mid, mid_out.at[layer]), (act, act_out.at[layer]),
+            (dg, dg_out.at[layer]), (hid, h_out.at[layer]), (a.at[:share], near_out.at[layer]),
+            (ag.at[layer], all_out.at[layer]), (post, post_out.at[layer]),
         ]
-        return [pltpu.make_async_copy(s, d, ssem.at[layer * 9 + k]) for k, (s, d) in enumerate(pieces)]
+        return [pltpu.make_async_copy(s, d, ssem.at[layer * 12 + k]) for k, (s, d) in enumerate(pieces)]
 
     def weight_saves():
         pieces = ((gq, fq), (go, fo), (gu, fu), (gd, fd))
@@ -204,7 +218,7 @@
         for layer in range(layers):
             for kind, (s, d) in enumerate(pieces):
                 k = layer * 4 + kind
-                out.append(pltpu.make_async_copy(s.at[layer], d.at[layer], ssem.at[9 * layers + k]))
+                out.append(pltpu.make_async_copy(s.at[layer], d.at[layer], ssem.at[12 * layers + k]))
         return out
 
     for i in range(3):
@@ -212,10 +226,16 @@
     par[...] = prm[...] + prm_buf[0] + prm_buf[1] + prm_buf[2]
     prm_out[...] = par[...]
 
-    first = lane_masks(rows)
+    for k in range(2):
+        at = slice(k * share, (k + 1) * share)
+        bias_c[at] = block_bias(blocks_of((share, share), 0), blocks_of((share, share), 1), k == 0)
+    same = blocks_of((share, share), 0) == blocks_of((share, share), 1)
+    bias_n[...] = jnp.where(same, 0.0, NEG).astype(F32)
     masks = head_masks()
+    here = tile_at(n, share)
     lanes = lax.broadcasted_iota(jnp.int32, (rows, 128), 1)
 
+    full_saves = weight_saves()
     for layer in range(layers):
         t_qkv, t_out, t_up, t_down = tensors[4 * layer:4 * layer + 4]
         later = tensors[4 * layer + 4:]
@@ -224,56 +244,76 @@
         bias1, bias2 = par[at:at + 1, :], par[at + 1:at + 2, :]
         saved = saves(layer)
         before = saves(layer - 1) if layer else None
+        if before:
+            before[9].wait()
         if layer == 0:
             norm_into(tok, a, gain1, bias1, rows)
         else:
             norm_into(hid, a, gain1, bias1, rows)
-        if layer == 0:
-            t_qkv.forward()
+        ag[layer, here] = a[share:]
+        t_qkv.forward()
+        for i in range(3):
+            @pl.when(gives[i])
+            def _():
+                share_a(layer, i).start()
+        saved[9].start()
+        t_out.issue()
+        t_up.issue()
         t_qkv.finish()
         t_qkv.use()
+        full_saves[4 * layer].start()
         if before:
             before[0].wait()
             before[1].wait()
+            before[2].wait()
 
         wqkv = gq.at[layer]
 
         def query_tile(j):
             x = dot(a[...], wqkv[:, tile_at(j, 256)])
             for part in range(2):
-                v = x[:, 128 * part:128 * part + 128]
-                v = v * cosr[...] + swap_halves(v, first) * sinr[...]
+                v = rotary_halves(x[:, 128 * part:128 * part + 128], cosr[here, :], sinr[here, :])
                 q[:, tile_at(2 * j + part, 128)] = (v.astype(BF16).astype(F32) * 0.125).astype(BF16)
 
         def key_tile(j):
             x = dot(a[...], wqkv[:, tile_at(j + 3, 256)])
             for part in range(2):
-                v = x[:, 128 * part:128 * part + 128]
-                v = (v * cosr[...] + swap_halves(v, first) * sinr[...]).astype(BF16)
+                v = rotary_halves(x[:, 128 * part:128 * part + 128], cosr[here, :], sinr[here, :]).astype(BF16)
                 nkv[:, tile_at(2 * j + part, 128)] = v[:share]
-                kv[layer, tile_at(n, share), tile_at(2 * j + part, 128)] = v[share:]
+                kv[here, tile_at(2 * j + part, 128)] = v[share:]
 
         def value_tile(j):
             v = dot(a[...], wqkv[:, tile_at(j + 6, 256)]).astype(BF16)
             nkv[:, tile_at(j + 3, 256)] = v[:share]
-            kv[layer, tile_at(n, share), tile_at(j + 3, 256)] = v[share:]
+            kv[here, tile_at(j + 3, 256)] = v[share:]
+
+        def far_tiles(g):
+            at = tile_at(g, share)
+
+            def far_key(j):
+                x = dot(ag[layer, at, :], wqkv[:, tile_at(j + 3, 256)])
+                for part in range(2):
+                    v = rotary(x[:, 128 * part:128 * part + 128], cosr[at, :], sinr[at, :])
+                    kv[at, tile_at(2 * j + part, 128)] = v.astype(BF16)
+
+            def far_value(j):
+                kv[at, tile_at(j + 3, 256)] = dot(ag[layer, at, :], wqkv[:, tile_at(j + 6, 256)]).astype(BF16)
+
+            loop(3, far_key)
+            loop(3, far_value)
 
         loop(3, key_tile)
         loop(3, value_tile)
-        for i in range(3):
-            @pl.when(gives[i])
-            def _():
-                share_kv(layer, i).start()
         loop(3, query_tile)
         saved[0].start()
         saved[1].start()
-        t_out.forward()
-        t_up.issue()
         t_down.issue()
         for i in range(3):
             @pl.when(takes[i])
             def _():
-                recv_kv(layer, i).wait_recv()
+                recv_a(layer, i).wait_recv()
+        saved[10].start()
+        loop(n, far_tiles)
         saved[2].start()
         if before:
             before[3].wait()
@@ -286,7 +326,7 @@
             outs = []
             for h in range(2):
                 qm = (q2 * masks[h]).astype(BF16)
-                s = dot_nt(qm, kv[layer, tile_at(n, group), at_pair]) + bias_c[...]
+                s = dot_nt(qm, kv[tile_at(n, group), at_pair]) + bias_c[...]
                 score[:, tile_at(n, group)] = s
                 top[...] = jnp.maximum(s[:, :128], s[:, 128:])
                 s = dot_nt(qm[:share], nkv[:, at_pair]) + bias_n[...]
@@ -294,7 +334,7 @@
                 top[:share] = jnp.maximum(top[:share], jnp.maximum(s[:, :128], s[:, 128:]))
 
                 def scores_of(g):
-                    s = dot_nt(qm, kv[layer, tile_at(g, group), at_pair])
+                    s = dot_nt(qm, kv[tile_at(g, group), at_pair])
                     score[:, tile_at(g, group)] = s
                     top[...] = jnp.maximum(top[...], jnp.maximum(s[:, :128], s[:, 128:]))
 
@@ -309,7 +349,7 @@
                     total, out = carry
                     p = jnp.exp(score[:, tile_at(g, group)] - most)
                     total = total + p[:, :128] + p[:, 128:]
-                    out = out + dot(p.astype(BF16), kv[layer, tile_at(g, group), at_value])
+                    out = out + dot(p.astype(BF16), kv[tile_at(g, group), at_value])
                     return total, out
 
                 total, out = lax.fori_loop(
@@ -320,15 +360,20 @@
                 lse[...] = jnp.where(lanes == 2 * pair + h, most + jnp.log(total), lse[...])
             ctx[:, at_pair] = (outs[0] + outs[1]).astype(BF16)
 
-        loop(pairs, pair_step)
+        loop(pairs // 2, pair_step)
+        t_out.forward()
+        t_up.forward()
+        loop(pairs - pairs // 2, lambda t: pair_step(t + pairs // 2))
+        lset[...] = lse[...].T[:16]
         saved[3].start()
         saved[4].start()
         t_out.finish()
-        t_out.use()
-        t_up.forward()
+        t_up.finish()
+        t_down.forward()
         if later:
             later[0].issue()
-            later[1].issue()
+        t_out.use()
+        full_saves[4 * layer + 1].start()
         if before:
             before[5].wait()
             before[6].wait()
@@ -342,13 +387,16 @@
 
         loop(width // 256, out_tile)
         saved[5].start()
-        norm_into(mid, a, gain2, bias2, rows)
-        t_up.finish()
+        if before:
+            before[11].wait()
+        norm_into(mid, post, gain2, bias2, rows)
+        saved[11].start()
         t_up.use()
+        full_saves[4 * layer + 2].start()
 
         def up_tile(j):
             at = tile_at(j, 256)
-            x = dot(a[...], gu[layer, :, at])
+            x = dot(post[...], gu[layer, :, at])
             x2 = x * x
             t = jnp.tanh(GELU_C * (x + GELU_A * (x * x2)))
             cdf = 0.5 + 0.5 * t
@@ -359,11 +407,9 @@
         loop(ff // 256, up_tile)
         saved[6].start()
         saved[7].start()
-        t_down.forward()
-        if later:
-            later[0].forward()
         t_down.finish()
         t_down.use()
+        full_saves[4 * layer + 3].start()
 
         def down_tile(j):
             at = tile_at(j, 256)
@@ -375,13 +421,11 @@
         loop(width // 256, down_tile)
         saved[8].start()
 
-    for c in weight_saves():
-        c.start()
     for c in saves(layers - 1):
         c.wait()
     for layer in range(layers - 1):
-        saves(layer)[2].wait()
-    for c in weight_saves():
+        saves(layer)[10].wait()
+    for c in full_saves:
         c.wait()
     for t in tensors:
         t.drain()
@@ -390,10 +434,10 @@
         for layer in range(layers):
             @pl.when(gives[i])
             def _():
-                share_kv(layer, i).wait_send()
-
-
-def forward(tokens, prm, cosr, sinr, bias_c, bias_n, w_qkv, w_out, w_up, w_down):
+                share_a(layer, i).wait_send()
+
+
+def forward(tokens, prm, cosr, sinr, w_qkv, w_out, w_up, w_down):
     rows, width = tokens.shape
     share = rows // 2
     layers = w_qkv.shape[0]
@@ -413,42 +457,50 @@
         shape((layers, rows, width), BF16),
         shape((layers, share, 2 * width), BF16),
         shape((layers, seq, 2 * width), BF16),
-        shape((layers, rows, 128), F32),
+        shape((layers, 16, rows), F32),
         shape((layers, rows, width), BF16),
         shape((layers, rows, width), F32),
         shape((layers, rows, ff), BF16),
         shape((layers, rows, ff), BF16),
+        shape((layers, share, width), BF16),
+        shape((layers, seq, width), BF16),
+        shape((layers, rows, width), BF16),
     ]
     dma, count = pltpu.SemaphoreType.DMA, 7 * 4 * layers
     return pl.pallas_call(
         partial(forward_kernel, layers),
         out_shape=[shape((rows, width), BF16)] + full + [shape(prm.shape, F32)] + kept,
-        in_specs=[vmem] * 6 + [hbm] * 4,
-        out_specs=[vmem] + [hbm] * 4 + [vmem] + [hbm] * 9,
+        in_specs=[vmem] * 4 + [hbm] * 4,
+        out_specs=[vmem] + [hbm] * 4 + [vmem] + [hbm] * 12,
         scratch_shapes=[pltpu.VMEM(f.shape, BF16) for f in full] + [
             pltpu.VMEM((3,) + prm.shape, F32),
             pltpu.VMEM(prm.shape, F32),
             pltpu.VMEM((rows, width), F32),
             pltpu.VMEM((rows, width), BF16),
+            pltpu.VMEM((layers, seq, width), BF16),
+            pltpu.VMEM((rows, width), BF16),
             pltpu.VMEM((rows, width), BF16),
             pltpu.VMEM((share, 2 * width), BF16),
-            pltpu.VMEM((layers, seq, 2 * width), BF16),
+            pltpu.VMEM((seq, 2 * width), BF16),
+            pltpu.VMEM((rows, share), F32),
+            pltpu.VMEM((share, share), F32),
             pltpu.VMEM((rows, seq + share), F32),
             pltpu.VMEM((rows, 128), F32),
             pltpu.VMEM((rows, 128), F32),
+            pltpu.VMEM((16, rows), F32),
             pltpu.VMEM((rows, width), BF16),
             pltpu.VMEM((rows, width), F32),
             pltpu.VMEM((rows, ff), BF16),
             pltpu.VMEM((rows, ff), BF16),
             dma((count,)), dma((count,)), dma((4 * layers,)),
             dma((3,)), dma((3,)), dma((3 * layers,)), dma((3 * layers,)),
-            dma((9 * layers + 4 * layers,)),
+            dma((16 * layers,)),
         ],
         compiler_params=pltpu.CompilerParams(
             collective_id=0, has_side_effects=True, vmem_limit_bytes=62 * 2**20),
         cost_estimate=pl.CostEstimate(flops=20 * 10**9, bytes_accessed=10**8, transcendentals=10**7),
         name="forward",
-    )(tokens, prm, cosr, sinr, bias_c, bias_n, w_qkv, w_out, w_up, w_down)
+    )(tokens, prm, cosr, sinr, w_qkv, w_out, w_up, w_down)
 
 
 def add_rows(dst, at, left, left_at, right, right_at, rows):
@@ -460,9 +512,10 @@
 
 
 class Reduce:
-    def __init__(self, here, turn, turns, grad, bufs, out, send, recv, base, credit, cbase, lsem):
+    def __init__(self, here, turn, turns, kind, grad, bufs, out, send, recv, base, credit, cbase, lend, lsem):
         self.n, self.w = here
-        self.turn, self.turns = turn, turns
+        self.turn, self.turns, self.kind = turn, turns, kind
+        self.lend = lend
         self.grad, self.out = grad, out
         self.s1, self.r2, self.r3, self.r4, self.r5, self.zb = bufs
         self.send, self.recv, self.base = send, recv, base
@@ -544,7 +597,13 @@
         return pltpu.make_async_copy(src, self.done_at(self.core, self.mine), self.lsem)
 
     def p1(self):
-        self.take(0)
+        if self.kind == "d":
+            self.take(0)
+        elif self.kind == "u":
+            for k in range(4 if self.turn else 0):
+                pl.semaphore_wait(self.lend.at[k + 4], 1)
+        else:
+            pl.semaphore_wait(self.lend.at["qkvo".index(self.kind)], 1)
         for c in self.to_sibling():
             c.start()
 
@@ -553,7 +612,16 @@
         for m, c in enumerate(self.to_sibling()):
             c.wait_recv()
             add_rows(g, self.at(m, self.core), g, self.at(m, self.core), self.s1, m * self.half, self.half)
-        self.give(0, self.s)
+        if self.kind == "d":
+            self.give(0, self.s)
+        elif self.kind == "u":
+            for k in range(4):
+                pl.semaphore_signal(self.lend.at[k], inc=1, device_id=self.s, device_id_type=MESH)
+        elif self.turn < self.turns - 1:
+            k = "qkvo".index(self.kind) + 4
+            pl.semaphore_signal(self.lend.at[k], inc=1, device_id=self.s, device_id_type=MESH)
+
+    def p2s(self):
         self.take(1)
         self.take(2)
         for c in self.first_hop():
@@ -575,15 +643,15 @@
         for k in range(2):
             hops[2 * k].wait_recv()
             at = self.at(self.n, self.core, k)
-            add_rows(g, at, g, at, self.r2, 2 * k * q, q)
+            add_rows(self.zb, k * q, g, at, self.r2, 2 * k * q, q)
         self.give(1, self.x)
         self.give(2, self.y)
 
     def p4(self):
-        g, q = self.grad, self.quarter
+        q = self.quarter
         for k, c in enumerate(self.second_hop()):
             c.wait_recv()
-            add_rows(self.zb, k * q, g, self.at(self.n, self.core, k), self.r3, k * q, q)
+            add_rows(self.zb, k * q, self.zb, k * q, self.r3, k * q, q)
         self.give(3, self.y)
         self.give(4, self.x)
 
@@ -757,19 +825,53 @@
             self.copy(5, self.outer).wait_send()
 
 
+PLAN = {
+    (0, "ffn2"): ("0u1",),
+    (0, "out"): ("0u2", "0us",),
+    (0, "send2"): ("0o1",),
+    (0, "send1"): ("0d1",),
+    (0, "rem0"): ("0u3",),
+    (0, "q"): ("0d2", "0ds",),
+    (0, "gk"): ("0q1", "0u4",),
+    (0, "da"): ("0k1",),
+    (0, "lna"): ("0v1", "0o2", "0k2", "0ks", "0d3", "0os",),
+    (1, "ffn2"): ("0d4", "0o3",),
+    (1, "lnb"): ("0k3", "0u5",),
+    (1, "out"): ("0v2", "0vs", "0q2", "0qs", "0k4",),
+    (1, "delta"): ("1d1",),
+    (1, "rem2"): ("0v3", "0d5", "0k5",),
+    (1, "send2"): ("0q3", "1u1",),
+    (1, "rem1"): ("1d2", "0u6", "0v4", "1u2", "1us",),
+    (1, "send1"): ("0q4", "0d6",),
+    (1, "own0"): ("0u7",),
+    (1, "own1"): ("1u3", "0q5",),
+    (1, "tr"): ("0d7",),
+    (1, "q"): ("1ds",),
+    (1, "gq"): ("0k6",),
+    (1, "gk"): ("0q6", "1q1", "1k1", "1u4", "0v5",),
+    (1, "da"): ("0o4",),
+    (9, "tot0"): ("1d3", "1v1", "0v6", "0v7", "0q7", "1k2", "1ks", "1o1",),
+    (9, "tot1"): ("1d4", "1u5", "1o2", "0k7",),
+    (9, "tot2"): ("0o5", "1u6", "1v2", "1vs", "1q2", "1qs",),
+    (9, "tot3"): ("1k3", "0o6",),
+    (9, "tot4"): ("1v3", "1os", "0o7", "1u7", "1d5", "1k4", "1o3", "1q3", "1v4", "1d6", "1k5", "1o4", "1q4", "1v5", "1d7", "1k6", "1o5", "1q5", "1v6", "1k7", "1o6", "1q6", "1v7", "1o7", "1q7",),
+}
 TILE = 512
 
 
 def backward_kernel(
     layers,
-    lens, cot, tok, par, cosr, sinr, bias_c, bias_n,
-    fq, fo, fu, fd, h_in, q_in, nkv_in, kv_in, lse_in, ctx_in, mid_in, act_in, dg_in,
+    lens, cot, tok, par, cosr, sinr,
+    fq, fo, fu, fd, h_in, q_in, nkv_in, kv_in, lse_in, ctx_in, mid_in, act_in, dg_in, near_in, all_in, post_in,
     grad_tok, oq, oo, ou, od, small,
-    gq, go, gu, gd, *rest,
+    *rest,
 ):
-    bufs, rest = [rest[6 * k:6 * k + 6] for k in range(4)], rest[24:]
-    (wd_s, wu_s, act_s, dg_s, wo, wq, dh, mid, da, at_, db, q, kv, nkv, ctx, dctx, lse, lset, delta, dqkv, xfer,
-     gacc, sbuf, send, recv, credit, lsem, ksend, krecv, kcredit, stsem, ldsem, ssend, srecv) = rest
+    width = cot.shape[1]
+    grads, big, small_s1 = dict(zip("qkvoud", rest[:6])), rest[6], rest[7]
+    bufs = {kind: rest[8 + 5 * k:13 + 5 * k] for k, kind in enumerate("qkvoud")}
+    rest = rest[38:]
+    (wd_s, wu_s, act_s, dg_s, wo, wq, dh, mid, da, at_, db, q, kv, nkv, ctx, dctx, lset, delta, dqkv, dkv, xda, far, acc,
+     gacc, sbuf, send, recv, credit, lend, lsem, ksend, krecv, kcredit, stsem, ldsem, ssend, srecv) = rest
     n = lax.axis_index("narrow")
     w = lax.axis_index("wide")
     here = (n, w)
@@ -786,17 +888,24 @@
 
     def reducers(turn):
         layer = order[turn]
-        made = []
-        for kind, (g, o) in enumerate(((gq, oq), (go, oo), (gu, ou), (gd, od))):
-            k = turn * 4 + kind
-            made.append(Reduce(here, turn, layers, g, bufs[kind], o.at[layer], send, recv, SLOTS * k,
-                               credit, 7 * kind, lsem.at[k]))
+        made = {}
+        for kind, name in enumerate("qkvoud"):
+            if name in "qkv":
+                out = oq.at[layer, :, kind * width:(kind + 1) * width]
+            else:
+                out = {"o": oo, "u": ou, "d": od}[name].at[layer]
+            s1 = {"u": big, "d": small_s1}.get(name)
+            if s1 is None:
+                s1 = big.at[:, kind * width:(kind + 1) * width]
+            k = turn * 6 + kind
+            made[name] = Reduce(here, turn, layers, name, grads[name], (s1,) + tuple(bufs[name]), out, send, recv,
+                                SLOTS * k, credit, 7 * kind, lend, lsem.at[k])
         return made
 
     every = [reducers(turn) for turn in range(layers)]
 
     barrier = pltpu.get_barrier_semaphore()
-    zdev = every[0][0]
+    zdev = every[0]["q"]
     hello = peers + ((n, w ^ 1), zdev.inner)
     for device in hello:
         pl.semaphore_signal(barrier, inc=1, device_id=device, device_id_type=MESH)
@@ -815,13 +924,22 @@
         ]
 
     def loads(layer):
-        pieces = ((mid_in, mid), (ctx_in, ctx), (q_in, q), (nkv_in, nkv), (kv_in, kv), (lse_in, lse), (fo, wo), (fq, wq))
+        pieces = ((mid_in, mid), (ctx_in, ctx), (q_in, q), (nkv_in, nkv), (kv_in, kv), (lse_in, lset), (fo, wo), (fq, wq),
+                  (post_in, dctx))
         return [pltpu.make_async_copy(s.at[layer], d, ldsem.at[k]) for k, (s, d) in enumerate(pieces)]
 
     def load_h(layer):
         if layer == 0:
-            return pltpu.make_async_copy(tok, db, ldsem.at[8])
-        return pltpu.make_async_copy(h_in.at[layer - 1], mid, ldsem.at[8])
+            return pltpu.make_async_copy(tok, db, ldsem.at[10])
+        return pltpu.make_async_copy(h_in.at[layer - 1], mid, ldsem.at[10])
+
+    def load_first(layer):
+        own = all_in.at[layer, tile_at(n, share)]
+        return [pltpu.make_async_copy(near_in.at[layer], ctx.at[:share], ldsem.at[11]),
+                pltpu.make_async_copy(own, ctx.at[share:], ldsem.at[12])]
+
+    def load_far(layer, i):
+        return pltpu.make_async_copy(all_in.at[layer, tile_at(peers[i][0], share)], far.at[i], ldsem.at[13 + i])
 
     for c in stream(order[0], 0, 0):
         c.start()
@@ -836,8 +954,9 @@
     for k in range(2):
         dh[k * share:(k + 1) * share] = db[k * share:(k + 1) * share, :].astype(F32) * valid
     gacc[...] = jnp.zeros_like(gacc)
-    first = lane_masks(rows)
+    go, gu, gd = grads["o"], grads["u"], grads["d"]
     masks = head_masks()
+    mine = tile_at(n, share)
 
     def to_bf16(dst):
         def body(i):
@@ -852,10 +971,9 @@
         inv = lax.rsqrt(jnp.mean(c * c, axis=-1, keepdims=True) + EPS)
         return c * inv, inv
 
-    def normed_transposed(src, gain, bias):
+    def transposed(src):
         for i in range(rows // 128):
-            normed, _ = norm_of(src, slice(128 * i, 128 * i + 128))
-            at_[:, 128 * i:128 * i + 128] = (normed * gain + bias).astype(BF16).T
+            at_[:, 128 * i:128 * i + 128] = src[128 * i:128 * i + 128, :].T
 
     def norm_back(src, gain, row_gain, row_bias):
         step = 32
@@ -889,7 +1007,7 @@
             km = (k2f * masks[h]).astype(BF16)
             s = dot_nt(k2, qm)
             if bias is not None:
-                s = s + bias
+                s = s + bias()
             p = jnp.exp(s - lset[row, at])
             dp = dot_nt(v2, dm)
             ds = (p * (dp - delta[row, at])).astype(BF16)
@@ -900,7 +1018,7 @@
     everyone = slice(0, rows)
 
     def kv_copy(i):
-        region = xfer.at[i]
+        region = xda.at[i]
         return pltpu.make_async_remote_copy(
             src_ref=region, dst_ref=region, send_sem=ksend.at[i], recv_sem=krecv.at[i],
             device_id=peers[i], device_id_type=MESH)
@@ -913,48 +1031,67 @@
             def pair_step(pair):
                 at_k, at_v = tile_at(pair, 128), tile_at(pair + pairs, 128)
                 dk, dv, dq = block(pair, kv[rows_of, at_k], kv[rows_of, at_v], everyone, None)
-                xfer[i, :, at_k] = dk.astype(BF16)
-                xfer[i, :, at_v] = dv.astype(BF16)
+                dkv[i, :, at_k] = rotary(dk, cosr[rows_of, :], -sinr[rows_of, :]).astype(BF16)
+                dkv[i, :, at_v] = dv.astype(BF16)
                 da[:, at_k] = da[:, at_k] + dq
 
+            def away_tile(j):
+                at = tile_at(j, 256)
+                xda[i, :, at] = dot_nt(dkv[i], wq[at, width:3 * width]).astype(BF16)
+
             loop(pairs, pair_step)
-
-    def attend_own():
+            loop(width // 256, away_tile)
+
+    def own_bias():
+        key = blocks_of((group, share), 0)
+        query = blocks_of((group, share), 1)
+        return jnp.concatenate([block_bias(query, key, True), block_bias(query, key, False)], axis=1)
+
+    def near_bias():
+        same = blocks_of((share, share), 0) == blocks_of((share, share), 1)
+        return jnp.where(same, 0.0, NEG).astype(F32)
+
+    def attend_own(low, high):
         rows_of = tile_at(n, group)
 
         def pair_step(pair):
             at_k, at_v = tile_at(pair, 128), tile_at(pair + pairs, 128)
-            dk, dv, dq = block(pair, kv[rows_of, at_k], kv[rows_of, at_v], everyone, bias_c[...])
-            dqkv[share:, tile_at(pair + pairs, 128)] = dk.astype(BF16)
+            dk, dv, dq = block(pair, kv[rows_of, at_k], kv[rows_of, at_v], everyone, own_bias)
+            dqkv[share:, tile_at(pair + pairs, 128)] = rotary(dk, cosr[mine, :], -sinr[mine, :]).astype(BF16)
             dqkv[share:, tile_at(pair + 2 * pairs, 128)] = dv.astype(BF16)
             da[:, at_k] = da[:, at_k] + dq
-            dk, dv, dq = block(pair, nkv[:, at_k], nkv[:, at_v], slice(0, share), bias_n[...])
-            dqkv[:share, tile_at(pair + pairs, 128)] = dk.astype(BF16)
+            dk, dv, dq = block(pair, nkv[:, at_k], nkv[:, at_v], slice(0, share), near_bias)
+            dqkv[:share, tile_at(pair + pairs, 128)] = rotary(dk, cosr[mine, :], -sinr[mine, :]).astype(BF16)
             dqkv[:share, tile_at(pair + 2 * pairs, 128)] = dv.astype(BF16)
             da[:share, at_k] = da[:share, at_k] + dq
 
-        loop(pairs, pair_step)
+        loop(high - low, lambda t: pair_step(t + low))
 
     pl.semaphore_wait(barrier, jnp.where(zdev.has_outer, 6, 5))
+
+    def run(turn, slot):
+        for word in PLAN.get((turn, slot), ()):
+            r, act = every[int(word[0])][word[1]], word[2]
+            if act == "3" and r.turn:
+                every[r.turn - 1][word[1]].free_zb()
+            {"1": r.p1, "2": r.p2, "s": r.p2s, "3": r.p3, "4": r.p4, "5": r.p5, "6": r.p6, "7": r.p7}[act]()
 
     for turn, layer in enumerate(order):
         last = turn == layers - 1
-        r_qkv, r_out, r_up, r_down = every[turn]
-        prev = every[turn - 1] if turn else None
+        after = lambda slot: run(turn, slot)
+
+        def reuse(*names):
+            if turn:
+                for name in names:
+                    every[turn - 1][name].free_grad()
+
         gain1, gain2 = par[2 * layer:2 * layer + 1, :], par[2 * layer + 1:2 * layer + 2, :]
-        at = 2 * layers + 2 * layer
-        bias1, bias2 = par[at:at + 1, :], par[at + 1:at + 2, :]
         load = loads(layer)
-        load[0].wait()
-        normed_transposed(mid, gain2, bias2)
+        load[8].wait()
+        transposed(dctx)
         to_bf16(db)
         da[...] = jnp.zeros_like(da)
-        if prev:
-            prev[0].p2()
-            prev[3].p4()
-            prev[2].p4()
-            prev[3].free_grad()
-            prev[2].free_grad()
+        reuse("u", "d")
 
         def ff_step(j):
             slot = lax.rem(j, 2)
@@ -973,21 +1110,20 @@
             gu[:, tile_at(j, TILE)] = dot(at_[...], dg_s[slot]).astype(BF16)
             da[...] = da[...] + dot_nt(dg_s[slot], wu_s[slot])
 
-        loop(tiles, ff_step)
-        r_down.p1()
-        r_up.p1()
+        for k in range(3):
+            low, high = tiles * k // 3, tiles * (k + 1) // 3
+            loop(high - low, lambda j: ff_step(j + low))
+            after("ffn%d" % k)
+        load[0].wait()
         norm_back(mid, gain2, 2 * layer + 1, 2 * layers + 2 * layer + 1)
         if layer:
             load_h(layer).start()
+        after("lnb")
         to_bf16(db)
-        if prev:
-            prev[3].p5()
-            prev[1].p4()
-            prev[2].p5()
-            prev[0].p3()
-            prev[1].free_grad()
+        after("bf")
         load[1].wait()
         load[6].wait()
+        reuse("o")
 
         def out_tile(j):
             at = tile_at(j, 256)
@@ -995,11 +1131,10 @@
             dctx[:, at] = dot_nt(db[...], wo[at, :]).astype(BF16)
 
         loop(width // 256, out_tile)
-        r_out.p1()
+        after("out")
         if layer == 0:
             load_h(layer).start()
         load[5].wait()
-        lset[...] = lse[...].T
 
         def delta_step(pair):
             at = tile_at(pair, 128)
@@ -1008,13 +1143,15 @@
                 delta[pl.ds(2 * pair + h, 1), :] = jnp.sum(both[64 * h:64 * h + 64], axis=0, keepdims=True)
 
         loop(pairs, delta_step)
+        for c in load_first(layer):
+            c.start()
+        for i in range(3):
+            @pl.when(takes[i])
+            def _():
+                load_far(layer, i).start()
         da[...] = jnp.zeros_like(da)
-        r_down.p2()
-        if prev:
-            prev[3].p6()
-            prev[1].p5()
-            prev[2].p6()
-        for k in (2, 3, 4):
+        after("delta")
+        for k in (2, 3, 4, 7):
             load[k].wait()
         for i in (2, 1, 0):
             if turn:
@@ -1022,131 +1159,97 @@
                 def _():
                     kv_copy(i).wait_send()
             attend_remote(i)
+            after("rem%d" % i)
 
             @pl.when(takes[i])
             def _():
                 if turn:
                     pl.semaphore_wait(kcredit.at[i], 1)
                 kv_copy(i).start()
-        r_up.p2()
-        r_out.p2()
-        attend_own()
-        r_down.p3()
-        if prev:
-            prev[0].p4()
-            prev[3].p7()
-            prev[1].p6()
-            prev[2].p7()
+            after("send%d" % i)
+        attend_own(0, pairs // 2)
+        after("own0")
+        attend_own(pairs // 2, pairs)
+        after("own1")
+        for c in load_first(layer):
+            c.wait()
+        transposed(ctx)
+        after("tr")
+
+        def query_tile(t):
+            v = da[:, tile_at(t, 128)] * 0.125
+            dqkv[:, tile_at(t, 128)] = rotary_halves(v, cosr[mine, :], -sinr[mine, :]).astype(BF16)
+
+        loop(pairs, query_tile)
+        after("q")
+        reuse("q")
+
+        def grad_tile(j):
+            at = tile_at(j, 256)
+            grads["q"][:, at] = dot(at_[...], dqkv[:, at]).astype(BF16)
+
+        loop(width // 256, grad_tile)
+        after("gq")
+        for i in range(3):
+            @pl.when(takes[i])
+            def _():
+                load_far(layer, i).wait()
+
+        def grad_tile_kv(j, skip, out):
+            acc[...] = dot(at_[...], dqkv[:, tile_at(j + (1 + skip) * (width // 256), 256)])
+            for i in range(3):
+                @pl.when(takes[i])
+                def _():
+                    acc[...] = acc[...] + dot_tn(far[i], dkv[i, :, tile_at(j + skip * (width // 256), 256)])
+            out[:, tile_at(j, 256)] = acc[...].astype(BF16)
+
+        for k, name in enumerate("kv"):
+            reuse(name)
+            loop(width // 256, lambda j: grad_tile_kv(j, k, grads[name]))
+            after("g" + name)
+
+        def first_tile(j):
+            at = tile_at(j, 256)
+            da[:, at] = dot_nt(dqkv[...], wq[at, :])
+
+        loop(width // 256, first_tile)
+        after("da")
         load_h(layer).wait()
         entry = mid if layer else db
-        normed_transposed(entry, gain1, bias1)
-
-        def query_tile(t):
-            v = da[:, tile_at(t, 128)] * 0.125
-            dqkv[:, tile_at(t, 128)] = (v * cosr[...] - swap_halves(v, first) * sinr[...]).astype(BF16)
-
-        loop(pairs, query_tile)
-        if prev:
-            prev[0].free_grad()
-
-        def grad_tile(j):
-            at = tile_at(j, 256)
-            gq[:, at] = dot(at_[...], dqkv[:, at]).astype(BF16)
-
-        loop(width // 256, grad_tile)
-        r_up.p3()
         for i in range(3):
             @pl.when(gives[i])
             def _():
                 kv_copy(i).wait_recv()
-
-        def arrived(cols):
-            total = dqkv[share:, pl.ds(pl.multiple_of(width + cols, 128), 128)].astype(F32)
-            for i in range(3):
-                total = total + jnp.where(gives[i], xfer[i, :, pl.ds(pl.multiple_of(cols, 128), 128)].astype(F32), 0.0)
-            return total
-
-        def key_tile(t):
-            at = tile_at(pairs + t, 128)
-            v = jnp.concatenate([dqkv[:share, at].astype(F32), arrived(128 * t)], axis=0)
-            dqkv[:, at] = (v * cosr[...] - swap_halves(v, first) * sinr[...]).astype(BF16)
-
-        def value_tile(t):
-            dqkv[share:, tile_at(2 * pairs + t, 128)] = arrived(128 * t + width).astype(BF16)
-
-        loop(pairs, key_tile)
-        loop(pairs, value_tile)
-        if not last:
-            for i in range(3):
-                @pl.when(gives[i])
-                def _():
+                da[share:, :] = da[share:, :] + xda[i].astype(F32)
+                if not last:
                     pl.semaphore_signal(kcredit.at[i], inc=1, device_id=peers[i], device_id_type=MESH)
-
-        def grad_tile_kv(j):
-            grad_tile(j + width // 256)
-
-        loop(2 * width // 256, grad_tile_kv)
-        r_qkv.p1()
-        load[7].wait()
-
-        def first_tile(j):
-            at = tile_at(j, 256)
-            da[:, at] = dot_nt(dqkv[...], wq[at, :])
-
-        loop(width // 256, first_tile)
-        r_out.p3()
+        after("kvwait")
         norm_back(entry, gain1, 2 * layer, 2 * layers + 2 * layer)
         if not last:
             for c in stream(order[turn + 1], 0, 0):
                 c.start()
             for c in loads(order[turn + 1]):
                 c.start()
-        if prev:
-            prev[0].p5()
-            prev[1].p7()
-
-    prev = every[-2] if layers > 1 else None
-    r_qkv, r_out, r_up, r_down = every[-1]
+        after("lna")
+
     tot = SmallSum(here, gacc, sbuf, ssend, srecv)
     tot.begin()
     to_bf16(grad_tok)
-    r_qkv.p2()
+    run(9, "tot0")
     tot.swap(0)
-    if prev:
-        prev[0].p6()
-        prev[3].free_zb()
-        prev[2].free_zb()
-    r_down.p4()
-    r_up.p4()
+    run(9, "tot1")
     tot.swap(1)
-    if prev:
-        prev[0].p7()
-        prev[1].free_zb()
-    r_out.p4()
-    r_qkv.p3()
+    run(9, "tot2")
     tot.swap(2)
-    r_down.p5()
-    r_up.p5()
-    r_out.p5()
+    run(9, "tot3")
     tot.chain()
-    r_down.p6()
-    if prev:
-        prev[0].free_zb()
-    r_qkv.p4()
-    r_up.p6()
-    r_out.p6()
+    run(9, "tot4")
     tot.settle()
-    r_down.p7()
-    r_qkv.p5()
-    r_up.p7()
-    r_out.p7()
-    r_qkv.p6()
-    r_qkv.p7()
     tot.finish(small)
     for turn in every:
-        for r in turn:
+        for r in turn.values():
             r.p8()
-    for r in every[-1]:
+    for r in every[-1].values():
         r.free_grad()
         r.free_zb()
     for i in range(3):
@@ -1156,7 +1259,7 @@
 
 
 def backward(lengths, cot, tok, par, tabs, full, kept):
-    cosr, sinr, bias_c, bias_n = tabs
+    cosr, sinr = tabs
     rows, width = cot.shape
     share = rows // 2
     layers = full[0].shape[0]
@@ -1167,11 +1270,11 @@
     v = pltpu.VMEM
     dma, regular = pltpu.SemaphoreType.DMA, pltpu.SemaphoreType.REGULAR
     outs = [shape((layers, f.shape[1] // 4, f.shape[2]), BF16) for f in full]
-    scratch = [v(f.shape[1:], BF16) for f in full]
-    for f in full:
-        total, cols = f.shape[1:]
+    kinds = [(width, width)] * 4 + [(width, ff), (ff, width)]
+    scratch = [v(k, BF16) for k in kinds] + [v((width // 2, ff), BF16), v((ff // 2, width), BF16)]
+    for total, cols in kinds:
         quarter = total // 16
-        scratch += [v((8 * quarter, cols), BF16), v((4 * quarter, cols), BF16), v((2 * quarter, cols), BF16),
+        scratch += [v((4 * quarter, cols), BF16), v((2 * quarter, cols), BF16),
                     v((2 * quarter, cols), BF16), v((quarter, cols), BF16), v((2 * quarter, cols), BF16)]
     scratch += [
         v((2, TILE, width), BF16), v((2, width, TILE), BF16), v((2, rows, TILE), BF16), v((2, rows, TILE), BF16),
@@ -1180,23 +1283,24 @@
         v((width, rows), BF16), v((rows, width), BF16),
         v((rows, width), BF16), v((4 * share, 2 * width), BF16), v((share, 2 * width), BF16),
         v((rows, width), BF16), v((rows, width), BF16),
-        v((rows, 128), F32), v((128, rows), F32), v((16, rows), F32),
-        v((rows, 3 * width), BF16), v((3, share, 2 * width), BF16),
+        v((16, rows), F32), v((16, rows), F32),
+        v((rows, 3 * width), BF16), v((3, share, 2 * width), BF16), v((3, share, width), BF16),
+        v((3, share, width), BF16), v((width, 256), F32),
         v(par.shape, F32), v((2, 6) + par.shape, F32),
-        dma((SLOTS * 4 * layers,)), dma((SLOTS * 4 * layers,)), regular((7 * 4,)), dma((4 * layers,)),
-        dma((3,)), dma((3,)), regular((3,)), dma((2, 4)), dma((10,)), dma((6,)), dma((6,)),
+        dma((SLOTS * 6 * layers,)), dma((SLOTS * 6 * layers,)), regular((7 * 6,)), regular((8,)), dma((6 * layers,)),
+        dma((3,)), dma((3,)), regular((3,)), dma((2, 4)), dma((16,)), dma((6,)), dma((6,)),
     ]
     return pl.pallas_call(
         partial(backward_kernel, layers),
         out_shape=[shape((rows, width), BF16)] + outs + [shape(par.shape, F32)],
-        in_specs=[pl.BlockSpec(memory_space=pltpu.SMEM)] + [hbm] * 2 + [vmem] * 5 + [hbm] * 13,
+        in_specs=[pl.BlockSpec(memory_space=pltpu.SMEM)] + [hbm] * 2 + [vmem] * 3 + [hbm] * 16,
         out_specs=[vmem] + [hbm] * 4 + [vmem],
         scratch_shapes=scratch,
         compiler_params=pltpu.CompilerParams(
             collective_id=1, has_side_effects=True, vmem_limit_bytes=63 * 2**20),
         cost_estimate=pl.CostEstimate(flops=40 * 10**9, bytes_accessed=10**8, transcendentals=10**7),
         name="backward",
-    )(lengths, cot, tok, par, cosr, sinr, bias_c.T, bias_n.T, *full, *kept)
+    )(lengths, cot, tok, par, cosr, sinr, *full, *kept)
 
 
 def shared_params(norm_gains, norm_biases):
@@ -1207,26 +1311,20 @@
     return jnp.where(owner[None, :, None], mine[:, None, :], 0.0).reshape(4 * layers, parts * part)
 
 
-def attend_tables(share, head_dim):
-    local = lax.axis_index("narrow") * share + jnp.arange(share, dtype=jnp.int32)
+def rotary_tables(seq, head_dim):
     half = head_dim // 2
-    freq = jnp.exp(-jnp.log(10000.0) * jnp.arange(half, dtype=F32) * 2.0 / head_dim)
-    angle = local.astype(F32)[:, None] * freq[None, :]
-    cosine, sine = jnp.cos(angle), jnp.sin(angle)
-    cosr = jnp.tile(jnp.concatenate([cosine, cosine], axis=1), (2, 2))
-    sinr = jnp.tile(jnp.concatenate([-sine, sine], axis=1), (2, 2))
-    block = jnp.arange(share, dtype=jnp.int32) // BLOCK
-    same = block[:, None] == block[None, :]
-    below = block[None, :] < block[:, None]
-    bias = lambda allow: jnp.where(allow, 0.0, NEG).astype(F32)
-    return cosr, sinr, jnp.concatenate([bias(below), bias(below | same)]), bias(same)
+    freq = np.exp(-np.log(np.float32(10000.0)) * np.arange(half, dtype=np.float32) * np.float32(2.0) / np.float32(head_dim))
+    angle = np.arange(seq, dtype=np.float32)[:, None] * freq.astype(np.float32)[None, :]
+    cosine, sine = np.cos(angle), np.sin(angle)
+    return (jnp.asarray(np.tile(cosine, (1, 4)), F32),
+            jnp.asarray(np.tile(np.concatenate([-sine, sine], axis=1), (1, 2)), F32))
 
 
 def on_device(tokens, lengths, w_qkv, w_out, w_up, w_down, norm_gains, norm_biases, cotangent):
     _, _, share, width = tokens.shape
     layers, _, part = norm_gains.shape
     tok = tokens.reshape(2 * share, width)
-    tabs = attend_tables(share, width // H)
+    tabs = rotary_tables(4 * share, width // H)
     outs = forward(tok, shared_params(norm_gains, norm_biases), *tabs, w_qkv, w_out, w_up, w_down)
     result, full, par, kept = outs[0], outs[1:5], outs[5], outs[6:]
     grad_tok, gq, go, gu, gd, small = backward(

time: 558 us -> 438 us (0.78); the launches traced: 558 us -> 431 us
  Pallas kernels: 535 us -> 413 us
    pallas_call x1, Pallas kernels: 246 us -> 168 us  [forward(): pl.pallas_call(partial(forward_kernel, layers), out_shape=[shape((rows, w...]
    pallas_call x1, Pallas kernels: 289 us -> 245 us  [backward(): pl.pallas_call(partial(backward_kernel, layers), out_shape=[shape((rows,...]
where the time goes in v3:
time: 438 us; the launch traced here: 431 us
  Pallas kernels  413 us (94%)
  other arithmetic  10.7 us (2%)
  local copies, waits for them, and re-layouts  5.51 us (1%)
    pallas_call x1, Pallas kernels, backward(): pl.pallas_call(partial(backward_kernel, layers), out_shape=[shape((rows,...  245 us
    pallas_call x1, Pallas kernels, forward(): pl.pallas_call(partial(forward_kernel, layers), out_shape=[shape((rows, w...  168 us

profile of v3, /device:TPU:0, one launch (start us, length us, event | category | flops | bytes accessed | tf_op | source)
XLA Modules:
  0.0 431.0 jit_solution(16832594600820412746)
XLA Ops:
  0.6 0.7 concatenate.12
  1.3 0.7 concatenate.11
  2.1 0.1 broadcast_in_dim.32
  2.2 0.1 broadcast_in_dim.28
  2.2 0.1 broadcast_in_dim.29
  2.3 0.6 broadcast_select_fusion.prm
  2.9 168.4 %forward.1 = (bf16[512,768]{1,0:T(8,128)(2,1)}, bf16[2,768,2304]{2,1,0:T(8,128)(2,1)}, bf16[2,768,768]{2,1,0:T(8,128)(2,1)}, bf16[2,768,3072]{2,1,0:T(8,128)(2,1...) custom-call(bf16[512,768]{1,0:T(8,128)(2,1)} %bitcast.10, ...), custom_call_target="tpu_custom_call" | custom-call | flops 20000000000 | bytes 100000000 | tf_op jit(solution)/shard_map/forward/pallas_call | solution.py:470
  172.0 244.6 %backward.1 = (bf16[512,768]{1,0:T(8,128)(2,1)}, bf16[2,192,2304]{2,1,0:T(8,128)(2,1)}, bf16[2,192,768]{2,1,0:T(8,128)(2,1)}, bf16[2,192,3072]{2,1,0:T(8,128)(2,...) custom-call(s32[1]{0:T(128)S(6)} %copy.28.lens, bf16[512,768]{1,0:T(8,128)(2,1)} %bitcast.12, ...), custom_call_target="tpu_custom_call" | custom-call | flops 40000000000 | bytes 100000000 | tf_op jit(solution)/shard_map/backward/pallas_call | solution.py:1293
  416.7 0.0 copy-start.4
  416.7 0.0 copy-start.1
  416.7 3.7 convert_element_type.20
  420.3 0.0 copy-done.4
  420.3 1.1 convert_element_type.21
  421.4 0.0 copy-done.1
  421.4 0.0 copy-start
  421.4 2.8 convert_element_type.22
  424.2 0.0 copy-done
  424.2 0.0 copy-start.2
  424.2 0.0 copy-start.3
  424.2 2.5 convert_element_type.23
  426.7 0.9 fusion
  427.6 0.6 reshape.66
  428.2 0.6 copy_bitcast_fusion
  428.8 0.0 copy-done.2
  428.8 0.9 copy.29
  429.7 0.0 copy-done.3
  429.7 0.9 copy.30
  (5 shorter events, 0.0 us)
Async XLA Ops:
  416.7 3.7 copy-start.4
  416.7 4.8 %copy-start.1 = (bf16[2,192,3072]{2,1,0:T(8,128)(2,1)S(1)}, bf16[2,192,3072]{2,1,0:T(8,128)(2,1)}, u32[]{:S(2)}) copy-start(bf16[2,192,3072]{2,1,0:T(8,128)(2,1)} %get-tuple-element.54) | copy-start | bytes 7077892
  421.4 2.8 copy-start
  424.2 4.6 %copy-start.2 = (bf16[512,768]{1,0:T(8,128)(2,1)S(1)}, bf16[512,768]{1,0:T(8,128)(2,1)}, u32[]{:S(2)}) copy-start(bf16[512,768]{1,0:T(8,128)(2,1)} %get-tuple-element.33) | copy-start | bytes 2359300
  424.2 5.5 %copy-start.3 = (bf16[512,768]{1,0:T(8,128)(2,1)S(1)}, bf16[512,768]{1,0:T(8,128)(2,1)}, u32[]{:S(2)}) copy-start(bf16[512,768]{1,0:T(8,128)(2,1)} %get-tuple-element.51) | copy-start | bytes 2359300

commit v4 on v3

--- a/solution.py
+++ b/solution.py
@@ -66,7 +66,7 @@
 
 
 def norm_into(src, dst, gain, bias, rows):
-    step = 32
+    step = 256
 
     def body(i):
         at = tile_at(i, step)
@@ -156,7 +156,7 @@
     result, fq, fo, fu, fd, prm_out,
     h_out, q_out, nkv_out, kv_out, lse_out, ctx_out, mid_out, act_out, dg_out, near_out, all_out, post_out,
     gq, go, gu, gd, prm_buf, par, hid, a, ag, post, q, nkv, kv, bias_c, bias_n,
-    score, top, lse, lset, ctx, mid, dg, act,
+    lset, ctx, mid, dg, act,
     send, recv, lsem, psend, precv, ksend, krecv, ssem,
 ):
     n = lax.axis_index("narrow")
@@ -228,12 +228,11 @@
 
     for k in range(2):
         at = slice(k * share, (k + 1) * share)
-        bias_c[at] = block_bias(blocks_of((share, share), 0), blocks_of((share, share), 1), k == 0)
+        bias_c[:, at] = block_bias(blocks_of((share, share), 1), blocks_of((share, share), 0), k == 0)
     same = blocks_of((share, share), 0) == blocks_of((share, share), 1)
     bias_n[...] = jnp.where(same, 0.0, NEG).astype(F32)
     masks = head_masks()
     here = tile_at(n, share)
-    lanes = lax.broadcasted_iota(jnp.int32, (rows, 128), 1)
 
     full_saves = weight_saves()
     for layer in range(layers):
@@ -319,52 +318,56 @@
             before[3].wait()
             before[4].wait()
 
+        def fold(v, how):
+            v = v.reshape(v.shape[0] // 8, 8, v.shape[1])
+            return how(how(v, axis=0), axis=0, keepdims=True)
+
         def pair_step(pair):
             at_pair = tile_at(pair, 128)
             at_value = tile_at(pair + pairs, 128)
             q2 = q[:, at_pair].astype(F32)
+            qm = [(q2 * masks[h]).astype(BF16) for h in range(2)]
+            lower = [slice(64 * h, 64 * h + 64) for h in range(2)]
+
+            def absorb(s, v2, carry):
+                most, total, out = carry
+                peak = jnp.maximum(most, fold(s, jnp.max))
+                p = jnp.exp(s - peak)
+                shrink = jnp.exp(most - peak)
+                total = total * shrink + fold(p, jnp.sum)
+                out = out * shrink + dot(v2, p.astype(BF16))
+                return peak, total, out
+
+            near_v = nkv[:, at_value].T
+            own_v = kv[here, at_value].T
+            blank = (jnp.full((1, share), NEG, F32), jnp.zeros((1, share), F32), jnp.zeros((64, share), F32))
+            states = []
+            for h in range(2):
+                s = dot_nt(nkv[:, at_pair], qm[h][:share]) + bias_n[...]
+                most = fold(s, jnp.max)
+                p = jnp.exp(s - most)
+                near = (most, fold(p, jnp.sum), dot(near_v[lower[h]], p.astype(BF16)))
+                state = tuple(jnp.concatenate([a, b], axis=1) for a, b in zip(near, blank))
+                s = dot_nt(kv[here, at_pair], qm[h]) + bias_c[...]
+                states.append(absorb(s, own_v[lower[h]], state))
+
+            def far_step(g, states):
+                at = tile_at(g, group)
+                far_v = kv[at, at_value].T
+                scores = [dot_nt(kv[at, at_pair], qm[h]) for h in range(2)]
+                return tuple(absorb(scores[h], far_v[lower[h]], states[h]) for h in range(2))
+
+            states = lax.fori_loop(0, n, far_step, tuple(states))
             outs = []
-            for h in range(2):
-                qm = (q2 * masks[h]).astype(BF16)
-                s = dot_nt(qm, kv[tile_at(n, group), at_pair]) + bias_c[...]
-                score[:, tile_at(n, group)] = s
-                top[...] = jnp.maximum(s[:, :128], s[:, 128:])
-                s = dot_nt(qm[:share], nkv[:, at_pair]) + bias_n[...]
-                score[:share, 4 * group:5 * group] = s
-                top[:share] = jnp.maximum(top[:share], jnp.maximum(s[:, :128], s[:, 128:]))
-
-                def scores_of(g):
-                    s = dot_nt(qm, kv[tile_at(g, group), at_pair])
-                    score[:, tile_at(g, group)] = s
-                    top[...] = jnp.maximum(top[...], jnp.maximum(s[:, :128], s[:, 128:]))
-
-                loop(n, scores_of)
-                most = jnp.max(top[...], axis=-1, keepdims=True)
-                p = jnp.exp(score[:share, 4 * group:5 * group] - most[:share])
-                part = p[:, :128] + p[:, 128:]
-                add = dot(p.astype(BF16), nkv[:, at_value])
-                zeros = jnp.zeros((share, 128), F32)
-
-                def probs_of(g, carry):
-                    total, out = carry
-                    p = jnp.exp(score[:, tile_at(g, group)] - most)
-                    total = total + p[:, :128] + p[:, 128:]
-                    out = out + dot(p.astype(BF16), kv[tile_at(g, group), at_value])
-                    return total, out
-
-                total, out = lax.fori_loop(
-                    0, n + 1, probs_of,
-                    (jnp.concatenate([part, zeros], axis=0), jnp.concatenate([add, zeros], axis=0)))
-                total = jnp.sum(total, axis=-1, keepdims=True)
-                outs.append(out * (masks[h] / total))
-                lse[...] = jnp.where(lanes == 2 * pair + h, most + jnp.log(total), lse[...])
-            ctx[:, at_pair] = (outs[0] + outs[1]).astype(BF16)
+            for h, (most, total, out) in enumerate(states):
+                outs.append(out / total)
+                lset[pl.ds(2 * pair + h, 1), :] = most + jnp.log(total)
+            ctx[:, at_pair] = jnp.concatenate(outs, axis=0).T.astype(BF16)
 
         loop(pairs // 2, pair_step)
         t_out.forward()
         t_up.forward()
         loop(pairs - pairs // 2, lambda t: pair_step(t + pairs // 2))
-        lset[...] = lse[...].T[:16]
         saved[3].start()
         saved[4].start()
         t_out.finish()
@@ -482,11 +485,8 @@
             pltpu.VMEM((rows, width), BF16),
             pltpu.VMEM((share, 2 * width), BF16),
             pltpu.VMEM((seq, 2 * width), BF16),
-            pltpu.VMEM((rows, share), F32),
+            pltpu.VMEM((share, rows), F32),
             pltpu.VMEM((share, share), F32),
-            pltpu.VMEM((rows, seq + share), F32),
-            pltpu.VMEM((rows, 128), F32),
-            pltpu.VMEM((rows, 128), F32),
             pltpu.VMEM((16, rows), F32),
             pltpu.VMEM((rows, width), BF16),
             pltpu.VMEM((rows, width), F32),
@@ -504,11 +504,13 @@
 
 
 def add_rows(dst, at, left, left_at, right, right_at, rows):
+    size = 48 if rows % 48 == 0 else 16
+
     def body(i):
-        step = lambda base: pl.ds(pl.multiple_of(base + 16 * i, 16), 16)
+        step = lambda base: pl.ds(pl.multiple_of(base + size * i, 16), size)
         dst[step(at), :] = left[step(left_at), :] + right[step(right_at), :]
 
-    loop(rows // 16, body)
+    loop(rows // size, body)
 
 
 class Reduce:
@@ -960,10 +962,10 @@
 
     def to_bf16(dst):
         def body(i):
-            at = tile_at(i, 64)
+            at = tile_at(i, 256)
             dst[at, :] = dh[at, :].astype(BF16)
 
-        loop(rows // 64, body)
+        loop(rows // 256, body)
 
     def norm_of(src, at):
         x = src[at, :].astype(F32)
@@ -976,7 +978,7 @@
             at_[:, 128 * i:128 * i + 128] = src[128 * i:128 * i + 128, :].T
 
     def norm_back(src, gain, row_gain, row_bias):
-        step = 32
+        step = 256
 
         def body(i, carry):
             at = tile_at(i, step)

time: 438 us -> 424 us (0.968)
  Pallas kernels: 413 us -> 399 us
    pallas_call x1, Pallas kernels: 245 us -> 233 us  [backward(): pl.pallas_call(partial(backward_kernel, layers), out_shape=[shape((rows,...]
where the time goes in v4:
time: 424 us; the launch traced here: 417 us
  Pallas kernels  399 us (94%)
  other arithmetic  10.7 us (3%)
  local copies, waits for them, and re-layouts  5.51 us (1%)
    pallas_call x1, Pallas kernels, backward(): pl.pallas_call(partial(backward_kernel, layers), out_shape=[shape((rows,...  233 us
    pallas_call x1, Pallas kernels, forward(): pl.pallas_call(partial(forward_kernel, layers), out_shape=[shape((rows, w...  166 us

profile of v4, /device:TPU:0, one launch (start us, length us, event | category | flops | bytes accessed | tf_op | source)
XLA Modules:
  0.0 416.8 jit_solution(16701473933680302976)
XLA Ops:
  0.6 0.7 concatenate.12
  1.3 0.7 concatenate.11
  2.1 0.1 broadcast_in_dim.32
  2.2 0.1 broadcast_in_dim.28
  2.2 0.1 broadcast_in_dim.29
  2.3 0.6 broadcast_select_fusion.prm
  2.9 166.0 %forward.1 = (bf16[512,768]{1,0:T(8,128)(2,1)}, bf16[2,768,2304]{2,1,0:T(8,128)(2,1)}, bf16[2,768,768]{2,1,0:T(8,128)(2,1)}, bf16[2,768,3072]{2,1,0:T(8,128)(2,1...) custom-call(bf16[512,768]{1,0:T(8,128)(2,1)} %bitcast.10, ...), custom_call_target="tpu_custom_call" | custom-call | flops 20000000000 | bytes 100000000 | tf_op jit(solution)/shard_map/forward/pallas_call | solution.py:473
  169.6 232.8 %backward.1 = (bf16[512,768]{1,0:T(8,128)(2,1)}, bf16[2,192,2304]{2,1,0:T(8,128)(2,1)}, bf16[2,192,768]{2,1,0:T(8,128)(2,1)}, bf16[2,192,3072]{2,1,0:T(8,128)(2,...) custom-call(s32[1]{0:T(128)S(6)} %copy.28.lens, bf16[512,768]{1,0:T(8,128)(2,1)} %bitcast.12, ...), custom_call_target="tpu_custom_call" | custom-call | flops 40000000000 | bytes 100000000 | tf_op jit(solution)/shard_map/backward/pallas_call | solution.py:1295
  402.4 0.0 copy-start.4
  402.4 0.0 copy-start.1
  402.4 3.7 convert_element_type.20
  406.1 0.0 copy-done.4
  406.1 1.1 convert_element_type.21
  407.2 0.0 copy-done.1
  407.2 0.0 copy-start
  407.2 2.8 convert_element_type.22
  409.9 0.0 copy-done
  409.9 0.0 copy-start.2
  409.9 0.0 copy-start.3
  409.9 2.5 convert_element_type.23
  412.5 0.9 fusion
  413.4 0.6 reshape.66
  414.0 0.6 copy_bitcast_fusion
  414.6 0.0 copy-done.2
  414.6 0.9 copy.29
  415.5 0.0 copy-done.3
  415.5 0.9 copy.30
  (5 shorter events, 0.0 us)
Async XLA Ops:
  402.4 3.7 copy-start.4
  402.4 4.8 %copy-start.1 = (bf16[2,192,3072]{2,1,0:T(8,128)(2,1)S(1)}, bf16[2,192,3072]{2,1,0:T(8,128)(2,1)}, u32[]{:S(2)}) copy-start(bf16[2,192,3072]{2,1,0:T(8,128)(2,1)} %get-tuple-element.54) | copy-start | bytes 7077892
  407.2 2.8 copy-start
  409.9 4.6 %copy-start.2 = (bf16[512,768]{1,0:T(8,128)(2,1)S(1)}, bf16[512,768]{1,0:T(8,128)(2,1)}, u32[]{:S(2)}) copy-start(bf16[512,768]{1,0:T(8,128)(2,1)} %get-tuple-element.33) | copy-start | bytes 2359300
  409.9 5.5 %copy-start.3 = (bf16[512,768]{1,0:T(8,128)(2,1)S(1)}, bf16[512,768]{1,0:T(8,128)(2,1)}, u32[]{:S(2)}) copy-start(bf16[512,768]{1,0:T(8,128)(2,1)} %get-tuple-element.51) | copy-start | bytes 2359300

commit v5 on v4

--- a/solution.py
+++ b/solution.py
@@ -809,8 +809,7 @@
         def _():
             self.copy(5, self.outer).start()
 
-    def finish(self, out):
-        out[...] = self.buf[0, 5]
+    def finish(self):
         for k in range(3):
             self.copy(k, self.others[k]).wait_send()
 
@@ -865,7 +864,7 @@
     layers,
     lens, cot, tok, par, cosr, sinr,
     fq, fo, fu, fd, h_in, q_in, nkv_in, kv_in, lse_in, ctx_in, mid_in, act_in, dg_in, near_in, all_in, post_in,
-    grad_tok, oq, oo, ou, od, small,
+    grad_tok, oq, oo, ou, od, out_gain, out_first, out_second,
     *rest,
 ):
     width = cot.shape[1]
@@ -1247,7 +1246,17 @@
     tot.chain()
     run(9, "tot4")
     tot.settle()
-    tot.finish(small)
+    tot.finish()
+    part = width // 4
+    for owner in range(4):
+        @pl.when(n == owner)
+        def _():
+            cut = sbuf[0, 5, :, owner * part:(owner + 1) * part]
+            for layer in range(layers):
+                out_gain[layer] = cut[2 * layer:2 * layer + 2]
+                row = 2 * layers + 2 * layer
+                out_first[layer:layer + 1] = cut[row:row + 1]
+                out_second[layer:layer + 1] = cut[row + 1:row + 2]
     for turn in every:
         for r in turn.values():
             r.p8()
@@ -1272,6 +1281,8 @@
     v = pltpu.VMEM
     dma, regular = pltpu.SemaphoreType.DMA, pltpu.SemaphoreType.REGULAR
     outs = [shape((layers, f.shape[1] // 4, f.shape[2]), BF16) for f in full]
+    part = width // 4
+    small = [shape((layers, 2, part), F32), shape((layers, part), F32), shape((layers, part), F32)]
     kinds = [(width, width)] * 4 + [(width, ff), (ff, width)]
     scratch = [v(k, BF16) for k in kinds] + [v((width // 2, ff), BF16), v((ff // 2, width), BF16)]
     for total, cols in kinds:
@@ -1294,9 +1305,9 @@
     ]
     return pl.pallas_call(
         partial(backward_kernel, layers),
-        out_shape=[shape((rows, width), BF16)] + outs + [shape(par.shape, F32)],
+        out_shape=[shape((rows, width), BF16)] + outs + small,
         in_specs=[pl.BlockSpec(memory_space=pltpu.SMEM)] + [hbm] * 2 + [vmem] * 3 + [hbm] * 16,
-        out_specs=[vmem] + [hbm] * 4 + [vmem],
+        out_specs=[vmem] + [hbm] * 4 + [vmem] * 3,
         scratch_shapes=scratch,
         compiler_params=pltpu.CompilerParams(
             collective_id=1, has_side_effects=True, vmem_limit_bytes=63 * 2**20),
@@ -1322,23 +1333,44 @@
             jnp.asarray(np.tile(np.concatenate([-sine, sine], axis=1), (1, 2)), F32))
 
 
+def settle_kernel(*refs):
+    half = len(refs) // 2
+    for src, dst in zip(refs[:half], refs[half:]):
+        dst[...] = src[...].astype(dst.dtype)
+
+
+def settle(grads, rows, small):
+    layers = grads[0].shape[0]
+    halves = 2
+    cut = lambda a: pl.BlockSpec((1, a.shape[1] // halves, a.shape[2]), lambda i, j: (i, j, 0))
+    strip = lambda a: pl.BlockSpec((a.shape[0] // (layers * halves), a.shape[1]), lambda i, j: (i * halves + j, 0))
+    whole = lambda a: pl.BlockSpec(a.shape, lambda i, j: (0,) * a.ndim)
+    specs = [cut(a) for a in grads] + [strip(a) for a in rows] + [whole(a) for a in small]
+    shape = jax.ShapeDtypeStruct
+    outs = [shape(a.shape, F32) for a in grads] + [shape(a.shape, a.dtype) for a in (*rows, *small)]
+    return pl.pallas_call(
+        settle_kernel,
+        grid=(layers, halves),
+        out_shape=outs,
+        in_specs=specs,
+        out_specs=specs,
+        compiler_params=pltpu.CompilerParams(vmem_limit_bytes=62 * 2**20),
+        name="settle",
+    )(*grads, *rows, *small)
+
+
 def on_device(tokens, lengths, w_qkv, w_out, w_up, w_down, norm_gains, norm_biases, cotangent):
     _, _, share, width = tokens.shape
-    layers, _, part = norm_gains.shape
     tok = tokens.reshape(2 * share, width)
     tabs = rotary_tables(4 * share, width // H)
     outs = forward(tok, shared_params(norm_gains, norm_biases), *tabs, w_qkv, w_out, w_up, w_down)
     result, full, par, kept = outs[0], outs[1:5], outs[5], outs[6:]
-    grad_tok, gq, go, gu, gd, small = backward(
+    grad_tok, gq, go, gu, gd, gains, first, second = backward(
         lengths, cotangent.reshape(2 * share, width), tok, par, tabs, full, kept)
-    mine = lax.dynamic_slice_in_dim(small, lax.axis_index("narrow") * part, part, 1)
-    gains = mine[:2 * layers].reshape(layers, 2, part)
-    biases = mine[2 * layers:].reshape(layers, 2, part)
+    gq, go, gu, gd, result, grad_tok, gains, first, second = settle(
+        (gq, go, gu, gd), (result, grad_tok), (gains, first, second))
     return (
-        result.reshape(tokens.shape), grad_tok.reshape(tokens.shape),
-        gq.astype(F32), go.astype(F32), gu.astype(F32), gd.astype(F32),
-        gains, biases[:, 0], biases[:, 1],
-    )
+        result.reshape(tokens.shape), grad_tok.reshape(tokens.shape), gq, go, gu, gd, gains, first, second)
 
 
 def solution(mesh):

time: 424 us -> 420 us (level)
  other arithmetic: 10.7 us -> 0.63 us
  Pallas kernels: 399 us -> 409 us
    convert_element_type x4 -> x0, other arithmetic: 10.1 us -> none  [the longest x1 3.65 us: on_device(): gq.astype(F32)]
    pallas_call x0 -> x1, Pallas kernels: none -> 9.46 us  [settle(): pl.pallas_call(settle_kernel, grid=(layers, halves), out_shape=outs, in_s...]
where the time goes in v5:
time: 420 us; the launch traced here: 413 us
  Pallas kernels  409 us (97%)
    pallas_call x1, Pallas kernels, backward(): pl.pallas_call(partial(backward_kernel, layers), out_shape=[shape((rows,...  233 us
    pallas_call x1, Pallas kernels, forward(): pl.pallas_call(partial(forward_kernel, layers), out_shape=[shape((rows, w...  166 us
    pallas_call x1, Pallas kernels, settle(): pl.pallas_call(settle_kernel, grid=(layers, halves), out_shape=outs, in_s...  9.46 us

profile of v5, /device:TPU:0, one launch (start us, length us, event | category | flops | bytes accessed | tf_op | source)
XLA Modules:
  0.0 412.7 jit_solution(2342187896492101698)
XLA Ops:
  1.3 0.1 broadcast_in_dim.28
  1.4 0.1 broadcast_in_dim.29
  1.5 0.7 concatenate.11
  2.2 0.7 concatenate.12
  2.9 0.1 broadcast_in_dim.32
  3.0 0.6 broadcast_select_fusion.prm
  3.6 166.0 %forward.1 = (bf16[512,768]{1,0:T(8,128)(2,1)}, bf16[2,768,2304]{2,1,0:T(8,128)(2,1)}, bf16[2,768,768]{2,1,0:T(8,128)(2,1)}, bf16[2,768,3072]{2,1,0:T(8,128)(2,1...) custom-call(bf16[512,768]{1,0:T(8,128)(2,1)} %bitcast.5, ...), custom_call_target="tpu_custom_call" | custom-call | flops 20000000000 | bytes 100000000 | tf_op jit(solution)/shard_map/forward/pallas_call | solution.py:473
  169.6 233.2 %backward.1 = (bf16[512,768]{1,0:T(8,128)(2,1)}, bf16[2,192,2304]{2,1,0:T(8,128)(2,1)}, bf16[2,192,768]{2,1,0:T(8,128)(2,1)}, bf16[2,192,3072]{2,1,0:T(8,128)(2,...) custom-call(s32[1]{0:T(128)S(6)} %copy.20.lens, ...), custom_call_target="tpu_custom_call" | custom-call | flops 40000000000 | bytes 100000000 | tf_op jit(solution)/shard_map/backward/pallas_call | solution.py:1306
  402.8 9.5 %settle.1 = (f32[2,192,2304]{2,1,0:T(8,128)}, f32[2,192,768]{2,1,0:T(8,128)}, f32[2,192,3072]{2,1,0:T(8,128)}, f32[2,768,768]{2,1,0:T(8,128)}, bf16[512,768]{1,0...) custom-call(bf16[2,192,2304]{2,1,0:T(8,128)(2,1)} %get-tuple-element.61.r, ...), custom_call_target="tpu_custom_call" | custom-call | tf_op jit(solution)/shard_map/settle/pallas_call | solution.py:1351
  (3 shorter events, 0.0 us)

commit v6 on v5

--- a/solution.py
+++ b/solution.py
@@ -1341,7 +1341,7 @@
 
 def settle(grads, rows, small):
     layers = grads[0].shape[0]
-    halves = 2
+    halves = 4
     cut = lambda a: pl.BlockSpec((1, a.shape[1] // halves, a.shape[2]), lambda i, j: (i, j, 0))
     strip = lambda a: pl.BlockSpec((a.shape[0] // (layers * halves), a.shape[1]), lambda i, j: (i * halves + j, 0))
     whole = lambda a: pl.BlockSpec(a.shape, lambda i, j: (0,) * a.ndim)

time: 420 us -> 421 us (level)
  no operation moved by 1% of the time
where the time goes in v6:
time: 421 us; the launch traced here: 413 us
  Pallas kernels  409 us (97%)
    pallas_call x1, Pallas kernels, backward(): pl.pallas_call(partial(backward_kernel, layers), out_shape=[shape((rows,...  233 us
    pallas_call x1, Pallas kernels, forward(): pl.pallas_call(partial(forward_kernel, layers), out_shape=[shape((rows, w...  166 us
    pallas_call x1, Pallas kernels, settle(): pl.pallas_call(settle_kernel, grid=(layers, halves), out_shape=outs, in_s...  10.2 us

profile of v6, /device:TPU:0, one launch (start us, length us, event | category | flops | bytes accessed | tf_op | source)
XLA Modules:
  0.0 413.5 jit_solution(11894811877937061293)
XLA Ops:
  1.3 0.1 broadcast_in_dim.28
  1.4 0.1 broadcast_in_dim.29
  1.5 0.7 concatenate.11
  2.2 0.7 concatenate.12
  2.9 0.1 broadcast_in_dim.32
  3.0 0.6 broadcast_select_fusion.prm
  3.6 166.0 %forward.1 = (bf16[512,768]{1,0:T(8,128)(2,1)}, bf16[2,768,2304]{2,1,0:T(8,128)(2,1)}, bf16[2,768,768]{2,1,0:T(8,128)(2,1)}, bf16[2,768,3072]{2,1,0:T(8,128)(2,1...) custom-call(bf16[512,768]{1,0:T(8,128)(2,1)} %bitcast.5, ...), custom_call_target="tpu_custom_call" | custom-call | flops 20000000000 | bytes 100000000 | tf_op jit(solution)/shard_map/forward/pallas_call | solution.py:473
  169.6 233.2 %backward.1 = (bf16[512,768]{1,0:T(8,128)(2,1)}, bf16[2,192,2304]{2,1,0:T(8,128)(2,1)}, bf16[2,192,768]{2,1,0:T(8,128)(2,1)}, bf16[2,192,3072]{2,1,0:T(8,128)(2,...) custom-call(s32[1]{0:T(128)S(6)} %copy.20.lens, ...), custom_call_target="tpu_custom_call" | custom-call | flops 40000000000 | bytes 100000000 | tf_op jit(solution)/shard_map/backward/pallas_call | solution.py:1306
  402.8 10.2 %settle.1 = (f32[2,192,2304]{2,1,0:T(8,128)}, f32[2,192,768]{2,1,0:T(8,128)}, f32[2,192,3072]{2,1,0:T(8,128)}, f32[2,768,768]{2,1,0:T(8,128)}, bf16[512,768]{1,0...) custom-call(bf16[2,192,2304]{2,1,0:T(8,128)(2,1)} %get-tuple-element.61.r, ...), custom_call_target="tpu_custom_call" | custom-call | tf_op jit(solution)/shard_map/settle/pallas_call | solution.py:1351
  (3 shorter events, 0.0 us)
